TPU v7x, 32 devices: a whole 2x2x4 slice. The times are simulated.
32 devices in a mesh: ctx: 16 (over z, y, core), tp: 2 (over x).
Axes of the slice: x: 2, y: 2, z: 4, core: 2. Of those that a mesh axis runs over, the one named last changes fastest.
Arguments:
- tokens: bfloat16 [8192, 1024], P('ctx'), may hold values from -6 to 6
- cotangent: bfloat16 [8192, 1024], P('ctx'), may hold values from -6 to 6
- block_order: int32 [16], replicated, may hold values from 0 to 15, each once
- segment_ids: int32 [1, 8192], replicated, may hold values from 0 to 3, as said below
- norm_gain: bfloat16 [1024], replicated, may hold values from 0.5 to 1.5
- w_query: bfloat16 [1024, 1024], P(None, 'tp'), may hold values from -0.1875 to 0.1875
- key_weight: bfloat16 [1024, 512], P(None, 'tp'), may hold values from -0.1875 to 0.1875
- value_weight: bfloat16 [1024, 512], P(None, 'tp'), may hold values from -0.1875 to 0.1875
- query_gain: bfloat16 [64], replicated, may hold values from 0.25 to 1.75
- key_gain: bfloat16 [64], replicated, may hold values from 0.25 to 1.75
- w_out: bfloat16 [1024, 1024], P('tp'), may hold values from -3 to 3
- ffn_gain: bfloat16 [1024], replicated, may hold values from 0.5 to 1.5
- w_gate: bfloat16 [1024, 4608], P(None, 'tp'), may hold values from -0.1875 to 0.1875
- w_up: bfloat16 [1024, 4608], P(None, 'tp'), may hold values from -0.1875 to 0.1875
- w_down: bfloat16 [4608, 1024], P('tp'), may hold values from -0.09375 to 0.09375
Outputs:
- output: bfloat16 [8192, 1024], P('ctx')
- input_grad: float32 [8192, 1024], P('ctx')
- grad_norm_gain: float32 [1024], replicated
- grad_w_query: float32 [1024, 1024], P(None, 'tp')
- grad_w_key: float32 [1024, 512], P(None, 'tp')
- grad_w_value: float32 [1024, 512], P(None, 'tp')
- grad_query_gain: float32 [64], replicated
- grad_key_gain: float32 [64], replicated
- grad_w_out: float32 [1024, 1024], P('tp')
- grad_ffn_gain: float32 [1024], replicated
- grad_w_gate: float32 [1024, 4608], P(None, 'tp')
- grad_w_up: float32 [1024, 4608], P(None, 'tp')
- grad_w_down: float32 [4608, 1024], P('tp')
Inputs may be any that keep to these rules, and one draw needn't show every extreme that they name: `block_order`: each index of ctx appears once. `segment_ids`: along each sequence the ids never fall; the first position has id 0 and the last id 3; document 0 covers more than the first three quarters of every sequence.
All inputs are finite; a program needn't handle non-finite values.
Results may differ from a plain program's by a relative error of at most 0.038.
Values may be sent and summed in bfloat16 or wider, within the bound.
No kernel may reach another device: no remote copies, remote signals or barrier semaphores. Data moves between devices by JAX's collectives and lax.ppermute only.
A program may use at most 576 MiB of HBM per device.

v0:
```python
import functools

import jax
import jax.numpy as jnp
import numpy as np
from jax import lax
from jax.experimental import pallas as pl
from jax.experimental.pallas import tpu as pltpu
from jax.sharding import PartitionSpec as P

HEAD_SIZE = 64
LANES = 2 * HEAD_SIZE
EPSILON = 1e-05
ROPE_BASE = 1000000.0
LOG2E = 1.4426950408889634
VMEM_BYTES = 24 * 2**20
COST_SCALE = 1
FFN_COLS = 768
LATE = True
f32, bf16 = jnp.float32, jnp.bfloat16
NT = (((1,), (1,)), ((), ()))


class Ring:
    def __init__(self, n_ctx):
        n = self.n = n_ctx // 2
        self.zs = 4 if n % 4 == 0 else n
        self.ys = n // self.zs
        order = [int(self.chip_at(np.int32(place))) for place in range(n)]

        def steps(flip, turned):
            return [
                (order[i] * 2 + c, order[(i + (1 - 2 * (c ^ turned))) % n] * 2 + (c ^ flip))
                for i in range(n)
                for c in (0, 1)
            ]

        self.onward, self.across, self.spread = steps(0, 0), steps(1, 0), steps(1, 1)
        self.to_sibling = [(i, i ^ 1) for i in range(n_ctx)]

    def chip_at(self, place):
        if self.ys == 1:
            return place
        where = np.where if isinstance(place, np.integer) else jnp.where
        turn = place - self.zs
        k, r = turn // (self.ys - 1), turn % (self.ys - 1)
        back = (self.zs - 1 - k) * self.ys + where(k % 2 == 0, 1 + r, self.ys - 1 - r)
        return where(place < self.zs, place * self.ys, back)

    def here(self):
        index = lax.axis_index("ctx")
        chip, core = index // 2, index % 2
        if self.ys == 1:
            return chip, core
        z, y = chip // self.ys, chip % self.ys
        k = self.zs - 1 - z
        back = self.zs + k * (self.ys - 1) + jnp.where(k % 2 == 0, y - 1, self.ys - 1 - y)
        return jnp.where(y == 0, z, back), core

    def at(self, slot):
        place, core = self.here()
        distance, other = slot
        return (place + (1 - 2 * core) * distance + self.n) % self.n, (core + other) % 2

    def device_at(self, slot):
        place, core = self.at(slot)
        return self.chip_at(place) * 2 + core

    def hop(self, x):
        return lax.ppermute(x, "ctx", self.onward)

    def sibling(self, x):
        return lax.ppermute(x, "ctx", self.to_sibling)


def total(*terms):
    out = terms[0].astype(f32)
    for term in terms[1:]:
        out = out + term.astype(f32)
    return out.astype(bf16)


class RingGather:
    def __init__(self, ring, own):
        self.ring, self.far = ring, ring.n // 2
        self.pieces = [([(0, 0)], own), ([(0, 1)], ring.sibling(own))]
        self.step = 0

    def sends(self):
        last = self.pieces[-2][1]
        if self.step == 0:
            return [self.pieces[0][1]]
        return [last[0]] if self.step + 1 == self.far else [last]

    def send(self, arrays):
        (x,) = arrays
        self.step += 1
        new = [self.ring.hop(x)]
        if self.step == 1:
            new.append(lax.ppermute(x, "ctx", self.ring.spread))
        return new

    def arrive(self, arrays):
        d = self.step
        if d == 1:
            new = [([(-1, c)], x) for c, x in enumerate(arrays)]
            pair = jnp.stack(arrays)
            self.pieces += [([(-1, 0), (-1, 1)], pair), ([(1, 1), (1, 0)], self.ring.sibling(pair))]
            return new
        (x,) = arrays
        if d == self.far:
            new = [([(d, 0)], x), ([(d, 1)], self.ring.sibling(x))]
        else:
            new = [([(-d, 0), (-d, 1)], x), ([(d, 1), (d, 0)], self.ring.sibling(x))]
        self.pieces += new
        return new[:1]

    def done(self):
        return self.step == self.far


def sum_steps(ring, terms, box=None):
    _, core = ring.here()
    far = ring.n // 2
    (x,) = yield [total(*terms(far))]
    (got,) = yield [ring.hop(x)]
    for d in range(far - 1, 1, -1):
        here = terms(d)
        if d == far - 1:
            x = jnp.stack([total(*[y[0] for y in here], got), total(*[y[1] for y in here])])
        else:
            x = total(*here, got)
        (x,) = yield [x]
        (got,) = yield [ring.hop(x)]
    here = terms(1)
    x = yield [total(*[y[c] for y in here], got[c]) for c in (0, 1)]
    got = yield [ring.hop(x[0]), lax.ppermute(x[1], "ctx", ring.across)]
    own = total(*terms(0), *got)
    if box is None:
        return own
    gather = RingGather(ring, own)
    box.append(gather)
    while not gather.done():
        late = [x for _, x in gather.pieces[-1:]]
        new = gather.send((yield gather.sends()))
        came = yield new + late
        gather.arrive(came[: len(new)])
    return gather


class Steps:
    def __init__(self, generator):
        self.generator, self.result = generator, None
        self.sent = self.came = None

    def arrivals(self):
        return self.generator.send(self.sent) if self.sent is not None else []

    def sends(self):
        try:
            return self.generator.send(self.came or None)
        except StopIteration as stop:
            self.result, self.generator = stop.value, None
            return []


def tied(lists, others):
    flat = lax.optimization_barrier((*[x for xs in lists for x in xs], *others))
    out = []
    for xs in lists:
        out.append(list(flat[: len(xs)]))
        flat = flat[len(xs) :]
    return out, flat


def advance(steps, *others):
    steps = [x for x in steps if x is not None and x.generator is not None]
    came, others = tied([x.arrivals() for x in steps], others)
    for x, arrays in zip(steps, came):
        x.came = arrays
    sends, others = tied([x.sends() for x in steps], others)
    for x, arrays in zip(steps, sends):
        x.sent = arrays
    return others


def sum_over_ctx(ring, arrays):
    n = ring.n
    far = n // 2
    outs = []
    for x in arrays:
        unit = x.shape[0] // (2 * n)
        cut = x.reshape(2, n, unit, x.shape[1])

        def piece(distance, other):
            place, core = ring.at((distance, other))
            return cut[core, place]

        def terms(d):
            if d in (0, far):
                return [piece(d, 0), ring.sibling(piece(d, 1))]
            keep = jnp.stack([piece(d, 0), piece(d, 1)])
            return [keep, ring.sibling(jnp.stack([piece(-d, 1), piece(-d, 0)]))]

        box = []
        steps = Steps(sum_steps(ring, terms, box))
        while steps.generator is not None:
            advance([steps])
        out = jnp.zeros(x.shape, f32)
        for slots, part in box[0].pieces:
            for i, slot in enumerate(slots):
                place, core = ring.at(slot)
                one = part if len(slots) == 1 else part[i]
                out = lax.dynamic_update_slice_in_dim(
                    out, one.astype(f32), (core * n + place) * unit, 0
                )
        outs.append(out)
    return outs


def exchange_steps(x):
    (x,) = yield [x]
    (theirs,) = yield [lax.ppermute(x, "tp", [(0, 1), (1, 0)])]
    return theirs


def pair_steps(x, axes):
    for axis, size in axes:
        step = 1
        while step < size:
            (mine,) = yield [x]
            (theirs,) = yield [lax.ppermute(mine, axis, [(i, i ^ step) for i in range(size)])]
            x = mine + theirs
            step *= 2
    return x


def from_other(xs):
    return [lax.ppermute(x, "tp", [(0, 1), (1, 0)]) for x in xs]


def sum_over_tp(x):
    size = lax.axis_size("tp")
    if size == 2:
        return x.astype(f32) + lax.ppermute(x, "tp", [(0, 1), (1, 0)]).astype(f32)
    return lax.psum(x, "tp").astype(f32)


def pair_count(slots, seq_count):
    return seq_count * (2 * len(slots) + ((0, 0) in slots))


class Tiles:
    def __init__(self, ring, slots, seq_count, blk, order_ref, starts_ref):
        self.ring, self.slots = ring, slots
        self.seq_count, self.blk = seq_count, blk
        self.order, self.starts = order_ref, starts_ref
        self.last = 4 * ring.n - 1
        self.rows = pair_count(slots, seq_count)

    def start_of(self, seq, place):
        start = jnp.int32(0)
        for d in range(3):
            at = self.starts[seq, d]
            start = jnp.where(place >= at, at, start)
        return start

    def pair(self, row):
        seq, row = row % self.seq_count, row // self.seq_count
        slot, which = row // 2, row % 2
        own = self.slots.index((0, 0)) if (0, 0) in self.slots else None
        if own is not None:
            both_high = slot == len(self.slots)
            slot = jnp.where(both_high, own, slot)
        distance, other = self.slots[0]
        for i, (d, c) in enumerate(self.slots):
            distance, other = jnp.where(slot == i, d, distance), jnp.where(slot == i, c, other)
        mine = self.order[lax.axis_index("ctx")]
        theirs = self.order[self.ring.device_at((distance, other))]
        low = (which == 1) & (theirs <= mine)
        high = (which == 1) & (theirs > mine)
        if own is not None:
            low, high = low & jnp.logical_not(both_high), high | both_high
        q_place = jnp.where(low, mine, self.last - mine) * self.blk
        k_place = jnp.where(high, self.last - theirs, theirs) * self.blk
        q_tile = 2 * seq + jnp.where(low, 0, 1)
        k_tile = 2 * (self.seq_count * slot + seq) + jnp.where(high, 1, 0)
        k_end, q_end = k_place + self.blk - 1, q_place + self.blk - 1
        whole = (k_end <= q_place) & (k_place >= self.start_of(seq, q_end))
        empty = k_end < self.start_of(seq, q_place)
        kind = jnp.where(whole, 0, jnp.where(empty, 2, 1))
        return q_tile, k_tile, kind, (seq, q_place, k_place)

    def allowed(self, at, query_axis, shape):
        seq, q_place, k_place = at
        query = q_place + lax.broadcasted_iota(jnp.int32, shape, query_axis) % self.blk
        key = k_place + lax.broadcasted_iota(jnp.int32, shape, 1 - query_axis)
        return (key <= query) & (key >= self.start_of(seq, query))

    def run(self, tile):
        def body(row, carry):
            q_tile, k_tile, kind, at = self.pair(row)
            keys = pl.ds(pl.multiple_of(k_tile * self.blk, self.blk), self.blk)
            pl.when(kind == 0)(lambda: tile(q_tile, keys, None))
            pl.when(kind == 1)(lambda: tile(q_tile, keys, functools.partial(self.allowed, at)))
            return carry

        lax.fori_loop(0, self.rows, body, 0)


def load_chunks(chunks, kv_ref):
    at = 0
    for chunk in chunks:
        for part in [chunk] if len(chunk.shape) == 2 else [chunk.at[0], chunk.at[1]]:
            kv_ref[at : at + part.shape[0]] = part[...]
            at += part.shape[0]


def forward_kernel(make, parts, heads, order_ref, starts_ref, q_ref, *refs):
    chunks, held, (out_ref, kv_ref) = refs[:parts], refs[parts:-2], refs[-2:]
    tiles = make(order_ref, starts_ref)
    blk = tiles.blk
    first = lax.broadcasted_iota(jnp.int32, (blk, LANES), 1) < HEAD_SIZE
    load_chunks(chunks, kv_ref)
    out_ref[...] = held[0][...] if held else jnp.zeros_like(out_ref)

    def tile(q_tile, keys, mask):
        if mask is not None:
            allowed = mask(0, (q_ref.shape[2], blk))
        for h in range(heads):
            kv = kv_ref[keys, h * LANES : (h + 1) * LANES]
            scores = lax.dot_general(q_ref[h, q_tile], kv, NT, preferred_element_type=f32)
            weights = jnp.exp2(scores * LOG2E)
            if mask is not None:
                weights = jnp.where(allowed, weights, 0.0)
            one_v = jnp.where(first, jnp.ones_like(kv), kv)
            out_ref[h, q_tile] += jnp.dot(weights.astype(bf16), one_v, preferred_element_type=f32)

    tiles.run(tile)


def backward_kernel(make, parts, held, heads, order_ref, starts_ref, q_ref, do_ref, stat_ref, *refs):
    chunks, held, refs = refs[:parts], refs[parts : parts + held], refs[parts + held :]
    dq_ref, keep_ref, give_ref, kv_ref, dkv_ref = refs
    tiles = make(order_ref, starts_ref)
    blk = tiles.blk
    load_chunks(chunks, kv_ref)
    dq_ref[...] = held[0][...] if held else jnp.zeros_like(dq_ref)
    dkv_ref[...] = jnp.zeros_like(dkv_ref)

    def tile(q_tile, keys, mask):
        if mask is not None:
            allowed = mask(1, (blk, q_ref.shape[2]))
        for h in range(heads):
            cols = slice(h * LANES, (h + 1) * LANES)
            kv = kv_ref[keys, cols]
            q = q_ref[h, q_tile]
            do = do_ref[h, q_tile]
            scores = lax.dot_general(kv, q, NT, preferred_element_type=f32)
            back_probs = lax.dot_general(kv, do, NT, preferred_element_type=f32)
            probs = jnp.exp2(scores * LOG2E - stat_ref[h, q_tile, 0:1])
            if mask is not None:
                probs = jnp.where(allowed, probs, 0.0)
            back_scores = (probs * (back_probs - stat_ref[h, q_tile, 1:2])).astype(bf16)
            both = jnp.concatenate([probs.astype(bf16), back_scores], axis=1)
            dkv_ref[keys, cols] += jnp.dot(
                both, jnp.concatenate([do, q], axis=0), preferred_element_type=f32
            )
            dq_ref[h, q_tile] += jnp.dot(kv.T[:HEAD_SIZE], back_scores, preferred_element_type=f32)

    tiles.run(tile)
    rows = keep_ref.shape[-2]
    if len(keep_ref.shape) == 2:
        keep_ref[...] = dkv_ref[:rows]
        give_ref[...] = dkv_ref[rows:].astype(bf16)
        return
    for c in (0, 1):
        keep_ref[c] = dkv_ref[(3 - c) * rows : (4 - c) * rows]
        give_ref[c] = dkv_ref[(1 - c) * rows : (2 - c) * rows].astype(bf16)


def in_smem():
    return pl.BlockSpec(memory_space=pltpu.SMEM)


def in_vmem():
    return pl.BlockSpec(memory_space=pltpu.VMEM)


class Attention:
    def __init__(self, ring, block_order, starts, blk):
        self.ring, self.order, self.starts = ring, block_order, starts
        self.blk, self.seq_count = blk, starts.shape[0]

    def _make(self, slots):
        return lambda order_ref, starts_ref: Tiles(
            self.ring, slots, self.seq_count, self.blk, order_ref, starts_ref
        )

    def _cost(self, slots, heads, products, arrays):
        tile = 2 * self.blk * self.blk * heads * pair_count(slots, self.seq_count)
        return pl.CostEstimate(
            flops=2 * tile * 256 * products // COST_SCALE,
            bytes_accessed=sum(x.size * x.dtype.itemsize for x in arrays) // COST_SCALE,
            transcendentals=tile // COST_SCALE,
        )

    def forward(self, pieces, q, acc):
        heads, tiles, rows, _ = q.shape
        out = jax.ShapeDtypeStruct((heads, tiles, rows, LANES), f32)
        held = [] if acc is None else [acc]
        slots, chunks = [x for xs, _ in pieces for x in xs], [x for _, x in pieces]
        keys, width = len(slots) * chunks[0].shape[-2], chunks[0].shape[-1]
        return pl.pallas_call(
            functools.partial(forward_kernel, self._make(slots), len(chunks), heads),
            out_shape=out,
            in_specs=[in_smem()] * 2 + [in_vmem()] * (1 + len(chunks) + len(held)),
            out_specs=in_vmem(),
            scratch_shapes=[pltpu.VMEM((keys, width), bf16)],
            compiler_params=pltpu.CompilerParams(vmem_limit_bytes=VMEM_BYTES),
            cost_estimate=self._cost(slots, heads, 2, [q, *chunks, out, out]),
            name="attend_forward",
        )(self.order, self.starts, q, *chunks, *held)

    def backward(self, pieces, q, do, stats, acc):
        heads, tiles, rows, _ = q.shape
        slots, chunks = [x for xs, _ in pieces for x in xs], [x for _, x in pieces]
        keys, width = len(slots) * chunks[0].shape[-2], chunks[0].shape[-1]
        outs = [
            jax.ShapeDtypeStruct((heads, tiles, HEAD_SIZE, rows), f32),
            jax.ShapeDtypeStruct(chunks[0].shape, f32),
            jax.ShapeDtypeStruct(chunks[0].shape, bf16),
        ]
        held = [] if acc is None else [acc]
        return pl.pallas_call(
            functools.partial(
                backward_kernel, self._make(slots), len(chunks), len(held), heads
            ),
            out_shape=outs,
            in_specs=[in_smem()] * 2 + [in_vmem()] * (3 + len(chunks) + len(held)),
            out_specs=[in_vmem()] * len(outs),
            scratch_shapes=[pltpu.VMEM((keys, width), bf16), pltpu.VMEM((keys, width), f32)],
            compiler_params=pltpu.CompilerParams(vmem_limit_bytes=VMEM_BYTES),
            cost_estimate=self._cost(slots, heads, 5, [q, do, outs[0], *chunks, *outs]),
            name="attend_backward",
        )(self.order, self.starts, q, do, stats, *chunks, *held)


def grads_kernel(ring, two_ref, gate_ref, up_ref, ffn_ref, cot_ref, *refs):
    outs, (lhs_ref, all_ref) = refs[:-2], refs[-2:]

    @pl.when(pl.program_id(0) == 0)
    def _():
        lhs_ref[...] = two_ref[...].T

    n = ring.n
    unit = lhs_ref.shape[0] // (2 * n)
    cols = gate_ref.shape[1]
    thin = cols // (2 * n)
    for i, ref in enumerate((gate_ref, up_ref)):
        grad = jnp.dot(lhs_ref[...], ref[...], preferred_element_type=f32).astype(bf16)
        all_ref[:, i * unit : (i + 1) * unit] = grad.reshape(2 * n, unit, cols)
    down = jnp.dot(ffn_ref[...].T, cot_ref[...], preferred_element_type=f32).astype(bf16)
    down = down.reshape(2 * n, thin, down.shape[1])
    for k in range(down.shape[2] // cols):
        at = 2 * unit + k * thin
        all_ref[:, at : at + thin] = down[:, :, k * cols : (k + 1) * cols]
    deal(ring, lambda at: all_ref[at], lambda ref, x: ref.at[0].__setitem__(..., x), outs)


def deal(ring, read, write, outs):
    far = ring.n // 2

    def part(distance, other):
        place, core = ring.at((distance, other))
        return read(core * ring.n + place)

    keep_far, give_far, *keep, give = outs
    write(keep_far, part(far, 0))
    write(give_far, part(far, 1))
    write(keep[0], part(0, 0))
    write(give.at[0], part(0, 1))
    for d in range(1, far):
        for c in (0, 1):
            write(keep[d].at[c], part(d, c))
            write(give.at[2 * d - 1 + c], part(-d, 1 - c))


def dealt(ring, cut):
    far = ring.n // 2
    heads = [(), (), ()] + [(2,)] * (far - 1) + [(2 * far - 1,)]
    return [jax.ShapeDtypeStruct((*head, *cut.shape), cut.dtype) for head in heads]


def dealt_terms(ring, outs):
    far = ring.n // 2
    keep_far, give_far, *keep, give = outs
    got_far = ring.sibling(give_far)
    give, got_far = lax.optimization_barrier((give, got_far))
    got = ring.sibling(give)

    def terms(d):
        if d == far:
            return [keep_far, got_far]
        if d == 0:
            return [keep[0], got[0]]
        return [keep[d], got[2 * d - 1 : 2 * d + 1]]

    return terms


def ffn_grads(ring, hidden_two, back_gate, back_up, hidden_ffn, cotangent):
    rows, width = hidden_two.shape
    units = back_gate.shape[1]
    n = ring.n
    wide = width // (2 * n) * 3
    cols = 256
    whole = pl.BlockSpec((rows, width), lambda j: (0, 0))
    block = pl.BlockSpec((rows, cols), lambda j: (0, j))
    outs = dealt(ring, shape(units // cols, wide, cols, dtype=bf16))
    cuts = [
        pl.BlockSpec(
            (*x.shape[:-3], 1, wide, cols), lambda j, k=len(x.shape): (0,) * (k - 3) + (j, 0, 0)
        )
        for x in outs
    ]
    return pl.pallas_call(
        functools.partial(grads_kernel, ring),
        grid=(units // cols,),
        out_shape=outs,
        in_specs=[whole, block, block, block, whole],
        out_specs=cuts,
        scratch_shapes=[pltpu.VMEM((width, rows), bf16), pltpu.VMEM((2 * n, wide, cols), bf16)],
        compiler_params=pltpu.CompilerParams(vmem_limit_bytes=VMEM_BYTES),
        cost_estimate=pl.CostEstimate(
            flops=6 * rows * width * units // COST_SCALE, bytes_accessed=2**20, transcendentals=0
        ),
        name="ffn_grads",
    )(hidden_two, back_gate, back_up, hidden_ffn, cotangent)


def place_kernel(ring, slots, count, *refs):
    arrays, outs, (wide_ref, down_ref, sem) = refs[:count], refs[-6:-3], refs[-3:]
    parts = [y for x in arrays for y in ([x] if len(x.shape) == 3 else [x.at[0], x.at[1]])]
    n = ring.n
    blocks, _, cols = parts[0].shape
    unit = outs[0].shape[0] // (2 * n)
    thin = cols // (2 * n)
    copies = []
    for i, slot in enumerate(slots):
        part = parts[i]
        place, core = ring.at(slot)
        r = core * n + place
        for w in range(2):
            for j in range(blocks):
                wide_ref[i, w, :, j * cols : (j + 1) * cols] = part[
                    j, w * unit : (w + 1) * unit
                ].astype(f32)
            rows = pl.ds(pl.multiple_of(r * unit, unit), unit)
            copies.append((wide_ref.at[i, w], outs[w].at[rows]))
        for j in range(blocks):
            for k in range(outs[2].shape[1] // cols):
                at = 2 * unit + k * thin
                down_ref[i, j, :, k * cols : (k + 1) * cols] = part[j, at : at + thin].astype(f32)
            rows = pl.ds(pl.multiple_of(j * cols + r * thin, thin), thin)
            copies.append((down_ref.at[i, j], outs[2].at[rows]))
        for k in range(i * (2 + blocks), (i + 1) * (2 + blocks)):
            pltpu.make_async_copy(*copies[k], sem.at[k]).start()
    for k, pair in enumerate(copies):
        pltpu.make_async_copy(*pair, sem.at[k]).wait()


def place_ffn(ring, pieces, width, held):
    slots, parts = [x for xs, _ in pieces for x in xs], [x for _, x in pieces]
    blocks, wide, cols = parts[0].shape[-3:]
    units = blocks * cols
    count = len(slots)
    thin = cols // (2 * ring.n)
    anywhere = pl.BlockSpec(memory_space=pl.ANY)
    return pl.pallas_call(
        functools.partial(place_kernel, ring, slots, len(parts)),
        out_shape=[shape(width, units), shape(width, units), shape(units, width)],
        in_specs=[in_vmem()] * len(parts) + [anywhere] * len(held),
        out_specs=[anywhere] * 3,
        input_output_aliases={len(parts) + i: i for i in range(len(held))},
        scratch_shapes=[
            pltpu.VMEM((count, 2, width // (2 * ring.n), units), f32),
            pltpu.VMEM((count, blocks, thin, width), f32),
            pltpu.SemaphoreType.DMA((count * (2 + blocks),)),
        ],
        compiler_params=pltpu.CompilerParams(vmem_limit_bytes=VMEM_BYTES),
        cost_estimate=pl.CostEstimate(
            flops=0, bytes_accessed=8 * count * wide * units, transcendentals=0
        ),
        name="place_ffn",
    )(*parts, *held)


def place_qkv_kernel(ring, slots, *refs):
    arrays, (query_ref, key_ref, value_ref, out_ref) = refs[:-4], refs[-4:]
    parts = [y for x in arrays for y in ([x] if len(x.shape) == 2 else [x.at[0], x.at[1]])]
    n = ring.n
    unit, thin = query_ref.shape[0] // (2 * n), out_ref.shape[0] // (2 * n)
    for slot, part in zip(slots, parts):
        place, core = ring.at(slot)
        r = core * n + place
        rows = pl.ds(pl.multiple_of(r * unit, unit), unit)
        at = query_ref.shape[1]
        query_ref[rows] = part[:unit, :at].astype(f32)
        for h in range(key_ref.shape[1] // HEAD_SIZE):
            cols = slice(h * HEAD_SIZE, (h + 1) * HEAD_SIZE)
            both = part[:unit, at + h * LANES : at + (h + 1) * LANES].astype(f32)
            key_ref[rows, cols] = both[:, :HEAD_SIZE]
            value_ref[rows, cols] = both[:, HEAD_SIZE:]
        rows = pl.ds(pl.multiple_of(r * thin, thin), thin)
        out_ref[rows] = part[unit:].astype(f32)


def place_qkv(ring, pieces, width, cols):
    slots, parts = [x for xs, _ in pieces for x in xs], [x for _, x in pieces]
    thin = parts[0].shape[-2] - width // (2 * ring.n)
    return whole_call(
        functools.partial(place_qkv_kernel, ring, slots),
        "place_qkv",
        [shape(width, c) for c in cols] + [shape(thin * 2 * ring.n, width)],
        parts,
        0,
    )


def whole_call(kernel, name, outs, args, flops, scratch=(), scalars=(0, 0)):
    moved = sum(x.size * x.dtype.itemsize for x in (*outs, *args))
    return pl.pallas_call(
        kernel,
        out_shape=list(outs),
        in_specs=[in_smem()] * scalars[0] + [in_vmem()] * (len(args) - scalars[0]),
        out_specs=[in_smem()] * scalars[1] + [in_vmem()] * (len(outs) - scalars[1]),
        scratch_shapes=list(scratch),
        compiler_params=pltpu.CompilerParams(vmem_limit_bytes=VMEM_BYTES),
        cost_estimate=pl.CostEstimate(
            flops=flops // COST_SCALE, bytes_accessed=moved // COST_SCALE, transcendentals=0
        ),
        name=name,
    )(*args)


def shape(*dims, dtype=f32):
    return jax.ShapeDtypeStruct(dims, dtype)


def first_lanes(rows):
    return lax.broadcasted_iota(jnp.int32, (rows, LANES), 1) < HEAD_SIZE


def head_mean(x):
    i = lax.broadcasted_iota(jnp.int32, (LANES, LANES), 0) // HEAD_SIZE
    j = lax.broadcasted_iota(jnp.int32, (LANES, LANES), 1) // HEAD_SIZE
    mean = jnp.where(i == j, 1.0 / HEAD_SIZE, 0.0).astype(bf16)
    high = x.astype(bf16)
    low = (x - high.astype(f32)).astype(bf16)
    return jnp.dot(high, mean, preferred_element_type=f32) + jnp.dot(
        low, mean, preferred_element_type=f32
    )


def turn(x, cosine, sines):
    lane = lax.broadcasted_iota(jnp.int32, x.shape, 1) % HEAD_SIZE
    half = HEAD_SIZE // 2
    other = jnp.where(
        lane < half, pltpu.roll(x, LANES - half, axis=1), pltpu.roll(x, half, axis=1)
    )
    return x * cosine + other * sines


def row_scale(x):
    return lax.rsqrt(jnp.mean(x * x, axis=-1, keepdims=True) + EPSILON)


def norm_back(upstream, x, scale, gain):
    inner = upstream * gain
    return scale * (inner - x * (scale * scale * jnp.mean(inner * x, axis=-1, keepdims=True)))


def head_norm_back(upstream, x, gain):
    scale = lax.rsqrt(head_mean(x * x) + EPSILON)
    inner = upstream * gain
    back = scale * (inner - x * (scale * scale * head_mean(inner * x)))
    return back, jnp.sum(upstream * x * scale, axis=0, keepdims=True)


def lanes(tile):
    return slice(tile * LANES, (tile + 1) * LANES)


def project_kv_kernel(
    tiles, last, order, segments, tokens, gain, w_key, w_value, key_gain, inverse, *refs
):
    starts, hidden, kv_raw, kv, w_kv, cosine, sines = refs
    x = tokens[...].astype(f32)
    hidden[...] = (x * row_scale(x) * gain[...]).astype(bf16)
    rows = x.shape[0]
    blk = rows // tiles
    mine = order[lax.axis_index("ctx")]
    lane = lax.broadcasted_iota(jnp.int32, (blk, LANES), 1) % HEAD_SIZE
    for t in range(tiles):
        block = last - mine if t % 2 else mine
        place = block * blk + lax.broadcasted_iota(jnp.int32, (blk, LANES), 0)
        angles = place.astype(f32) * inverse[...]
        at = slice(t * blk, (t + 1) * blk)
        cosine[at] = jnp.cos(angles)
        sine = jnp.sin(angles)
        sines[at] = jnp.where(lane < HEAD_SIZE // 2, -sine, sine)
    first = first_lanes(rows)
    for h in range(kv.shape[1] // LANES):
        cols = slice(h * HEAD_SIZE, (h + 1) * HEAD_SIZE)
        w_kv[:, lanes(h)] = jnp.concatenate([w_key[:, cols], w_value[:, cols]], axis=1)
        raw = jnp.dot(hidden[...], w_kv[:, lanes(h)], preferred_element_type=f32)
        kv_raw[:, lanes(h)] = raw
        normed = raw * lax.rsqrt(head_mean(raw * raw) + EPSILON) * key_gain[...]
        kv[:, lanes(h)] = jnp.where(first, turn(normed, cosine[...], sines[...]), raw).astype(bf16)
    for seq in range(segments.shape[0]):
        for d in range(3):
            before = jnp.where(segments[seq : seq + 1] <= d, 1.0, 0.0)
            starts[seq, d] = jnp.sum(before).astype(jnp.int32)


def project_q_kernel(tiles, hidden, w_query, query_gain, cosine, sines, query_raw, q_tiles):
    rows = hidden.shape[0]
    blk = rows // tiles
    first = first_lanes(rows)
    for h in range(q_tiles.shape[0]):
        raw = jnp.dot(hidden[...], w_query[:, lanes(h)], preferred_element_type=f32)
        query_raw[:, lanes(h)] = raw
        normed = raw * lax.rsqrt(head_mean(raw * raw) + EPSILON) * query_gain[...]
        turned = turn(normed, cosine[...], sines[...]).astype(bf16).astype(f32) * 0.125
        pair = [
            jnp.where(first, turned, 0.0),
            jnp.where(first, pltpu.roll(turned, HEAD_SIZE, axis=1), 0.0),
        ]
        for g, one in enumerate(pair):
            for t in range(tiles):
                q_tiles[h, t, g * blk : (g + 1) * blk] = one[t * blk : (t + 1) * blk].astype(bf16)


def mix_kernel(acc, w_out, *refs):
    attended, o, lse, halves = refs[0], refs[1], refs[2], refs[3:]
    heads, tiles, rows, _ = acc.shape
    blk = rows // 2
    first = first_lanes(rows)
    for h in range(heads):
        for t in range(tiles):
            x = acc[h, t]
            value = jnp.where(first, 0.0, x * pltpu.roll(1.0 / x, HEAD_SIZE, axis=1))
            o[h, t] = value
            lse[h, t] = jnp.log2(x.T[:8])
            low = pltpu.roll(value[:blk], HEAD_SIZE, axis=1) + value[blk:]
            attended[t * blk : (t + 1) * blk, lanes(h)] = low.astype(bf16)
    part = attended.shape[0] // len(halves)
    for i, half in enumerate(halves):
        half[...] = jnp.dot(
            attended[i * part : (i + 1) * part], w_out[...], preferred_element_type=f32
        ).astype(bf16)


def ffn_kernel(
    terms,
    tokens,
    gain,
    hidden_back,
    w_gate,
    w_up,
    *refs,
):
    mine, theirs, refs = refs[:terms], refs[terms : 2 * terms], refs[2 * terms :]
    mixed, hidden_two, hidden_ffn, back_gate, back_up, gain_grad = refs[:6]
    halves, sums = refs[6:-1], refs[-1]
    step, last = pl.program_id(0), pl.num_programs(0) - 1

    @pl.when(step == 0)
    def _():
        part = tokens.shape[0] // terms
        for i in range(terms):
            rows = slice(i * part, (i + 1) * part)
            x = tokens[rows].astype(f32) + (mine[i][...].astype(f32) + theirs[i][...].astype(f32))
            mixed[rows] = x
            hidden_two[rows] = (x * row_scale(x) * gain[...]).astype(bf16)
        sums[...] = jnp.zeros_like(sums)

    gating = jnp.dot(hidden_two[...], w_gate[...], preferred_element_type=f32)
    lifted = jnp.dot(hidden_two[...], w_up[...], preferred_element_type=f32)
    upstream = hidden_back[...]
    logistic = jax.nn.sigmoid(gating)
    silu = gating * logistic
    hidden_ffn[...] = (silu * lifted).astype(bf16)
    back_gate[...] = (
        upstream * lifted * logistic * (1.0 + gating * (1.0 - logistic))
    ).astype(bf16)
    back_up[...] = (upstream * silu).astype(bf16)
    sums[...] += lax.dot_general(
        back_gate[...], w_gate[...], NT, preferred_element_type=f32
    ) + lax.dot_general(back_up[...], w_up[...], NT, preferred_element_type=f32)

    @pl.when(step == last)
    def _():
        x = mixed[...]
        gain_grad[...] = jnp.sum(sums[...] * x * row_scale(x), axis=0, keepdims=True)
        part = sums.shape[0] // len(halves)
        for i, half in enumerate(halves):
            half[...] = sums[i * part : (i + 1) * part].astype(bf16)


def feed_forward(tokens, gain, hidden_back, w_gate, w_up, mine, theirs):
    rows, width = tokens.shape
    units = w_gate.shape[1]
    cols = FFN_COLS if units % FFN_COLS == 0 else units
    whole = pl.BlockSpec((rows, width), lambda j: (0, 0))
    line = pl.BlockSpec((1, width), lambda j: (0, 0))
    block = pl.BlockSpec((rows, cols), lambda j: (0, j))
    weight = pl.BlockSpec((width, cols), lambda j: (0, j))
    part = pl.BlockSpec((rows // len(mine), width), lambda j: (0, 0))
    half = pl.BlockSpec((rows // 2, width), lambda j: (0, 0))
    low = shape(rows, units, dtype=bf16)
    return pl.pallas_call(
        functools.partial(ffn_kernel, len(mine)),
        grid=(units // cols,),
        out_shape=[shape(rows, width), shape(rows, width, dtype=bf16), low, low, low]
        + [shape(1, width)]
        + [shape(rows // 2, width, dtype=bf16)] * 2,
        in_specs=[whole, line, block, weight, weight] + [part] * (2 * len(mine)),
        out_specs=[whole, whole, block, block, block, line, half, half],
        scratch_shapes=[pltpu.VMEM((rows, width), f32)],
        compiler_params=pltpu.CompilerParams(vmem_limit_bytes=VMEM_BYTES),
        cost_estimate=pl.CostEstimate(
            flops=8 * rows * width * units // COST_SCALE, bytes_accessed=2**20, transcendentals=0
        ),
        name="feed_forward",
    )(tokens, gain, hidden_back, w_gate, w_up, *mine, *theirs)


def back_kernel(terms, cotangent, mixed, gain, w_out, o, lse, *refs):
    mine, theirs, (back_mixed, back_proj, do_tiles, stats) = (
        refs[:terms],
        refs[terms : 2 * terms],
        refs[2 * terms :],
    )
    part = cotangent.shape[0] // terms
    for i in range(terms):
        rows = slice(i * part, (i + 1) * part)
        x = mixed[rows]
        upstream = mine[i][...].astype(f32) + theirs[i][...].astype(f32)
        back = cotangent[rows].astype(f32) + norm_back(upstream, x, row_scale(x), gain[...])
        back_mixed[rows] = back
        back_proj[rows] = back.astype(bf16)
    heads, tiles, rows, _ = o.shape
    blk = rows // 2
    first = first_lanes(blk)
    row = lax.broadcasted_iota(jnp.int32, (8, rows), 0)
    for h in range(heads):
        attn = lax.dot_general(back_proj[...], w_out[lanes(h)], NT, preferred_element_type=f32)
        for t in range(tiles):
            here = attn[t * blk : (t + 1) * blk]
            do = jnp.concatenate(
                [
                    jnp.where(first, 0.0, pltpu.roll(here, HEAD_SIZE, axis=1)),
                    jnp.where(first, 0.0, here),
                ],
                axis=0,
            ).astype(bf16)
            do_tiles[h, t] = do
            delta = jnp.sum((do.astype(f32) * o[h, t]).T, axis=0, keepdims=True)
            stats[h, t] = jnp.where(row == 0, lse[h, t], delta)


def back_query_kernel(dq, query_raw, query_gain, cosine, sines, query_delta, gain_grad):
    heads, tiles, _, rows = dq.shape
    blk = rows // 2
    gain_grad[...] = jnp.zeros_like(gain_grad)
    for t in range(tiles):
        at = slice(t * blk, (t + 1) * blk)
        for h in range(heads):
            both = jnp.concatenate([dq[h, t, :, :blk], dq[h, t, :, blk:]], axis=0) * 0.125
            turned = turn(both.T, cosine[at], -sines[at])
            back, gain_terms = head_norm_back(turned, query_raw[at, lanes(h)], query_gain[...])
            query_delta[at, lanes(h)] = back.astype(bf16)
            gain_grad[...] += gain_terms


def back_project_kernel(
    ring,
    tokens,
    hidden,
    query_delta,
    own_dkv,
    kv_raw,
    key_gain,
    cosine,
    sines,
    w_query,
    w_kv,
    attended,
    back_proj,
    *refs,
):
    low, norm_grad, gain_grad, kv_delta = refs[:4]
    outs, all_ref = refs[4:-1], refs[-1]
    rows, width = tokens.shape
    first = first_lanes(rows)
    gain_grad[...] = jnp.zeros_like(gain_grad)
    for h in range(own_dkv.shape[1] // LANES):
        dkv = own_dkv[:, lanes(h)].astype(f32)
        turned = turn(dkv, cosine[...], -sines[...])
        back, gain_terms = head_norm_back(turned, kv_raw[:, lanes(h)], key_gain[...])
        kv_delta[:, lanes(h)] = jnp.where(first, back, dkv).astype(bf16)
        gain_grad[...] += gain_terms
    part = lax.dot_general(
        query_delta[...], w_query[...], NT, preferred_element_type=f32
    ) + lax.dot_general(kv_delta[...], w_kv[...], NT, preferred_element_type=f32)
    low[...] = part.astype(bf16)
    x = tokens[...].astype(f32)
    norm_grad[...] = jnp.sum(part * x * row_scale(x), axis=0, keepdims=True)
    if not outs:
        return
    lhs = hidden[...].T
    n = ring.n
    unit = width // (2 * n)
    q_cols = query_delta.shape[1]
    for cols, right in (
        (slice(0, q_cols), query_delta),
        (slice(q_cols, q_cols + kv_delta.shape[1]), kv_delta),
    ):
        grad = jnp.dot(lhs, right[...], preferred_element_type=f32).astype(bf16)
        all_ref[:, :unit, cols] = grad.reshape(2 * n, unit, grad.shape[1])
    grad = jnp.dot(attended[...].T, back_proj[...], preferred_element_type=f32).astype(bf16)
    all_ref[:, unit:] = grad.reshape(2 * n, -1, width)
    deal(ring, lambda at: all_ref[at], lambda ref, x: ref.__setitem__(..., x), outs)


def dot(a, b, dims):
    return lax.dot_general(a, b, ((dims[:1], dims[1:]), ((), ())), preferred_element_type=f32)


def on_device(
    tokens,
    cotangent,
    block_order,
    segment_ids,
    norm_gain,
    w_query,
    key_weight,
    value_weight,
    query_gain,
    key_gain,
    w_out,
    ffn_gain,
    w_gate,
    w_up,
    w_down,
):
    devices = lax.axis_size("ctx")
    ring = Ring(devices)
    far = ring.n // 2
    rows, width = tokens.shape
    seq_count = segment_ids.shape[0]
    blk = rows // seq_count // 2
    tiles = 2 * seq_count
    kv_heads = key_weight.shape[1] // HEAD_SIZE
    q_cols, k_cols = w_query.shape[1], key_weight.shape[1]
    units = w_gate.shape[1]
    packed = units % 256 == 0 and width % (32 * ring.n) == 0 and w_out.shape[0] % (32 * ring.n) == 0
    pair = lax.axis_size("tp") == 2

    def shared(halves):
        if pair:
            return from_other(halves), list(halves)
        return [lax.psum(x, "tp") for x in halves], [jnp.zeros_like(x) for x in halves]

    def line(x):
        return x.astype(f32).reshape(1, -1)

    def head_line(x):
        return jnp.tile(line(x), (1, 2))

    inverse = ROPE_BASE ** (-np.arange(0, HEAD_SIZE, 2) / HEAD_SIZE)
    inverse = np.tile(inverse, 4)[None, :].astype(np.float32)
    starts, hidden_input, kv_raw, own_kv, w_kv, cosine, sines = whole_call(
        functools.partial(project_kv_kernel, tiles, 2 * devices - 1),
        "project_kv",
        [
            shape(seq_count, 3, dtype=jnp.int32),
            shape(rows, width, dtype=bf16),
            shape(rows, 2 * k_cols),
            shape(rows, 2 * k_cols, dtype=bf16),
            shape(width, 2 * k_cols, dtype=bf16),
            shape(rows, LANES),
            shape(rows, LANES),
        ],
        [
            block_order,
            segment_ids,
            tokens,
            line(norm_gain),
            key_weight,
            value_weight,
            head_line(key_gain),
            jnp.asarray(inverse),
        ],
        4 * rows * width * k_cols,
        scalars=(1, 1),
    )
    gather = RingGather(ring, own_kv)
    flying = gather.send(gather.sends())
    query_raw, q_tiles = whole_call(
        functools.partial(project_q_kernel, tiles),
        "project_q",
        [shape(rows, q_cols), shape(kv_heads, tiles, 2 * blk, LANES, dtype=bf16)],
        [hidden_input, w_query, head_line(query_gain), cosine, sines],
        2 * rows * width * q_cols,
    )

    attention = Attention(ring, block_order, starts, blk)
    acc = attention.forward(gather.pieces[:1], q_tiles, None)
    late = gather.pieces[1]
    while True:
        *came, acc = lax.optimization_barrier((*flying, acc))
        now = gather.arrive(came)
        if gather.done():
            break
        flying = gather.send(gather.sends())
        acc = attention.forward([late, *now], q_tiles, acc)
        late = gather.pieces[-1]
        if gather.step == far:
            acc = attention.forward([late], q_tiles, acc)
    acc = attention.forward(gather.pieces[-2:], q_tiles, acc)
    kv_pieces = {
        max(abs(d) for d, _ in slots): gather.pieces[i - 1 : i + 1]
        for i, (slots, _) in enumerate(gather.pieces)
        if i % 2
    }
    attended, o, lse, *mix_halves = whole_call(
        mix_kernel,
        "mix",
        [
            shape(rows, q_cols, dtype=bf16),
            shape(*acc.shape),
            shape(kv_heads, tiles, 8, 2 * blk),
            shape(rows // 2, width, dtype=bf16),
            shape(rows // 2, width, dtype=bf16),
        ],
        [acc, w_out],
        2 * rows * width * q_cols,
    )
    theirs, mine = shared(mix_halves)
    back_hidden = dot(cotangent, w_down, (1, 1))
    back_hidden, *theirs = lax.optimization_barrier((back_hidden, *theirs))

    mixed, hidden_two, hidden_ffn, back_gate, back_up, grad_ffn_gain, *halves = feed_forward(
        tokens, line(ffn_gain), back_hidden, w_gate, w_up, mine, theirs
    )
    if packed:
        first, mine_first = shared(halves[:1])
        dealt_out = ffn_grads(ring, hidden_two, back_gate, back_up, hidden_ffn, cotangent)
        second, first[0], *dealt_out = lax.optimization_barrier((halves[1], first[0], *dealt_out))
        second, mine_second = shared([second])
        hidden_ffn, dealt_out[0] = lax.optimization_barrier((hidden_ffn, dealt_out[0]))
        output_part = dot(hidden_ffn, w_down, (1, 0)).astype(bf16)
        ffn_box = []
        ffn_sum = Steps(sum_steps(ring, dealt_terms(ring, dealt_out), ffn_box))
        advance([ffn_sum])
        *theirs, output_part = advance([ffn_sum], first[0], second[0], output_part)
        mine = mine_first + mine_second
    else:
        theirs, mine = shared(halves)
        grad_w_down = dot(hidden_ffn, cotangent, (0, 0)).astype(bf16)
        grad_w_gate = dot(hidden_two, back_gate, (0, 0)).astype(bf16)
        grad_w_up = dot(hidden_two, back_up, (0, 0)).astype(bf16)
        grad_w_gate, grad_w_up, grad_w_down = sum_over_ctx(
            ring, [grad_w_gate, grad_w_up, grad_w_down]
        )
        ffn_sum = None
        output_part = dot(hidden_ffn, w_down, (1, 0)).astype(bf16)
    back_mixed, back_proj, do_tiles, stats = whole_call(
        functools.partial(back_kernel, 2),
        "back",
        [
            shape(rows, width),
            shape(rows, width, dtype=bf16),
            shape(*q_tiles.shape, dtype=bf16),
            shape(*lse.shape),
        ],
        [cotangent, mixed, line(ffn_gain), w_out, o, lse, *mine, *theirs],
        2 * rows * width * q_cols,
    )
    output_swap = Steps(exchange_steps(output_part)) if pair else None
    dq = None
    terms = {}

    dkv_sum = Steps(sum_steps(ring, lambda d: terms[d]))
    for d in range(far, -1, -1):
        if d < far:
            chains = [ffn_sum, dkv_sum if d < far - 1 else None]
            if d == 0:
                chains.append(output_swap)
            do_tiles, dq = advance(chains, do_tiles, dq)
        dq, keep, give = attention.backward(kv_pieces[d], q_tiles, do_tiles, stats, dq)
        terms[d] = [keep, ring.sibling(give)]
    placed, done = [], 0
    (dq,) = advance([None if LATE else ffn_sum, dkv_sum], dq)
    query_delta, grad_query_gain = whole_call(
        back_query_kernel,
        "back_query",
        [shape(rows, q_cols, dtype=bf16), shape(1, LANES)],
        [dq, query_raw, head_line(query_gain), cosine, sines],
        2 * rows * width,
    )
    if packed:
        placed, done = place_ffn(ring, ffn_box[0].pieces[:4], width, []), 4
    query_delta, *placed = advance([dkv_sum], query_delta, *placed)
    own_dkv = dkv_sum.result
    wide = width // (2 * ring.n) + w_out.shape[0] // (2 * ring.n)
    one_low, grad_norm_gain, grad_key_gain, kv_delta, *cuts = whole_call(
        functools.partial(back_project_kernel, ring),
        "back_project",
        [
            shape(rows, width, dtype=bf16),
            shape(1, width),
            shape(1, LANES),
            shape(rows, 2 * k_cols, dtype=bf16),
        ]
        + (dealt(ring, shape(wide, width, dtype=bf16)) if packed else []),
        [
            tokens,
            hidden_input,
            query_delta,
            own_dkv,
            kv_raw,
            head_line(key_gain),
            cosine,
            sines,
            w_query,
            w_kv,
            attended,
            back_proj,
        ],
        4 * rows * width * (q_cols + 2 * k_cols),
        [pltpu.VMEM((2 * ring.n, wide, width), bf16)],
    )

    gains = jnp.concatenate(
        [
            grad_norm_gain[0],
            grad_ffn_gain[0],
            grad_query_gain[0, :HEAD_SIZE] + grad_query_gain[0, HEAD_SIZE:],
            grad_key_gain[0, :HEAD_SIZE],
        ]
    )
    gain_sum = Steps(pair_steps(gains, [("tp", lax.axis_size("tp")), ("ctx", devices)]))
    one_swap = Steps(exchange_steps(one_low)) if pair else None
    if packed:
        qkv_box = []
        qkv_sum = Steps(sum_steps(ring, dealt_terms(ring, cuts), qkv_box))
        gather = ffn_box[0]
        round_at = 0
        while qkv_sum.generator is not None:
            came = len(gather.pieces)
            chains = [ffn_sum if round_at % 2 == 0 else None, qkv_sum, gain_sum]
            if round_at == 0:
                chains.append(output_swap)
            elif round_at in (1, 4):
                chains.append(one_swap)
            placed = advance(chains, *placed)
            if came > done:
                placed = place_ffn(ring, gather.pieces[done:came], width, placed)
                done = came
            round_at += 1
        if done < len(gather.pieces):
            placed = place_ffn(ring, gather.pieces[done:], width, placed)
        grad_w_gate, grad_w_up, grad_w_down = placed
        grad_w_query, grad_w_key, grad_w_value, grad_w_out = place_qkv(
            ring, qkv_box[0].pieces, width, (q_cols, k_cols, k_cols)
        )
    else:
        while gain_sum.generator is not None:
            advance([gain_sum])
        grad_w_query, grad_kv, grad_w_out = sum_over_ctx(
            ring,
            [
                dot(hidden_input, query_delta, (0, 0)).astype(bf16),
                dot(hidden_input, kv_delta, (0, 0)).astype(bf16),
                dot(attended, back_proj, (0, 0)).astype(bf16),
            ],
        )
        grad_kv = grad_kv.reshape(width, kv_heads, 2, HEAD_SIZE)
        grad_w_key = grad_kv[:, :, 0].reshape(width, k_cols)
        grad_w_value = grad_kv[:, :, 1].reshape(width, k_cols)
    gains = gain_sum.result
    if pair:
        for swap in (output_swap, one_swap):
            while swap.generator is not None:
                advance([swap])
        output = output_part.astype(f32) + output_swap.result.astype(f32)
        back_one = one_low.astype(f32) + one_swap.result.astype(f32)
    else:
        output = lax.psum(output_part, "tp").astype(f32)
        back_one = lax.psum(one_low, "tp").astype(f32)
    output = (mixed + output).astype(bf16)
    inputs = tokens.astype(f32)
    input_grad = back_mixed + norm_back(back_one, inputs, row_scale(inputs), norm_gain)

    return (
        output,
        input_grad,
        gains[:width],
        grad_w_query,
        grad_w_key,
        grad_w_value,
        gains[2 * width : 2 * width + HEAD_SIZE],
        gains[2 * width + HEAD_SIZE :],
        grad_w_out,
        gains[width : 2 * width],
        grad_w_gate,
        grad_w_up,
        grad_w_down,
    )


def solution(mesh):
    return jax.shard_map(
        on_device,
        mesh=mesh,
        in_specs=(
            P("ctx", None),
            P("ctx", None),
            P(),
            P(),
            P(),
            P(None, "tp"),
            P(None, "tp"),
            P(None, "tp"),
            P(),
            P(),
            P("tp", None),
            P(),
            P(None, "tp"),
            P(None, "tp"),
            P("tp", None),
        ),
        out_specs=(
            P("ctx", None),
            P("ctx", None),
            P(),
            P(None, "tp"),
            P(None, "tp"),
            P(None, "tp"),
            P(),
            P(),
            P("tp", None),
            P(),
            P(None, "tp"),
            P(None, "tp"),
            P("tp", None),
        ),
        check_vma=False,
    )
```

profile of v0, /device:TPU:0, one launch (start us, length us, event | category | flops | bytes accessed | tf_op | source)
XLA Modules:
  0.0 440.3 jit_solution(17748888187925309445)
XLA Ops:
  7.5 5.7 %project_kv.1 = (s32[1,3]{1,0:T(1,128)S(1)}, bf16[512,1024]{1,0:T(8,128)(2,1)S(1)}, f32[512,512]{1,0:T(8,128)S(1)}, bf16[512,512]{1,0:T(8,128)(2,1)}, bf16[1024,...) custom-call(s32[16]{0:T(128)S(1)} %copy-done.33, s32[1,8192]{1,0:T(1,128)S(1)} %copy-done.32, ...), custom_call_target="tpu_custom_call" | custom-call | flops 536870912 | bytes 6329420 | tf_op jit(solution)/shard_map/project_kv/pallas_call | solution.py:633
  22.2 4.3 attend_forward.6.refs_3_
  37.5 6.7 %attend_forward.7.refs_2_ = f32[4,2,512,128]{3,2,1,0:T(8,128)S(1)} custom-call(s32[16]{0:T(128)S(1)} %copy-done.34, s32[1,3]{1,0:T(1,128)S(1)} %get-tuple-element.263.starts_ref, bf16[4,2,512,128]{3,2,1,0:T(8,128)(2,1)S(1)} %get-tuple-element.267.q_ref, bf16[512,512]{1,0:T(8,128)(2,1)S(1)} %collective-permute-done.3.refs_0_.refs_1_, ...), custom_call_target="tpu_custom_call" | custom-call | flops 3221225472 | bytes 6815744 | tf_op jit(solution)/shard_map/attend_forward/pallas_call | solution.py:414
  49.6 7.9 %attend_forward.8.refs_2_ = f32[4,2,512,128]{3,2,1,0:T(8,128)S(1)} custom-call(s32[16]{0:T(128)S(1)} %copy-done.34, s32[1,3]{1,0:T(1,128)S(1)} %get-tuple-element.263.starts_ref, bf16[4,2,512,128]{3,2,1,0:T(8,128)(2,1)S(1)} %get-tuple-element.267.q_ref, bf16[2,512,512]{2,1,0:T(8,128)(2,1)S(1)} %collective-permute-done.5.refs_0_.refs_1_, ...), custom_call_target="tpu_custom_call" | custom-call | flops 4294967296 | bytes 7340032 | tf_op jit(solution)/shard_map/attend_forward/pallas_call | solution.py:414
  57.5 4.8 %collective-permute-done.4.refs_1_.refs_0_ = bf16[2,512,512]{2,1,0:T(8,128)(2,1)S(1)} collective-permute-done((bf16[2,512,512]{2,1,0:T(8,128)(2,1)S(1)}, bf16[2,512,512]{2,1,0:T(8,128)(2,1)S(1)}, u32[]{:S(2)}, u32[]{:S(2)}) %collective-permute-start.4) | collective-permute-done | bytes 1048608 | tf_op jit(solution)/shard_map/ppermute | solution.py:70
  64.5 7.8 %attend_forward.9.refs_1_ = f32[4,2,512,128]{3,2,1,0:T(8,128)S(1)} custom-call(s32[16]{0:T(128)S(1)} %copy-done.34, s32[1,3]{1,0:T(1,128)S(1)} %get-tuple-element.263.starts_ref, bf16[4,2,512,128]{3,2,1,0:T(8,128)(2,1)S(1)} %get-tuple-element.267.q_ref, bf16[2,512,512]{2,1,0:T(8,128)(2,1)S(1)} %collective-permute-done.8.refs_0_.refs_1_, ...), custom_call_target="tpu_custom_call" | custom-call | flops 4294967296 | bytes 7340032 | tf_op jit(solution)/shard_map/attend_forward/pallas_call | solution.py:414
  72.4 4.3 attend_forward.10.refs_2_
  78.7 4.2 attend_forward.11.acc
  87.5 4.3 fusion.25.hidden_back
  91.8 8.3 %collective-permute-done.10.refs_2_ = bf16[256,1024]{1,0:T(8,128)(2,1)S(1)} collective-permute-done((bf16[256,1024]{1,0:T(8,128)(2,1)S(1)}, bf16[256,1024]{1,0:T(8,128)(2,1)S(1)}, u32[]{:S(2)}, u32[]{:S(2)}) %collective-permute-start.10) | collective-permute-done | bytes 524320 | tf_op jit(solution)/shard_map/ppermute | solution.py:239
  100.2 10.5 %collective-permute-done.11.refs_3_ = bf16[256,1024]{1,0:T(8,128)(2,1)S(1)} collective-permute-done((bf16[256,1024]{1,0:T(8,128)(2,1)S(1)}, bf16[256,1024]{1,0:T(8,128)(2,1)S(1)}, u32[]{:S(2)}, u32[]{:S(2)}) %collective-permute-start.11) | collective-permute-done | bytes 524320 | tf_op jit(solution)/shard_map/ppermute | solution.py:239
  113.0 14.2 %feed_forward.1 = (f32[512,1024]{1,0:T(8,128)S(1)}, bf16[512,1024]{1,0:T(8,128)(2,1)S(1)}, bf16[512,2304]{1,0:T(8,128)(2,1)S(1)}, bf16[512,2304]{1,0:T(8,128)(2,...) custom-call(bf16[512,1024]{1,0:T(8,128)(2,1)S(1)} %copy-done.1, ...), custom_call_target="tpu_custom_call" | custom-call | flops 9663676416 | bytes 1048576 | tf_op jit(solution)/shard_map/feed_forward/pallas_call | solution.py:823
  134.9 11.7 %ffn_grads.1 = (bf16[9,192,256]{2,1,0:T(8,128)(2,1)S(1)}, bf16[9,192,256]{2,1,0:T(8,128)(2,1)S(1)}, bf16[9,192,256]{2,1,0:T(8,128)(2,1)S(1)}, bf16[2,9,192,256]{...) custom-call(bf16[512,1024]{1,0:T(8,128)(2,1)S(1)} %get-tuple-element, ...), custom_call_target="tpu_custom_call" | custom-call | flops 7247757312 | bytes 1048576 | tf_op jit(solution)/shard_map/ffn_grads/pallas_call | solution.py:527
  150.1 5.9 %convolution_convert_fusion = bf16[512,1024]{1,0:T(8,128)(2,1)} fusion(bf16[512,2304]{1,0:T(8,128)(2,1)S(1)} %copy-done.54, bf16[2304,1024]{1,0:T(8,128)(2,1)} %param.30), kind=kOutput, calls=%fused_computation.24 | convolution fusion | flops 2416443392 | bytes 8126464 | tf_op jit(solution)/shard_map/dot_general | solution.py:939
  156.0 7.8 %collective-permute-done.16.refs_3_ = bf16[256,1024]{1,0:T(8,128)(2,1)S(1)} collective-permute-done((bf16[256,1024]{1,0:T(8,128)(2,1)S(1)}, bf16[256,1024]{1,0:T(8,128)(2,1)S(1)}, u32[]{:S(2)}, u32[]{:S(2)}) %collective-permute-start.16) | collective-permute-done | bytes 524320 | tf_op jit(solution)/shard_map/ppermute | solution.py:239
  170.9 7.4 %attend_backward.5 = (f32[4,2,64,512]{3,2,1,0:T(8,128)S(1)}, f32[512,512]{1,0:T(8,128)S(1)}, bf16[512,512]{1,0:T(8,128)(2,1)S(1)}) custom-call(s32[16]{0:T(128)S(1)} %copy-done.34, s32[1,3]{1,0:T(1,128)S(1)} %get-tuple-element.263.starts_ref, bf16[4,2,512,128]{3,2,1,0:T(8,128)(2,1)S(1)} %copy-done.37, ...), custom_call_target="tpu_custom_call" | custom-call | flops 5368709120 | bytes 6815744 | tf_op jit(solution)/shard_map/attend_backward/pallas_call | solution.py:435
  178.4 11.6 %collective-permute-done.17 = bf16[2,9,192,256]{3,2,1,0:T(8,128)(2,1)S(1)} collective-permute-done((bf16[2,9,192,256]{3,2,1,0:T(8,128)(2,1)S(1)}, bf16[2,9,192,256]{3,2,1,0:T(8,128)(2,1)S(1)}, u32[]{:S(2)}, u32[]{:S(2)}) %collective-permute-start.17) | collective-permute-done | bytes 1769504 | tf_op jit(solution)/shard_map/ppermute | solution.py:70
  192.6 13.5 %attend_backward.6 = (f32[4,2,64,512]{3,2,1,0:T(8,128)S(1)}, f32[2,512,512]{2,1,0:T(8,128)S(1)}, bf16[2,512,512]{2,1,0:T(8,128)(2,1)S(1)}) custom-call(s32[16]{0:T(128)S(1)} %copy-done.34, s32[1,3]{1,0:T(1,128)S(1)} %get-tuple-element.263.starts_ref, bf16[4,2,512,128]{3,2,1,0:T(8,128)(2,1)S(1)} %copy-done.37, ...), custom_call_target="tpu_custom_call" | custom-call | flops 10737418240 | bytes 9437184 | tf_op jit(solution)/shard_map/attend_backward/pallas_call | solution.py:435
  210.5 4.5 %collective-permute-done.18 = bf16[2,9,192,256]{3,2,1,0:T(8,128)(2,1)S(1)} collective-permute-done((bf16[2,9,192,256]{3,2,1,0:T(8,128)(2,1)S(1)}, bf16[2,9,192,256]{3,2,1,0:T(8,128)(2,1)S(1)}, u32[]{:S(2)}, u32[]{:S(2)}) %collective-permute-start.18) | collective-permute-done | bytes 1769504 | tf_op jit(solution)/shard_map/ppermute | solution.py:70
  219.0 13.7 %attend_backward.7 = (f32[4,2,64,512]{3,2,1,0:T(8,128)S(1)}, f32[2,512,512]{2,1,0:T(8,128)S(1)}, bf16[2,512,512]{2,1,0:T(8,128)(2,1)S(1)}) custom-call(s32[16]{0:T(128)S(1)} %copy-done.34, s32[1,3]{1,0:T(1,128)S(1)} %get-tuple-element.263.starts_ref, bf16[4,2,512,128]{3,2,1,0:T(8,128)(2,1)S(1)} %copy-done.37, ...), custom_call_target="tpu_custom_call" | custom-call | flops 10737418240 | bytes 9437184 | tf_op jit(solution)/shard_map/attend_backward/pallas_call | solution.py:435
  232.7 12.9 %collective-permute-done.22 = bf16[512,512]{1,0:T(8,128)(2,1)S(1)} collective-permute-done((bf16[512,512]{1,0:T(8,128)(2,1)S(1)}, bf16[512,512]{1,0:T(8,128)(2,1)S(1)}, u32[]{:S(2)}, u32[]{:S(2)}) %collective-permute-start.22) | collective-permute-done | bytes 524320 | tf_op jit(solution)/shard_map/ppermute | solution.py:70
  251.9 13.5 %attend_backward.8 = (f32[4,2,64,512]{3,2,1,0:T(8,128)S(1)}, f32[2,512,512]{2,1,0:T(8,128)S(1)}, bf16[2,512,512]{2,1,0:T(8,128)(2,1)S(1)}) custom-call(s32[16]{0:T(128)S(1)} %copy-done.34, s32[1,3]{1,0:T(1,128)S(1)} %get-tuple-element.263.starts_ref, bf16[4,2,512,128]{3,2,1,0:T(8,128)(2,1)S(1)} %copy-done.37, ...), custom_call_target="tpu_custom_call" | custom-call | flops 10737418240 | bytes 9437184 | tf_op jit(solution)/shard_map/attend_backward/pallas_call | solution.py:435
  265.4 16.1 %collective-permute-done.24 = bf16[9,192,256]{2,1,0:T(8,128)(2,1)S(1)} collective-permute-done((bf16[9,192,256]{2,1,0:T(8,128)(2,1)S(1)}, bf16[9,192,256]{2,1,0:T(8,128)(2,1)S(1)}, u32[]{:S(2)}, u32[]{:S(2)}) %collective-permute-start.24) | collective-permute-done | bytes 884768 | tf_op jit(solution)/shard_map/ppermute | solution.py:70
  284.6 9.6 %attend_backward.9 = (f32[4,2,64,512]{3,2,1,0:T(8,128)S(1)}, f32[512,512]{1,0:T(8,128)S(1)}, bf16[512,512]{1,0:T(8,128)(2,1)S(1)}) custom-call(s32[16]{0:T(128)S(1)} %copy-done.34, s32[1,3]{1,0:T(1,128)S(1)} %get-tuple-element.263.starts_ref, bf16[4,2,512,128]{3,2,1,0:T(8,128)(2,1)S(1)} %copy-done.37, ...), custom_call_target="tpu_custom_call" | custom-call | flops 6710886400 | bytes 6815744 | tf_op jit(solution)/shard_map/attend_backward/pallas_call | solution.py:435
  302.0 4.6 %place_ffn.4 = (f32[1024,2304]{1,0:T(8,128)}, f32[1024,2304]{1,0:T(8,128)}, f32[2304,1024]{1,0:T(8,128)}) custom-call(bf16[9,192,256]{2,1,0:T(8,128)(2,1)S(1)} %fusion.7.refs_0_, bf16[9,192,256]{2,1,0:T(8,128)(2,1)S(1)} %collective-permute-done.26.refs_1_, bf16[2,9,192,256]{3,2,1,0:T(8,128)(2,1)S(1)} %pad_maximum_fusion.1.refs_2_, ...), custom_call_target="tpu_custom_call" | custom-call | bytes 21233664 | tf_op jit(solution)/shard_map/place_ffn/pallas_call | solution.py:580
  306.7 15.1 %collective-permute-done.34 = bf16[512,512]{1,0:T(8,128)(2,1)S(1)} collective-permute-done((bf16[512,512]{1,0:T(8,128)(2,1)S(1)}, bf16[512,512]{1,0:T(8,128)(2,1)S(1)}, u32[]{:S(2)}, u32[]{:S(2)}) %collective-permute-start.34) | collective-permute-done | bytes 524320 | tf_op jit(solution)/shard_map/ppermute | solution.py:70
  321.7 5.1 %collective-permute-done.35 = bf16[512,512]{1,0:T(8,128)(2,1)S(1)} collective-permute-done((bf16[512,512]{1,0:T(8,128)(2,1)S(1)}, bf16[512,512]{1,0:T(8,128)(2,1)S(1)}, u32[]{:S(2)}, u32[]{:S(2)}) %collective-permute-start.35) | collective-permute-done | bytes 524320 | tf_op jit(solution)/shard_map/ppermute | solution.py:137
  327.2 5.6 %back_project.1 = (bf16[512,1024]{1,0:T(8,128)(2,1)S(1)}, f32[1,1024]{1,0:T(1,128)S(1)}, f32[1,128]{1,0:T(1,128)S(1)}, bf16[512,512]{1,0:T(8,128)(2,1)}, bf16[96...) custom-call(bf16[512,1024]{1,0:T(8,128)(2,1)S(1)} %copy-done.1, ...), custom_call_target="tpu_custom_call" | custom-call | flops 2147483648 | bytes 13112320 | tf_op jit(solution)/shard_map/back_project/pallas_call | solution.py:633
  347.1 19.1 %collective-permute-done.41 = bf16[96,1024]{1,0:T(8,128)(2,1)S(1)} collective-permute-done((bf16[96,1024]{1,0:T(8,128)(2,1)S(1)}, bf16[96,1024]{1,0:T(8,128)(2,1)S(1)}, u32[]{:S(2)}, u32[]{:S(2)}) %collective-permute-start.41) | collective-permute-done | bytes 196640 | tf_op jit(solution)/shard_map/ppermute | solution.py:70
  369.7 5.3 %place_ffn.5 = (f32[1024,2304]{1,0:T(8,128)}, f32[1024,2304]{1,0:T(8,128)}, f32[2304,1024]{1,0:T(8,128)}) custom-call(bf16[2,9,192,256]{3,2,1,0:T(8,128)(2,1)} %collective-permute-done.29.refs_0_, bf16[2,9,192,256]{3,2,1,0:T(8,128)(2,1)} %collective-permute-done.39.refs_1_, ...), custom_call_target="tpu_custom_call", output_to_operand_aliasing={{0}: (2, {}), {1}: (3, {}), {2}: (4, {})} | custom-call | bytes 14155776 | tf_op jit(solution)/shard_map/place_ffn/pallas_call | solution.py:580
  380.6 15.2 %collective-permute-done.48 = f32[2176]{0:T(1024)S(1)} collective-permute-done((f32[2176]{0:T(1024)S(1)}, f32[2176]{0:T(1024)S(1)}, u32[]{:S(2)}, u32[]{:S(2)}) %collective-permute-start.48) | collective-permute-done | bytes 8736 | tf_op jit(solution)/shard_map/ppermute | solution.py:232
  424.7 4.7 %collective-permute-done.61.refs_6_ = bf16[2,96,1024]{2,1,0:T(8,128)(2,1)S(1)} collective-permute-done((bf16[2,96,1024]{2,1,0:T(8,128)(2,1)S(1)}, bf16[2,96,1024]{2,1,0:T(8,128)(2,1)S(1)}, u32[]{:S(2)}, u32[]{:S(2)}) %collective-permute-start.61) | collective-permute-done | bytes 393248 | tf_op jit(solution)/shard_map/ppermute | solution.py:70
  (312 shorter events, 152.2 us)
Async XLA Ops:
  32.5 14.9 %collective-permute-start.2 = (bf16[2,512,512]{2,1,0:T(8,128)(2,1)S(1)}, bf16[2,512,512]{2,1,0:T(8,128)(2,1)S(1)}, u32[]{:S(2)}, u32[]{:S(2)}) collective-permute-start(bf16[2,512,512]{2,1,0:T(8,128)(2,1)S(1)} %pad_maximum_fusion.2.refs_0_), channel_id=1, source_target_pairs={{0,8},{2,6},{8,16},{10,2},{16,24},{18,10},{24,28},{26,18},{28,20},... | collective-permute-start | bytes 3145736 | tf_op jit(solution)/shard_map/ppermute | solution.py:70
  34.6 15.0 %collective-permute-start.5 = (bf16[2,512,512]{2,1,0:T(8,128)(2,1)S(1)}, bf16[2,512,512]{2,1,0:T(8,128)(2,1)S(1)}, u32[]{:S(2)}, u32[]{:S(2)}) collective-permute-start(bf16[2,512,512]{2,1,0:T(8,128)(2,1)S(1)} %pad_maximum_fusion.2.refs_0_), channel_id=1, source_target_pairs={{0,2},{2,0},{4,6},{6,4},{8,10},{10,8},{12,14},{14,12},{16,18},{18,... | collective-permute-start | bytes 3145736 | tf_op jit(solution)/shard_map/ppermute | solution.py:73
  47.3 14.9 %collective-permute-start.4 = (bf16[2,512,512]{2,1,0:T(8,128)(2,1)S(1)}, bf16[2,512,512]{2,1,0:T(8,128)(2,1)S(1)}, u32[]{:S(2)}, u32[]{:S(2)}) collective-permute-start(bf16[2,512,512]{2,1,0:T(8,128)(2,1)S(1)} %collective-permute-done.2.refs_1_.refs_0_), channel_id=1, source_target_pairs={{0,8},{2,6},{8,16},{10,2},{16,24},{18,10},{24,28},{26,18},{28,20},... | collective-permute-start | bytes 3145736 | tf_op jit(solution)/shard_map/ppermute | solution.py:70
  49.6 14.9 %collective-permute-start.8 = (bf16[2,512,512]{2,1,0:T(8,128)(2,1)S(1)}, bf16[2,512,512]{2,1,0:T(8,128)(2,1)S(1)}, u32[]{:S(2)}, u32[]{:S(2)}) collective-permute-start(bf16[2,512,512]{2,1,0:T(8,128)(2,1)S(1)} %collective-permute-done.2.refs_1_.refs_0_), channel_id=1, source_target_pairs={{0,2},{2,0},{4,6},{6,4},{8,10},{10,8},{12,14},{14,12},{16,18},{18,... | collective-permute-start | bytes 3145736 | tf_op jit(solution)/shard_map/ppermute | solution.py:73
  86.9 23.7 %collective-permute-start.11 = (bf16[256,1024]{1,0:T(8,128)(2,1)S(1)}, bf16[256,1024]{1,0:T(8,128)(2,1)S(1)}, u32[]{:S(2)}, u32[]{:S(2)}) collective-permute-start(bf16[256,1024]{1,0:T(8,128)(2,1)S(1)} %get-tuple-element.279.refs_1_), channel_id=1, source_target_pairs={{0,1},{1,0},{2,3},{3,2},{4,5},{5,4},{6,7},{7,6},{8,9},{9,8},{10,11... | collective-permute-start | bytes 1572872 | tf_op jit(solution)/shard_map/ppermute | solution.py:239
  130.1 16.5 %collective-permute-start.12 = (bf16[256,1024]{1,0:T(8,128)(2,1)S(1)}, bf16[256,1024]{1,0:T(8,128)(2,1)S(1)}, u32[]{:S(2)}, u32[]{:S(2)}) collective-permute-start(bf16[256,1024]{1,0:T(8,128)(2,1)S(1)} %get-tuple-element.285.refs_0_), channel_id=1, source_target_pairs={{0,1},{1,0},{2,3},{3,2},{4,5},{5,4},{6,7},{7,6},{8,9},{9,8},{10,11... | collective-permute-start | bytes 1572872 | tf_op jit(solution)/shard_map/ppermute | solution.py:239
  166.9 23.1 %collective-permute-start.17 = (bf16[2,9,192,256]{3,2,1,0:T(8,128)(2,1)S(1)}, bf16[2,9,192,256]{3,2,1,0:T(8,128)(2,1)S(1)}, u32[]{:S(2)}, u32[]{:S(2)}) collective-permute-start(bf16[2,9,192,256]{3,2,1,0:T(8,128)(2,1)S(1)} %pad_maximum_fusion), channel_id=1, source_target_pairs={{0,8},{2,6},{8,16},{10,2},{16,24},{18,10},{24,28},{26,18},{28,20},... | collective-permute-start | bytes 5308424 | tf_op jit(solution)/shard_map/ppermute | solution.py:70
  192.5 22.6 %collective-permute-start.18 = (bf16[2,9,192,256]{3,2,1,0:T(8,128)(2,1)S(1)}, bf16[2,9,192,256]{3,2,1,0:T(8,128)(2,1)S(1)}, u32[]{:S(2)}, u32[]{:S(2)}) collective-permute-start(bf16[2,9,192,256]{3,2,1,0:T(8,128)(2,1)S(1)} %add_convert_fusion), channel_id=1, source_target_pairs={{0,8},{2,6},{8,16},{10,2},{16,24},{18,10},{24,28},{26,18},{28,20},... | collective-permute-start | bytes 5308424 | tf_op jit(solution)/shard_map/ppermute | solution.py:70
  217.4 28.2 %collective-permute-start.20 = (bf16[9,192,256]{2,1,0:T(8,128)(2,1)S(1)}, bf16[9,192,256]{2,1,0:T(8,128)(2,1)S(1)}, u32[]{:S(2)}, u32[]{:S(2)}) collective-permute-start(bf16[9,192,256]{2,1,0:T(8,128)(2,1)S(1)} %get-tuple-element.335), channel_id=1, source_target_pairs={{0,8},{2,6},{8,16},{10,2},{16,24},{18,10},{24,28},{26,18},{28,20},... | collective-permute-start | bytes 2654216 | tf_op jit(solution)/shard_map/ppermute | solution.py:70
  217.5 28.1 %collective-permute-start.21 = (bf16[9,192,256]{2,1,0:T(8,128)(2,1)S(1)}, bf16[9,192,256]{2,1,0:T(8,128)(2,1)S(1)}, u32[]{:S(2)}, u32[]{:S(2)}) collective-permute-start(bf16[9,192,256]{2,1,0:T(8,128)(2,1)S(1)} %get-tuple-element.336), channel_id=1, source_target_pairs={{0,10},{2,4},{8,18},{10,0},{16,26},{18,8},{24,30},{26,16},{28,22},... | collective-permute-start | bytes 2654216 | tf_op jit(solution)/shard_map/ppermute | solution.py:137
  217.6 28.0 %collective-permute-start.22 = (bf16[512,512]{1,0:T(8,128)(2,1)S(1)}, bf16[512,512]{1,0:T(8,128)(2,1)S(1)}, u32[]{:S(2)}, u32[]{:S(2)}) collective-permute-start(bf16[512,512]{1,0:T(8,128)(2,1)S(1)} %add_convert_fusion.11), channel_id=1, source_target_pairs={{0,8},{2,6},{8,16},{10,2},{16,24},{18,10},{24,28},{26,18},{28,20},... | collective-permute-start | bytes 1572872 | tf_op jit(solution)/shard_map/ppermute | solution.py:70
  247.7 33.8 %collective-permute-start.27 = (bf16[2,512,512]{2,1,0:T(8,128)(2,1)S(1)}, bf16[2,512,512]{2,1,0:T(8,128)(2,1)S(1)}, u32[]{:S(2)}, u32[]{:S(2)}) collective-permute-start(bf16[2,512,512]{2,1,0:T(8,128)(2,1)S(1)} %pad_maximum_fusion.3), channel_id=1, source_target_pairs={{0,8},{2,6},{8,16},{10,2},{16,24},{18,10},{24,28},{26,18},{28,20},... | collective-permute-start | bytes 3145736 | tf_op jit(solution)/shard_map/ppermute | solution.py:70
  247.8 34.0 %collective-permute-start.28 = (bf16[2,512,512]{2,1,0:T(8,128)(2,1)S(1)}, bf16[2,512,512]{2,1,0:T(8,128)(2,1)S(1)}, u32[]{:S(2)}, u32[]{:S(2)}) collective-permute-start(bf16[2,512,512]{2,1,0:T(8,128)(2,1)S(1)} %get-tuple-element.356), channel_id=1, source_target_pairs={{0,2},{2,0},{4,6},{6,4},{8,10},{10,8},{12,14},{14,12},{16,18},{18,... | collective-permute-start | bytes 3145736 | tf_op jit(solution)/shard_map/ppermute | solution.py:73
  247.9 33.7 %collective-permute-start.24 = (bf16[9,192,256]{2,1,0:T(8,128)(2,1)S(1)}, bf16[9,192,256]{2,1,0:T(8,128)(2,1)S(1)}, u32[]{:S(2)}, u32[]{:S(2)}) collective-permute-start(bf16[9,192,256]{2,1,0:T(8,128)(2,1)S(1)} %fusion.7.refs_0_), channel_id=1, source_target_pairs={{0,8},{2,6},{8,16},{10,2},{16,24},{18,10},{24,28},{26,18},{28,20},... | collective-permute-start | bytes 2654216 | tf_op jit(solution)/shard_map/ppermute | solution.py:70
  249.3 32.2 %collective-permute-start.25 = (bf16[9,192,256]{2,1,0:T(8,128)(2,1)S(1)}, bf16[9,192,256]{2,1,0:T(8,128)(2,1)S(1)}, u32[]{:S(2)}, u32[]{:S(2)}) collective-permute-start(bf16[9,192,256]{2,1,0:T(8,128)(2,1)S(1)} %fusion.7.refs_0_), channel_id=1, source_target_pairs={{0,6},{2,8},{8,2},{10,16},{16,10},{18,24},{24,18},{26,28},{28,26},... | collective-permute-start | bytes 2654216 | tf_op jit(solution)/shard_map/ppermute | solution.py:100
  251.7 29.9 %collective-permute-start.26 = (bf16[9,192,256]{2,1,0:T(8,128)(2,1)S(1)}, bf16[9,192,256]{2,1,0:T(8,128)(2,1)S(1)}, u32[]{:S(2)}, u32[]{:S(2)}) collective-permute-start(bf16[9,192,256]{2,1,0:T(8,128)(2,1)S(1)} %fusion.7.refs_0_), channel_id=1, source_target_pairs={{0,2},{2,0},{4,6},{6,4},{8,10},{10,8},{12,14},{14,12},{16,18},{18,... | collective-permute-start | bytes 2654216 | tf_op jit(solution)/shard_map/ppermute | solution.py:73
  281.7 18.2 %collective-permute-start.30 = (bf16[2,9,192,256]{3,2,1,0:T(8,128)(2,1)S(1)}, bf16[2,9,192,256]{3,2,1,0:T(8,128)(2,1)S(1)}, u32[]{:S(2)}, u32[]{:S(2)}) collective-permute-start(bf16[2,9,192,256]{3,2,1,0:T(8,128)(2,1)S(1)} %pad_maximum_fusion.1.refs_2_), channel_id=1, source_target_pairs={{0,2},{2,0},{4,6},{6,4},{8,10},{10,8},{12,14},{14,12},{16,18},{18,... | collective-permute-start | bytes 5308424 | tf_op jit(solution)/shard_map/ppermute | solution.py:73
  282.3 14.9 %collective-permute-start.33 = (bf16[2,512,512]{2,1,0:T(8,128)(2,1)S(1)}, bf16[2,512,512]{2,1,0:T(8,128)(2,1)S(1)}, u32[]{:S(2)}, u32[]{:S(2)}) collective-permute-start(bf16[2,512,512]{2,1,0:T(8,128)(2,1)S(1)} %add_convert_fusion.2), channel_id=1, source_target_pairs={{0,8},{2,6},{8,16},{10,2},{16,24},{18,10},{24,28},{26,18},{28,20},... | collective-permute-start | bytes 3145736 | tf_op jit(solution)/shard_map/ppermute | solution.py:70
  284.5 54.7 %collective-permute-start.29 = (bf16[2,9,192,256]{3,2,1,0:T(8,128)(2,1)S(1)}, bf16[2,9,192,256]{3,2,1,0:T(8,128)(2,1)}, u32[]{:S(2)}, u32[]{:S(2)}) collective-permute-start(bf16[2,9,192,256]{3,2,1,0:T(8,128)(2,1)S(1)} %pad_maximum_fusion.1.refs_2_), channel_id=1, source_target_pairs={{0,8},{2,6},{8,16},{10,2},{16,24},{18,10},{24,28},{26,18},{28,20},... | collective-permute-start | bytes 5308424 | tf_op jit(solution)/shard_map/ppermute | solution.py:70
  297.7 24.0 %collective-permute-start.34 = (bf16[512,512]{1,0:T(8,128)(2,1)S(1)}, bf16[512,512]{1,0:T(8,128)(2,1)S(1)}, u32[]{:S(2)}, u32[]{:S(2)}) collective-permute-start(bf16[512,512]{1,0:T(8,128)(2,1)S(1)} %get-tuple-element.370), channel_id=1, source_target_pairs={{0,8},{2,6},{8,16},{10,2},{16,24},{18,10},{24,28},{26,18},{28,20},... | collective-permute-start | bytes 1572872 | tf_op jit(solution)/shard_map/ppermute | solution.py:70
  297.8 29.1 %collective-permute-start.35 = (bf16[512,512]{1,0:T(8,128)(2,1)S(1)}, bf16[512,512]{1,0:T(8,128)(2,1)S(1)}, u32[]{:S(2)}, u32[]{:S(2)}) collective-permute-start(bf16[512,512]{1,0:T(8,128)(2,1)S(1)} %get-tuple-element.371), channel_id=1, source_target_pairs={{0,10},{2,4},{8,18},{10,0},{16,26},{18,8},{24,30},{26,16},{28,22},... | collective-permute-start | bytes 1572872 | tf_op jit(solution)/shard_map/ppermute | solution.py:137
  298.8 28.1 %collective-permute-start.36 = (bf16[512,512]{1,0:T(8,128)(2,1)S(1)}, bf16[512,512]{1,0:T(8,128)(2,1)S(1)}, u32[]{:S(2)}, u32[]{:S(2)}) collective-permute-start(bf16[512,512]{1,0:T(8,128)(2,1)S(1)} %get-tuple-element.389), channel_id=1, source_target_pairs={{0,2},{2,0},{4,6},{6,4},{8,10},{10,8},{12,14},{14,12},{16,18},{18,... | collective-permute-start | bytes 1572872 | tf_op jit(solution)/shard_map/ppermute | solution.py:73
  300.0 39.2 %collective-permute-start.31 = (bf16[512,1024]{1,0:T(8,128)(2,1)S(1)}, bf16[512,1024]{1,0:T(8,128)(2,1)S(1)}, u32[]{:S(2)}, u32[]{:S(2)}) collective-permute-start(bf16[512,1024]{1,0:T(8,128)(2,1)S(1)} %copy-done.57), channel_id=1, source_target_pairs={{0,1},{1,0},{2,3},{3,2},{4,5},{5,4},{6,7},{7,6},{8,9},{9,8},{10,11... | collective-permute-start | bytes 3145736 | tf_op jit(solution)/shard_map/ppermute | solution.py:223
  338.8 27.3 %collective-permute-start.40 = (bf16[7,96,1024]{2,1,0:T(8,128)(2,1)}, bf16[7,96,1024]{2,1,0:T(8,128)(2,1)}, u32[]{:S(2)}, u32[]{:S(2)}) collective-permute-start(bf16[7,96,1024]{2,1,0:T(8,128)(2,1)} %get-tuple-element.411), channel_id=1, source_target_pairs={{0,2},{2,0},{4,6},{6,4},{8,10},{10,8},{12,14},{14,12},{16,18},{18,... | collective-permute-start | bytes 4128776 | tf_op jit(solution)/shard_map/ppermute | solution.py:73
  339.2 30.5 %collective-permute-start.39 = (bf16[2,9,192,256]{3,2,1,0:T(8,128)(2,1)}, bf16[2,9,192,256]{3,2,1,0:T(8,128)(2,1)}, u32[]{:S(2)}, u32[]{:S(2)}) collective-permute-start(bf16[2,9,192,256]{3,2,1,0:T(8,128)(2,1)} %collective-permute-done.29.refs_0_), channel_id=1, source_target_pairs={{0,2},{2,0},{4,6},{6,4},{8,10},{10,8},{12,14},{14,12},{16,18},{18,... | collective-permute-start | bytes 5308424 | tf_op jit(solution)/shard_map/ppermute | solution.py:73
  341.2 33.9 %collective-permute-start.38 = (bf16[2,9,192,256]{3,2,1,0:T(8,128)(2,1)}, bf16[2,9,192,256]{3,2,1,0:T(8,128)(2,1)S(1)}, u32[]{:S(2)}, u32[]{:S(2)}) collective-permute-start(bf16[2,9,192,256]{3,2,1,0:T(8,128)(2,1)} %collective-permute-done.29.refs_0_), channel_id=1, source_target_pairs={{0,8},{2,6},{8,16},{10,2},{16,24},{18,10},{24,28},{26,18},{28,20},... | collective-permute-start | bytes 5308424 | tf_op jit(solution)/shard_map/ppermute | solution.py:70
  341.3 24.8 %collective-permute-start.41 = (bf16[96,1024]{1,0:T(8,128)(2,1)S(1)}, bf16[96,1024]{1,0:T(8,128)(2,1)S(1)}, u32[]{:S(2)}, u32[]{:S(2)}) collective-permute-start(bf16[96,1024]{1,0:T(8,128)(2,1)S(1)} %add_convert_fusion.16), channel_id=1, source_target_pairs={{0,8},{2,6},{8,16},{10,2},{16,24},{18,10},{24,28},{26,18},{28,20},... | collective-permute-start | bytes 589832 | tf_op jit(solution)/shard_map/ppermute | solution.py:70
  376.5 21.2 %collective-permute-start.46 = (bf16[2,9,192,256]{3,2,1,0:T(8,128)(2,1)S(1)}, bf16[2,9,192,256]{3,2,1,0:T(8,128)(2,1)S(1)}, u32[]{:S(2)}, u32[]{:S(2)}) collective-permute-start(bf16[2,9,192,256]{3,2,1,0:T(8,128)(2,1)S(1)} %collective-permute-done.38.refs_0_), channel_id=1, source_target_pairs={{0,2},{2,0},{4,6},{6,4},{8,10},{10,8},{12,14},{14,12},{16,18},{18,... | collective-permute-start | bytes 5308424 | tf_op jit(solution)/shard_map/ppermute | solution.py:73
  376.5 26.7 %collective-permute-start.52 = (bf16[512,1024]{1,0:T(8,128)(2,1)S(1)}, bf16[512,1024]{1,0:T(8,128)(2,1)S(1)}, u32[]{:S(2)}, u32[]{:S(2)}) collective-permute-start(bf16[512,1024]{1,0:T(8,128)(2,1)S(1)} %copy-done.7), channel_id=1, source_target_pairs={{0,1},{1,0},{2,3},{3,2},{4,5},{5,4},{6,7},{7,6},{8,9},{9,8},{10,11... | collective-permute-start | bytes 3145736 | tf_op jit(solution)/shard_map/ppermute | solution.py:223
  378.3 24.9 %collective-permute-start.45 = (bf16[9,192,256]{2,1,0:T(8,128)(2,1)S(1)}, bf16[9,192,256]{2,1,0:T(8,128)(2,1)S(1)}, u32[]{:S(2)}, u32[]{:S(2)}) collective-permute-start(bf16[9,192,256]{2,1,0:T(8,128)(2,1)S(1)} %slice_bitcast_fusion.1), channel_id=1, source_target_pairs={{0,8},{2,6},{8,16},{10,2},{16,24},{18,10},{24,28},{26,18},{28,20},... | collective-permute-start | bytes 2654216 | tf_op jit(solution)/shard_map/ppermute | solution.py:70
  378.6 17.3 %collective-permute-start.47 = (bf16[2,96,1024]{2,1,0:T(8,128)(2,1)S(1)}, bf16[2,96,1024]{2,1,0:T(8,128)(2,1)S(1)}, u32[]{:S(2)}, u32[]{:S(2)}) collective-permute-start(bf16[2,96,1024]{2,1,0:T(8,128)(2,1)S(1)} %add_convert_fusion.12), channel_id=1, source_target_pairs={{0,8},{2,6},{8,16},{10,2},{16,24},{18,10},{24,28},{26,18},{28,20},... | collective-permute-start | bytes 1179656 | tf_op jit(solution)/shard_map/ppermute | solution.py:70
  380.5 15.3 %collective-permute-start.48 = (f32[2176]{0:T(1024)S(1)}, f32[2176]{0:T(1024)S(1)}, u32[]{:S(2)}, u32[]{:S(2)}) collective-permute-start(f32[2176]{0:T(1024)S(1)} %add.230), channel_id=1, source_target_pairs={{0,4},{2,6},{4,0},{6,2},{8,12},{10,14},{12,8},{14,10},{16,20},{18,... | collective-permute-start | bytes 26120 | tf_op jit(solution)/shard_map/ppermute | solution.py:232
  (102 other events, 838.9 us)
where the time goes:
time: 448 us; the launch traced here: 440 us
  waiting for transfers between devices  174 us (39%)
  Pallas kernels  157 us (35%)
  starting transfers between devices  46.3 us (10%)
  local copies, waits for them, and re-layouts  25.7 us (6%)
  other arithmetic  24.9 us (6%)
  matrix products  10.2 us (2%)
    ppermute x24, waiting for transfers between devices, hop(): return lax.ppermute(x, 'ctx', self.onward)  108 us
    pallas_call x5, Pallas kernels, backward(): pl.pallas_call(functools.partial(backward_kernel, self._make(slots), len(...  57.7 us
    pallas_call x6, Pallas kernels, forward(): pl.pallas_call(functools.partial(forward_kernel, self._make(slots), len(c...  35.2 us
    ppermute x4, waiting for transfers between devices, from_other(): return [lax.ppermute(x, 'tp', [(0, 1), (1, 0)]) for x in xs]  26.5 us
    unnamed x138, local copies, waits for them, and re-layouts  23.5 us
    pallas_call x7, Pallas kernels, whole_call(): pl.pallas_call(kernel, out_shape=list(outs), in_specs=[in_smem()] * scala...  23.3 us
    ppermute x24, starting transfers between devices, hop(): return lax.ppermute(x, 'ctx', self.onward)  23.2 us
    ppermute x5, waiting for transfers between devices, pair_steps(): lax.ppermute(mine, axis, [(i, i ^ step) for i in range(size)])  21 us
  transfers between devices with their start and end apart: 65, of which 31 were waited for; matrix products, arithmetic and copies ran while one was open for 5% of the time, Pallas kernels for 29%

commit v1 on v0

--- a/solution.py
+++ b/solution.py
@@ -14,9 +14,10 @@
 ROPE_BASE = 1000000.0
 LOG2E = 1.4426950408889634
 VMEM_BYTES = 24 * 2**20
-COST_SCALE = 1
+COST_SCALE = 4
 FFN_COLS = 768
 LATE = True
+ALL_VMEM = 56 * 2**20
 f32, bf16 = jnp.float32, jnp.bfloat16
 NT = (((1,), (1,)), ((), ()))
 
@@ -446,21 +447,25 @@
         )(self.order, self.starts, q, do, stats, *chunks, *held)
 
 
-def grads_kernel(ring, two_ref, gate_ref, up_ref, ffn_ref, cot_ref, *refs):
-    outs, (lhs_ref, all_ref) = refs[:-2], refs[-2:]
+def grads_kernel(ring, *refs):
+    two, gate, up, ffn, cot = (refs[2 * i : 2 * i + 2] for i in range(5))
+    outs, (lhs_ref, cot_ref, all_ref) = refs[10:-3], refs[-3:]
 
     @pl.when(pl.program_id(0) == 0)
     def _():
-        lhs_ref[...] = two_ref[...].T
+        lhs_ref[...] = jnp.concatenate([x[...] for x in two], axis=0).T
+        cot_ref[...] = jnp.concatenate([x[...] for x in cot], axis=0)
 
     n = ring.n
     unit = lhs_ref.shape[0] // (2 * n)
-    cols = gate_ref.shape[1]
+    cols = gate[0].shape[2]
     thin = cols // (2 * n)
-    for i, ref in enumerate((gate_ref, up_ref)):
-        grad = jnp.dot(lhs_ref[...], ref[...], preferred_element_type=f32).astype(bf16)
+    for i, half in enumerate((gate, up)):
+        right = jnp.concatenate([x[0] for x in half], axis=0)
+        grad = jnp.dot(lhs_ref[...], right, preferred_element_type=f32).astype(bf16)
         all_ref[:, i * unit : (i + 1) * unit] = grad.reshape(2 * n, unit, cols)
-    down = jnp.dot(ffn_ref[...].T, cot_ref[...], preferred_element_type=f32).astype(bf16)
+    left = jnp.concatenate([x[0] for x in ffn], axis=0).T
+    down = jnp.dot(left, cot_ref[...], preferred_element_type=f32).astype(bf16)
     down = down.reshape(2 * n, thin, down.shape[1])
     for k in range(down.shape[2] // cols):
         at = 2 * unit + k * thin
@@ -510,13 +515,13 @@
 
 
 def ffn_grads(ring, hidden_two, back_gate, back_up, hidden_ffn, cotangent):
-    rows, width = hidden_two.shape
-    units = back_gate.shape[1]
+    rows, width = hidden_two[0].shape
+    blocks, _, cols = back_gate[0].shape
+    units = blocks * cols
     n = ring.n
     wide = width // (2 * n) * 3
-    cols = 256
-    whole = pl.BlockSpec((rows, width), lambda j: (0, 0))
-    block = pl.BlockSpec((rows, cols), lambda j: (0, j))
+    whole = [pl.BlockSpec((rows, width), lambda j: (0, 0))] * 2
+    block = [pl.BlockSpec((1, rows, cols), lambda j: (j, 0, 0))] * 2
     outs = dealt(ring, shape(units // cols, wide, cols, dtype=bf16))
     cuts = [
         pl.BlockSpec(
@@ -528,15 +533,19 @@
         functools.partial(grads_kernel, ring),
         grid=(units // cols,),
         out_shape=outs,
-        in_specs=[whole, block, block, block, whole],
+        in_specs=whole + block * 3 + whole,
         out_specs=cuts,
-        scratch_shapes=[pltpu.VMEM((width, rows), bf16), pltpu.VMEM((2 * n, wide, cols), bf16)],
+        scratch_shapes=[
+            pltpu.VMEM((width, 2 * rows), bf16),
+            pltpu.VMEM((2 * rows, width), bf16),
+            pltpu.VMEM((2 * n, wide, cols), bf16),
+        ],
         compiler_params=pltpu.CompilerParams(vmem_limit_bytes=VMEM_BYTES),
         cost_estimate=pl.CostEstimate(
-            flops=6 * rows * width * units // COST_SCALE, bytes_accessed=2**20, transcendentals=0
+            flops=12 * rows * width * units // COST_SCALE, bytes_accessed=2**20, transcendentals=0
         ),
         name="ffn_grads",
-    )(hidden_two, back_gate, back_up, hidden_ffn, cotangent)
+    )(*hidden_two, *back_gate, *back_up, *hidden_ffn, *cotangent)
 
 
 def place_kernel(ring, slots, count, *refs):
@@ -628,7 +637,7 @@
     )
 
 
-def whole_call(kernel, name, outs, args, flops, scratch=(), scalars=(0, 0)):
+def whole_call(kernel, name, outs, args, flops, scratch=(), scalars=(0, 0), vmem=VMEM_BYTES):
     moved = sum(x.size * x.dtype.itemsize for x in (*outs, *args))
     return pl.pallas_call(
         kernel,
@@ -636,7 +645,7 @@
         in_specs=[in_smem()] * scalars[0] + [in_vmem()] * (len(args) - scalars[0]),
         out_specs=[in_smem()] * scalars[1] + [in_vmem()] * (len(outs) - scalars[1]),
         scratch_shapes=list(scratch),
-        compiler_params=pltpu.CompilerParams(vmem_limit_bytes=VMEM_BYTES),
+        compiler_params=pltpu.CompilerParams(vmem_limit_bytes=vmem),
         cost_estimate=pl.CostEstimate(
             flops=flops // COST_SCALE, bytes_accessed=moved // COST_SCALE, transcendentals=0
         ),
@@ -688,6 +697,14 @@
     return back, jnp.sum(upstream * x * scale, axis=0, keepdims=True)
 
 
+def gain_of(ref):
+    return ref[...].astype(f32)
+
+
+def head_gain(ref):
+    return jnp.concatenate([gain_of(ref)] * 2, axis=1)
+
+
 def lanes(tile):
     return slice(tile * LANES, (tile + 1) * LANES)
 
@@ -697,7 +714,7 @@
 ):
     starts, hidden, kv_raw, kv, w_kv, cosine, sines = refs
     x = tokens[...].astype(f32)
-    hidden[...] = (x * row_scale(x) * gain[...]).astype(bf16)
+    hidden[...] = (x * row_scale(x) * gain_of(gain)).astype(bf16)
     rows = x.shape[0]
     blk = rows // tiles
     mine = order[lax.axis_index("ctx")]
@@ -716,7 +733,7 @@
         w_kv[:, lanes(h)] = jnp.concatenate([w_key[:, cols], w_value[:, cols]], axis=1)
         raw = jnp.dot(hidden[...], w_kv[:, lanes(h)], preferred_element_type=f32)
         kv_raw[:, lanes(h)] = raw
-        normed = raw * lax.rsqrt(head_mean(raw * raw) + EPSILON) * key_gain[...]
+        normed = raw * lax.rsqrt(head_mean(raw * raw) + EPSILON) * head_gain(key_gain)
         kv[:, lanes(h)] = jnp.where(first, turn(normed, cosine[...], sines[...]), raw).astype(bf16)
     for seq in range(segments.shape[0]):
         for d in range(3):
@@ -731,7 +748,7 @@
     for h in range(q_tiles.shape[0]):
         raw = jnp.dot(hidden[...], w_query[:, lanes(h)], preferred_element_type=f32)
         query_raw[:, lanes(h)] = raw
-        normed = raw * lax.rsqrt(head_mean(raw * raw) + EPSILON) * query_gain[...]
+        normed = raw * lax.rsqrt(head_mean(raw * raw) + EPSILON) * head_gain(query_gain)
         turned = turn(normed, cosine[...], sines[...]).astype(bf16).astype(f32) * 0.125
         pair = [
             jnp.where(first, turned, 0.0),
@@ -742,8 +759,12 @@
                 q_tiles[h, t, g * blk : (g + 1) * blk] = one[t * blk : (t + 1) * blk].astype(bf16)
 
 
-def mix_kernel(acc, w_out, *refs):
-    attended, o, lse, halves = refs[0], refs[1], refs[2], refs[3:]
+def half_rows(pair, rows, which):
+    first = (lax.axis_index("tp") + which) % 2 if pair else which
+    return pl.ds(pl.multiple_of(first * (rows // 2), rows // 2), rows // 2)
+
+
+def mix_kernel(pair, acc, w_out, attended, o, lse, *halves):
     heads, tiles, rows, _ = acc.shape
     blk = rows // 2
     first = first_lanes(rows)
@@ -755,35 +776,20 @@
             lse[h, t] = jnp.log2(x.T[:8])
             low = pltpu.roll(value[:blk], HEAD_SIZE, axis=1) + value[blk:]
             attended[t * blk : (t + 1) * blk, lanes(h)] = low.astype(bf16)
-    part = attended.shape[0] // len(halves)
-    for i, half in enumerate(halves):
-        half[...] = jnp.dot(
-            attended[i * part : (i + 1) * part], w_out[...], preferred_element_type=f32
-        ).astype(bf16)
-
-
-def ffn_kernel(
-    terms,
-    tokens,
-    gain,
-    hidden_back,
-    w_gate,
-    w_up,
-    *refs,
-):
-    mine, theirs, refs = refs[:terms], refs[terms : 2 * terms], refs[2 * terms :]
-    mixed, hidden_two, hidden_ffn, back_gate, back_up, gain_grad = refs[:6]
-    halves, sums = refs[6:-1], refs[-1]
+    for which, half in enumerate(halves):
+        rows = half_rows(pair, attended.shape[0], which)
+        half[...] = jnp.dot(attended[rows], w_out[...], preferred_element_type=f32).astype(bf16)
+
+
+def ffn_kernel(tokens, attn, gain, hidden_back, w_gate, w_up, *refs):
+    mixed, hidden_two, hidden_ffn, back_gate, back_up, gain_grad, low, sums = refs
     step, last = pl.program_id(0), pl.num_programs(0) - 1
 
     @pl.when(step == 0)
     def _():
-        part = tokens.shape[0] // terms
-        for i in range(terms):
-            rows = slice(i * part, (i + 1) * part)
-            x = tokens[rows].astype(f32) + (mine[i][...].astype(f32) + theirs[i][...].astype(f32))
-            mixed[rows] = x
-            hidden_two[rows] = (x * row_scale(x) * gain[...]).astype(bf16)
+        x = tokens[...].astype(f32) + attn[...].astype(f32)
+        mixed[...] = x
+        hidden_two[...] = (x * row_scale(x) * gain_of(gain)).astype(bf16)
         sums[...] = jnp.zeros_like(sums)
 
     gating = jnp.dot(hidden_two[...], w_gate[...], preferred_element_type=f32)
@@ -791,64 +797,77 @@
     upstream = hidden_back[...]
     logistic = jax.nn.sigmoid(gating)
     silu = gating * logistic
-    hidden_ffn[...] = (silu * lifted).astype(bf16)
-    back_gate[...] = (
-        upstream * lifted * logistic * (1.0 + gating * (1.0 - logistic))
-    ).astype(bf16)
-    back_up[...] = (upstream * silu).astype(bf16)
-    sums[...] += lax.dot_general(
-        back_gate[...], w_gate[...], NT, preferred_element_type=f32
-    ) + lax.dot_general(back_up[...], w_up[...], NT, preferred_element_type=f32)
+    gate = (upstream * lifted * logistic * (1.0 + gating * (1.0 - logistic))).astype(bf16)
+    up = (upstream * silu).astype(bf16)
+    ffn = (silu * lifted).astype(bf16)
+    for ref, value in ((hidden_ffn, ffn), (back_gate, gate), (back_up, up)):
+        cols = ref.shape[2]
+        for k in range(ref.shape[0]):
+            ref[k] = value[:, k * cols : (k + 1) * cols]
+    sums[...] += lax.dot_general(gate, w_gate[...], NT, preferred_element_type=f32)
+    sums[...] += lax.dot_general(up, w_up[...], NT, preferred_element_type=f32)
 
     @pl.when(step == last)
     def _():
         x = mixed[...]
         gain_grad[...] = jnp.sum(sums[...] * x * row_scale(x), axis=0, keepdims=True)
-        part = sums.shape[0] // len(halves)
-        for i, half in enumerate(halves):
-            half[...] = sums[i * part : (i + 1) * part].astype(bf16)
-
-
-def feed_forward(tokens, gain, hidden_back, w_gate, w_up, mine, theirs):
+        low[...] = sums[...].astype(bf16)
+
+
+def block_cols(units):
+    return 256 if units % 256 == 0 else units
+
+
+def feed_forward(tokens, attn, gain, hidden_back, w_gate, w_up):
     rows, width = tokens.shape
     units = w_gate.shape[1]
     cols = FFN_COLS if units % FFN_COLS == 0 else units
+    thin = block_cols(units)
     whole = pl.BlockSpec((rows, width), lambda j: (0, 0))
     line = pl.BlockSpec((1, width), lambda j: (0, 0))
-    block = pl.BlockSpec((rows, cols), lambda j: (0, j))
     weight = pl.BlockSpec((width, cols), lambda j: (0, j))
-    part = pl.BlockSpec((rows // len(mine), width), lambda j: (0, 0))
-    half = pl.BlockSpec((rows // 2, width), lambda j: (0, 0))
-    low = shape(rows, units, dtype=bf16)
+    block = pl.BlockSpec((cols // thin, rows, thin), lambda j: (j, 0, 0))
+    low = shape(units // thin, rows, thin, dtype=bf16)
     return pl.pallas_call(
-        functools.partial(ffn_kernel, len(mine)),
+        ffn_kernel,
         grid=(units // cols,),
         out_shape=[shape(rows, width), shape(rows, width, dtype=bf16), low, low, low]
-        + [shape(1, width)]
-        + [shape(rows // 2, width, dtype=bf16)] * 2,
-        in_specs=[whole, line, block, weight, weight] + [part] * (2 * len(mine)),
-        out_specs=[whole, whole, block, block, block, line, half, half],
+        + [shape(1, width), shape(rows, width, dtype=bf16)],
+        in_specs=[whole, whole, line, pl.BlockSpec((rows, cols), lambda j: (0, j)), weight, weight],
+        out_specs=[whole, whole, block, block, block, line, whole],
         scratch_shapes=[pltpu.VMEM((rows, width), f32)],
         compiler_params=pltpu.CompilerParams(vmem_limit_bytes=VMEM_BYTES),
         cost_estimate=pl.CostEstimate(
             flops=8 * rows * width * units // COST_SCALE, bytes_accessed=2**20, transcendentals=0
         ),
         name="feed_forward",
-    )(tokens, gain, hidden_back, w_gate, w_up, *mine, *theirs)
-
-
-def back_kernel(terms, cotangent, mixed, gain, w_out, o, lse, *refs):
-    mine, theirs, (back_mixed, back_proj, do_tiles, stats) = (
-        refs[:terms],
-        refs[terms : 2 * terms],
-        refs[2 * terms :],
+    )(tokens, attn, gain, hidden_back, w_gate, w_up)
+
+
+def down_kernel(pair, *refs):
+    ffn, w_down, out = refs[:2], refs[2], refs[3]
+    cols = ffn[0].shape[2]
+    for which, x in enumerate(ffn):
+        part = jnp.zeros((x.shape[1], out.shape[1]), f32)
+        for k in range(x.shape[0]):
+            part += jnp.dot(
+                x[k], w_down[k * cols : (k + 1) * cols], preferred_element_type=f32
+            )
+        out[half_rows(pair, out.shape[0], which)] = part.astype(bf16)
+
+
+def back_kernel(pair, cotangent, gain, w_out, o, lse, *refs):
+    mixed, mine, theirs, (back_mixed, back_proj, do_tiles, stats) = (
+        refs[:2],
+        refs[2:4],
+        refs[4:6],
+        refs[6:],
     )
-    part = cotangent.shape[0] // terms
-    for i in range(terms):
-        rows = slice(i * part, (i + 1) * part)
-        x = mixed[rows]
-        upstream = mine[i][...].astype(f32) + theirs[i][...].astype(f32)
-        back = cotangent[rows].astype(f32) + norm_back(upstream, x, row_scale(x), gain[...])
+    for which in (0, 1):
+        rows = half_rows(pair, cotangent.shape[0], which)
+        x = mixed[which][...]
+        upstream = mine[which][...].astype(f32) + theirs[which][...].astype(f32)
+        back = cotangent[rows].astype(f32) + norm_back(upstream, x, row_scale(x), gain_of(gain))
         back_mixed[rows] = back
         back_proj[rows] = back.astype(bf16)
     heads, tiles, rows, _ = o.shape
@@ -880,7 +899,7 @@
         for h in range(heads):
             both = jnp.concatenate([dq[h, t, :, :blk], dq[h, t, :, blk:]], axis=0) * 0.125
             turned = turn(both.T, cosine[at], -sines[at])
-            back, gain_terms = head_norm_back(turned, query_raw[at, lanes(h)], query_gain[...])
+            back, gain_terms = head_norm_back(turned, query_raw[at, lanes(h)], head_gain(query_gain))
             query_delta[at, lanes(h)] = back.astype(bf16)
             gain_grad[...] += gain_terms
 
@@ -909,7 +928,7 @@
     for h in range(own_dkv.shape[1] // LANES):
         dkv = own_dkv[:, lanes(h)].astype(f32)
         turned = turn(dkv, cosine[...], -sines[...])
-        back, gain_terms = head_norm_back(turned, kv_raw[:, lanes(h)], key_gain[...])
+        back, gain_terms = head_norm_back(turned, kv_raw[:, lanes(h)], head_gain(key_gain))
         kv_delta[:, lanes(h)] = jnp.where(first, back, dkv).astype(bf16)
         gain_grad[...] += gain_terms
     part = lax.dot_general(
@@ -969,16 +988,8 @@
     packed = units % 256 == 0 and width % (32 * ring.n) == 0 and w_out.shape[0] % (32 * ring.n) == 0
     pair = lax.axis_size("tp") == 2
 
-    def shared(halves):
-        if pair:
-            return from_other(halves), list(halves)
-        return [lax.psum(x, "tp") for x in halves], [jnp.zeros_like(x) for x in halves]
-
     def line(x):
-        return x.astype(f32).reshape(1, -1)
-
-    def head_line(x):
-        return jnp.tile(line(x), (1, 2))
+        return x.reshape(1, -1)
 
     inverse = ROPE_BASE ** (-np.arange(0, HEAD_SIZE, 2) / HEAD_SIZE)
     inverse = np.tile(inverse, 4)[None, :].astype(np.float32)
@@ -1001,11 +1012,12 @@
             line(norm_gain),
             key_weight,
             value_weight,
-            head_line(key_gain),
+            line(key_gain),
             jnp.asarray(inverse),
         ],
         4 * rows * width * k_cols,
         scalars=(1, 1),
+        vmem=ALL_VMEM,
     )
     gather = RingGather(ring, own_kv)
     flying = gather.send(gather.sends())
@@ -1013,7 +1025,7 @@
         functools.partial(project_q_kernel, tiles),
         "project_q",
         [shape(rows, q_cols), shape(kv_heads, tiles, 2 * blk, LANES, dtype=bf16)],
-        [hidden_input, w_query, head_line(query_gain), cosine, sines],
+        [hidden_input, w_query, line(query_gain), cosine, sines],
         2 * rows * width * q_cols,
     )
 
@@ -1028,16 +1040,15 @@
         flying = gather.send(gather.sends())
         acc = attention.forward([late, *now], q_tiles, acc)
         late = gather.pieces[-1]
-        if gather.step == far:
-            acc = attention.forward([late], q_tiles, acc)
+    acc = attention.forward([late], q_tiles, acc)
     acc = attention.forward(gather.pieces[-2:], q_tiles, acc)
     kv_pieces = {
         max(abs(d) for d, _ in slots): gather.pieces[i - 1 : i + 1]
         for i, (slots, _) in enumerate(gather.pieces)
         if i % 2
     }
-    attended, o, lse, *mix_halves = whole_call(
-        mix_kernel,
+    attended, o, lse, attn_mine, attn_send = whole_call(
+        functools.partial(mix_kernel, pair),
         "mix",
         [
             shape(rows, q_cols, dtype=bf16),
@@ -1049,37 +1060,69 @@
         [acc, w_out],
         2 * rows * width * q_cols,
     )
-    theirs, mine = shared(mix_halves)
-    back_hidden = dot(cotangent, w_down, (1, 1))
-    back_hidden, *theirs = lax.optimization_barrier((back_hidden, *theirs))
-
-    mixed, hidden_two, hidden_ffn, back_gate, back_up, grad_ffn_gain, *halves = feed_forward(
-        tokens, line(ffn_gain), back_hidden, w_gate, w_up, mine, theirs
-    )
+
+    def halves_of(x):
+        at = lax.axis_index("tp") if pair else 0
+        return [
+            lax.dynamic_slice_in_dim(x, (at + k) % 2 * (rows // 2), rows // 2, 0) for k in (0, 1)
+        ]
+
+    def from_first(xs):
+        at = lax.axis_index("tp") if pair else 0
+        return jnp.concatenate([jnp.where(at == k, xs[0], xs[1]) for k in (0, 1)])
+
+    cots, toks = halves_of(cotangent), halves_of(tokens)
+    if pair:
+        (attn_theirs,) = from_other([attn_send])
+        upstream = [dot(x, w_down, (1, 1)) for x in cots]
+        attn_theirs, *upstream = lax.optimization_barrier((attn_theirs, *upstream))
+        attn = total(attn_mine, attn_theirs)
+    else:
+        attn, attn_next = lax.psum((attn_mine, attn_send), "tp")
+        upstream = [dot(x, w_down, (1, 1)) for x in cots]
+
+    def feed(k, attn):
+        return feed_forward(toks[k], attn, line(ffn_gain), upstream[k], w_gate, w_up)
+
+    if pair:
+        (attn_next,) = from_other([attn])
+        fed = [feed(0, attn)]
+        attn_next, *fed[0] = lax.optimization_barrier((attn_next, *fed[0]))
+        (last,) = from_other([fed[0][-1]])
+        fed.append(feed(1, attn_next))
+        last, *fed[1] = lax.optimization_barrier((last, *fed[1]))
+        (first,) = from_other([fed[1][-1]])
+    else:
+        fed = [feed(0, attn), feed(1, attn_next)]
+        first, last = lax.psum((fed[0][-1], fed[1][-1]), "tp")
+    mixed, hidden_two, hidden_ffn, back_gate, back_up, ffn_gain_grads, mine = zip(*fed)
+    if not pair:
+        mine = [jnp.zeros_like(x) for x in mine]
+    grad_ffn_gain = ffn_gain_grads[0] + ffn_gain_grads[1]
     if packed:
-        first, mine_first = shared(halves[:1])
-        dealt_out = ffn_grads(ring, hidden_two, back_gate, back_up, hidden_ffn, cotangent)
-        second, first[0], *dealt_out = lax.optimization_barrier((halves[1], first[0], *dealt_out))
-        second, mine_second = shared([second])
-        hidden_ffn, dealt_out[0] = lax.optimization_barrier((hidden_ffn, dealt_out[0]))
-        output_part = dot(hidden_ffn, w_down, (1, 0)).astype(bf16)
+        dealt_out = ffn_grads(ring, hidden_two, back_gate, back_up, hidden_ffn, cots)
+        first, *dealt_out = lax.optimization_barrier((first, *dealt_out))
         ffn_box = []
         ffn_sum = Steps(sum_steps(ring, dealt_terms(ring, dealt_out), ffn_box))
-        advance([ffn_sum])
-        *theirs, output_part = advance([ffn_sum], first[0], second[0], output_part)
-        mine = mine_first + mine_second
+        first, last = advance([ffn_sum], first, last)
     else:
-        theirs, mine = shared(halves)
-        grad_w_down = dot(hidden_ffn, cotangent, (0, 0)).astype(bf16)
-        grad_w_gate = dot(hidden_two, back_gate, (0, 0)).astype(bf16)
-        grad_w_up = dot(hidden_two, back_up, (0, 0)).astype(bf16)
+
+        def by_units(xs):
+            return jnp.concatenate(xs, axis=1).transpose(1, 0, 2).reshape(rows, units)
+
+        two, cot = jnp.concatenate(hidden_two), jnp.concatenate(cots)
         grad_w_gate, grad_w_up, grad_w_down = sum_over_ctx(
-            ring, [grad_w_gate, grad_w_up, grad_w_down]
+            ring,
+            [
+                dot(two, by_units(back_gate), (0, 0)).astype(bf16),
+                dot(two, by_units(back_up), (0, 0)).astype(bf16),
+                dot(by_units(hidden_ffn), cot, (0, 0)).astype(bf16),
+            ],
         )
         ffn_sum = None
-        output_part = dot(hidden_ffn, w_down, (1, 0)).astype(bf16)
+
     back_mixed, back_proj, do_tiles, stats = whole_call(
-        functools.partial(back_kernel, 2),
+        functools.partial(back_kernel, pair),
         "back",
         [
             shape(rows, width),
@@ -1087,10 +1130,10 @@
             shape(*q_tiles.shape, dtype=bf16),
             shape(*lse.shape),
         ],
-        [cotangent, mixed, line(ffn_gain), w_out, o, lse, *mine, *theirs],
+        [cotangent, line(ffn_gain), w_out, o, lse, *mixed, *mine, first, last],
         2 * rows * width * q_cols,
     )
-    output_swap = Steps(exchange_steps(output_part)) if pair else None
+    output_swap, more = None, hidden_ffn
     dq = None
     terms = {}
 
@@ -1098,9 +1141,19 @@
     for d in range(far, -1, -1):
         if d < far:
             chains = [ffn_sum, dkv_sum if d < far - 1 else None]
-            if d == 0:
+            if d == 0 and pair:
+                output_swap = Steps(exchange_steps(output_part))
                 chains.append(output_swap)
-            do_tiles, dq = advance(chains, do_tiles, dq)
+            do_tiles, dq, *more = advance(chains, do_tiles, dq, *more)
+            if d == far - 1:
+                (output_part,) = whole_call(
+                    functools.partial(down_kernel, pair),
+                    "down",
+                    [shape(rows, width, dtype=bf16)],
+                    [*more, w_down],
+                    2 * rows * width * units,
+                )
+                more = [output_part]
         dq, keep, give = attention.backward(kv_pieces[d], q_tiles, do_tiles, stats, dq)
         terms[d] = [keep, ring.sibling(give)]
     placed, done = [], 0
@@ -1109,11 +1162,12 @@
         back_query_kernel,
         "back_query",
         [shape(rows, q_cols, dtype=bf16), shape(1, LANES)],
-        [dq, query_raw, head_line(query_gain), cosine, sines],
+        [dq, query_raw, line(query_gain), cosine, sines],
         2 * rows * width,
     )
     if packed:
-        placed, done = place_ffn(ring, ffn_box[0].pieces[:4], width, []), 4
+        done = len(ffn_box[0].pieces)
+        placed = place_ffn(ring, ffn_box[0].pieces, width, [])
     query_delta, *placed = advance([dkv_sum], query_delta, *placed)
     own_dkv = dkv_sum.result
     wide = width // (2 * ring.n) + w_out.shape[0] // (2 * ring.n)
@@ -1133,7 +1187,7 @@
             query_delta,
             own_dkv,
             kv_raw,
-            head_line(key_gain),
+            line(key_gain),
             cosine,
             sines,
             w_query,
@@ -1162,12 +1216,14 @@
         round_at = 0
         while qkv_sum.generator is not None:
             came = len(gather.pieces)
-            chains = [ffn_sum if round_at % 2 == 0 else None, qkv_sum, gain_sum]
+            chains = [qkv_sum, gain_sum]
             if round_at == 0:
                 chains.append(output_swap)
             elif round_at in (1, 4):
                 chains.append(one_swap)
             placed = advance(chains, *placed)
+            if round_at % 2 == 0:
+                placed = advance([ffn_sum, gain_sum], *placed)
             if came > done:
                 placed = place_ffn(ring, gather.pieces[done:came], width, placed)
                 done = came
@@ -1202,7 +1258,7 @@
     else:
         output = lax.psum(output_part, "tp").astype(f32)
         back_one = lax.psum(one_low, "tp").astype(f32)
-    output = (mixed + output).astype(bf16)
+    output = (from_first(mixed) + output).astype(bf16)
     inputs = tokens.astype(f32)
     input_grad = back_mixed + norm_back(back_one, inputs, row_scale(inputs), norm_gain)
 

time: 448 us -> 425 us (0.949)
  Pallas kernels: 157 us -> 108 us
  starting transfers between devices: 46.3 us -> 74.6 us
  waiting for transfers between devices: 174 us -> 184 us
  matrix products: 10.2 us -> 2.85 us
  local copies, waits for them, and re-layouts: 25.7 us -> 19.1 us
    pallas_call x5, Pallas kernels: 57.7 us -> 22.1 us  [backward(): pl.pallas_call(functools.partial(backward_kernel, self._make(slots), len(...]
    ppermute x24, starting transfers between devices: 23.2 us -> 52.3 us  [hop(): return lax.ppermute(x, 'ctx', self.onward)]
    pallas_call x6, Pallas kernels: 35.2 us -> 15.4 us  [forward(): pl.pallas_call(functools.partial(forward_kernel, self._make(slots), len(c...]
    ppermute x4, waiting for transfers between devices: 26.5 us -> 10.4 us  [from_other(): return [lax.ppermute(x, 'tp', [(0, 1), (1, 0)]) for x in xs]]
    ppermute x3, waiting for transfers between devices: 5.5 us -> 17.5 us  [sum_steps(): got = (yield [ring.hop(x[0]), lax.ppermute(x[1], 'ctx', ring.across)])]
    unnamed x138 -> x134, local copies, waits for them, and re-layouts: 23.5 us -> 11.5 us
    ppermute x24, waiting for transfers between devices: 108 us -> 118 us  [hop(): return lax.ppermute(x, 'ctx', self.onward)]
    dot_general x2, matrix products: 10.2 us -> 2.85 us  [dot(): lax.dot_general(a, b, ((dims[:1], dims[1:]), ((), ())), preferred_element...]
  transfers between devices with their start and end apart: 65 -> 65, of which waited for: 31 -> 35; matrix products, arithmetic and copies ran while one was open for 5% -> 6% of each run, Pallas kernels for 29% -> 22%
where the time goes in v1:
time: 425 us; the launch traced here: 417 us
  waiting for transfers between devices  184 us (43%)
  Pallas kernels  108 us (25%)
  starting transfers between devices  74.6 us (18%)
  other arithmetic  26.8 us (6%)
  local copies, waits for them, and re-layouts  19.1 us (4%)
    ppermute x24, waiting for transfers between devices, hop(): return lax.ppermute(x, 'ctx', self.onward)  118 us
    ppermute x24, starting transfers between devices, hop(): return lax.ppermute(x, 'ctx', self.onward)  52.3 us
    pallas_call x8, Pallas kernels, whole_call(): pl.pallas_call(kernel, out_shape=list(outs), in_specs=[in_smem()] * scala...  27.3 us
    ppermute x5, waiting for transfers between devices, pair_steps(): lax.ppermute(mine, axis, [(i, i ^ step) for i in range(size)])  26.8 us
    pallas_call x5, Pallas kernels, backward(): pl.pallas_call(functools.partial(backward_kernel, self._make(slots), len(...  22.1 us
    ppermute x3, waiting for transfers between devices, sum_steps(): got = (yield [ring.hop(x[0]), lax.ppermute(x[1], 'ctx', ring.across)])  17.5 us
    pallas_call x5, Pallas kernels, place_ffn(): pl.pallas_call(functools.partial(place_kernel, ring, slots, len(parts)),...  17.4 us
    convert_element_type x16, other arithmetic, total(): return out.astype(bf16)  16.5 us
  transfers between devices with their start and end apart: 65, of which 35 were waited for; matrix products, arithmetic and copies ran while one was open for 6% of the time, Pallas kernels for 22%

profile of v1, /device:TPU:0, one launch (start us, length us, event | category | flops | bytes accessed | tf_op | source)
XLA Modules:
  0.0 417.3 jit_solution(16924959427020516203)
XLA Ops:
  2.0 7.4 %project_kv.1 = (s32[1,3]{1,0:T(1,128)}, bf16[512,1024]{1,0:T(8,128)(2,1)}, f32[512,512]{1,0:T(8,128)}, bf16[512,512]{1,0:T(8,128)(2,1)}, bf16[1024,512]{1,0:T(8...) custom-call(s32[16]{0:T(128)} %order_ref.21, s32[1,8192]{1,0:T(1,128)} %segments.1, bf16[512,1024]{1,0:T(8,128)(2,1)} %tokens.3, ...), custom_call_target="tpu_custom_call" | custom-call | flops 134217728 | bytes 1581747 | tf_op jit(solution)/shard_map/project_kv/pallas_call | solution.py:642
  30.9 9.6 %collective-permute-done.2.refs_1_.refs_0_ = bf16[2,512,512]{2,1,0:T(8,128)(2,1)S(1)} collective-permute-done((bf16[2,512,512]{2,1,0:T(8,128)(2,1)S(1)}, bf16[2,512,512]{2,1,0:T(8,128)(2,1)S(1)}, u32[]{:S(2)}, u32[]{:S(2)}) %collective-permute-start.2) | collective-permute-done | bytes 1048608 | tf_op jit(solution)/shard_map/ppermute | solution.py:71
  45.8 9.8 %collective-permute-done.4.refs_1_.refs_0_ = bf16[2,512,512]{2,1,0:T(8,128)(2,1)} collective-permute-done((bf16[2,512,512]{2,1,0:T(8,128)(2,1)S(1)}, bf16[2,512,512]{2,1,0:T(8,128)(2,1)}, u32[]{:S(2)}, u32[]{:S(2)}) %collective-permute-start.4) | collective-permute-done | bytes 1048608 | tf_op jit(solution)/shard_map/ppermute | solution.py:71
  58.7 3.3 attend_forward.9.refs_1_
  62.0 3.9 collective-permute-done.6.refs_0_
  71.1 3.4 attend_forward.11.acc
  80.6 6.4 %collective-permute-done.10 = bf16[256,1024]{1,0:T(8,128)(2,1)S(1)} collective-permute-done((bf16[256,1024]{1,0:T(8,128)(2,1)S(1)}, bf16[256,1024]{1,0:T(8,128)(2,1)S(1)}, u32[]{:S(2)}, u32[]{:S(2)}) %collective-permute-start.10) | collective-permute-done | bytes 524320 | tf_op jit(solution)/shard_map/ppermute | solution.py:240
  88.9 7.6 %feed_forward.2 = (f32[256,1024]{1,0:T(8,128)S(1)}, bf16[256,1024]{1,0:T(8,128)(2,1)S(1)}, bf16[9,256,256]{2,1,0:T(8,128)(2,1)S(1)}, bf16[9,256,256]{2,1,0:T(8,1...) custom-call(bf16[256,1024]{1,0:T(8,128)(2,1)S(1)} %get-tuple-element.622.tokens, ...), custom_call_target="tpu_custom_call" | custom-call | flops 1207959552 | bytes 1048576 | tf_op jit(solution)/shard_map/feed_forward/pallas_call | solution.py:831
  100.5 7.3 %feed_forward.3 = (f32[256,1024]{1,0:T(8,128)S(1)}, bf16[256,1024]{1,0:T(8,128)(2,1)S(1)}, bf16[9,256,256]{2,1,0:T(8,128)(2,1)S(1)}, bf16[9,256,256]{2,1,0:T(8,1...) custom-call(bf16[256,1024]{1,0:T(8,128)(2,1)S(1)} %get-tuple-element.621.tokens, ...), custom_call_target="tpu_custom_call" | custom-call | flops 1207959552 | bytes 1048576 | tf_op jit(solution)/shard_map/feed_forward/pallas_call | solution.py:831
  107.9 3.4 collective-permute-done.12.refs_5_
  113.3 11.1 %ffn_grads.1 = (bf16[9,192,256]{2,1,0:T(8,128)(2,1)S(1)}, bf16[9,192,256]{2,1,0:T(8,128)(2,1)S(1)}, bf16[9,192,256]{2,1,0:T(8,128)(2,1)S(1)}, bf16[2,9,192,256]{...) custom-call(bf16[256,1024]{1,0:T(8,128)(2,1)S(1)} %get-tuple-element, ...), custom_call_target="tpu_custom_call" | custom-call | flops 1811939328 | bytes 1048576 | tf_op jit(solution)/shard_map/ffn_grads/pallas_call | solution.py:532
  131.5 9.9 %collective-permute-start.16 = (bf16[9,192,256]{2,1,0:T(8,128)(2,1)S(1)}, bf16[9,192,256]{2,1,0:T(8,128)(2,1)S(1)}, u32[]{:S(2)}, u32[]{:S(2)}) collective-permute-start(bf16[9,192,256]{2,1,0:T(8,128)(2,1)S(1)} %add_convert_fusion.5), channel_id=1, source_target_pairs={{0,8},{2,6},{8,16},{10,2},{16,24},{18,10},{24,28},{26,18},{28,20},... | collective-permute-start | bytes 2654216 | tf_op jit(solution)/shard_map/ppermute | solution.py:71
  144.1 6.0 %attend_backward.5 = (f32[4,2,64,512]{3,2,1,0:T(8,128)S(1)}, f32[512,512]{1,0:T(8,128)S(1)}, bf16[512,512]{1,0:T(8,128)(2,1)S(1)}) custom-call(s32[16]{0:T(128)S(1)} %copy-done.48, s32[1,3]{1,0:T(1,128)S(1)} %copy-done.49, bf16[4,2,512,128]{3,2,1,0:T(8,128)(2,1)S(1)} %get-tuple-element.316.q_ref, bf16[4,2,512,128]{3,2,1,0:T(8,128)(2,1)S(1)} %get-tuple-element.431.do_ref, ...), custom_call_target="tpu_custom_call" | custom-call | flops 1342177280 | bytes 1703936 | tf_op jit(solution)/shard_map/attend_backward/pallas_call | solution.py:436
  162.4 4.7 %attend_backward.6 = (f32[4,2,64,512]{3,2,1,0:T(8,128)S(1)}, f32[2,512,512]{2,1,0:T(8,128)S(1)}, bf16[2,512,512]{2,1,0:T(8,128)(2,1)S(1)}) custom-call(s32[16]{0:T(128)S(1)} %copy-done.48, s32[1,3]{1,0:T(1,128)S(1)} %copy-done.49, bf16[4,2,512,128]{3,2,1,0:T(8,128)(2,1)S(1)} %get-tuple-element.316.q_ref, ...), custom_call_target="tpu_custom_call" | custom-call | flops 2684354560 | bytes 2359296 | tf_op jit(solution)/shard_map/attend_backward/pallas_call | solution.py:436
  167.1 10.7 %collective-permute-done.17 = bf16[2,9,192,256]{3,2,1,0:T(8,128)(2,1)S(1)} collective-permute-done((bf16[2,9,192,256]{3,2,1,0:T(8,128)(2,1)S(1)}, bf16[2,9,192,256]{3,2,1,0:T(8,128)(2,1)S(1)}, u32[]{:S(2)}, u32[]{:S(2)}) %collective-permute-start.17) | collective-permute-done | bytes 1769504 | tf_op jit(solution)/shard_map/ppermute | solution.py:71
  185.5 5.0 %attend_backward.7 = (f32[4,2,64,512]{3,2,1,0:T(8,128)S(1)}, f32[2,512,512]{2,1,0:T(8,128)S(1)}, bf16[2,512,512]{2,1,0:T(8,128)(2,1)S(1)}) custom-call(s32[16]{0:T(128)S(1)} %copy-done.48, s32[1,3]{1,0:T(1,128)S(1)} %copy-done.49, bf16[4,2,512,128]{3,2,1,0:T(8,128)(2,1)S(1)} %get-tuple-element.316.q_ref, ...), custom_call_target="tpu_custom_call" | custom-call | flops 2684354560 | bytes 2359296 | tf_op jit(solution)/shard_map/attend_backward/pallas_call | solution.py:436
  190.5 17.8 %collective-permute-done.20 = bf16[512,512]{1,0:T(8,128)(2,1)S(1)} collective-permute-done((bf16[512,512]{1,0:T(8,128)(2,1)S(1)}, bf16[512,512]{1,0:T(8,128)(2,1)S(1)}, u32[]{:S(2)}, u32[]{:S(2)}) %collective-permute-start.20) | collective-permute-done | bytes 524320 | tf_op jit(solution)/shard_map/ppermute | solution.py:71
  217.5 17.8 %collective-permute-done.22 = bf16[9,192,256]{2,1,0:T(8,128)(2,1)S(1)} collective-permute-done((bf16[9,192,256]{2,1,0:T(8,128)(2,1)S(1)}, bf16[9,192,256]{2,1,0:T(8,128)(2,1)S(1)}, u32[]{:S(2)}, u32[]{:S(2)}) %collective-permute-start.22) | collective-permute-done | bytes 884768 | tf_op jit(solution)/shard_map/ppermute | solution.py:71
  235.4 9.5 %collective-permute-done.23 = bf16[9,192,256]{2,1,0:T(8,128)(2,1)S(1)} collective-permute-done((bf16[9,192,256]{2,1,0:T(8,128)(2,1)S(1)}, bf16[9,192,256]{2,1,0:T(8,128)(2,1)S(1)}, u32[]{:S(2)}, u32[]{:S(2)}) %collective-permute-start.23) | collective-permute-done | bytes 884768 | tf_op jit(solution)/shard_map/ppermute | solution.py:138
  250.3 4.7 %attend_backward.9 = (f32[4,2,64,512]{3,2,1,0:T(8,128)S(1)}, f32[512,512]{1,0:T(8,128)S(1)}, bf16[512,512]{1,0:T(8,128)(2,1)S(1)}) custom-call(s32[16]{0:T(128)S(1)} %copy-done.48, s32[1,3]{1,0:T(1,128)S(1)} %copy-done.49, bf16[4,2,512,128]{3,2,1,0:T(8,128)(2,1)S(1)} %get-tuple-element.316.q_ref, bf16[4,2,512,128]{3,2,1,0:T(8,128)(2,1)S(1)} %get-tuple-element.431.do_ref, ...), custom_call_target="tpu_custom_call" | custom-call | flops 1677721600 | bytes 1703936 | tf_op jit(solution)/shard_map/attend_backward/pallas_call | solution.py:436
  254.9 7.8 %collective-permute-done.28 = bf16[2,512,512]{2,1,0:T(8,128)(2,1)S(1)} collective-permute-done((bf16[2,512,512]{2,1,0:T(8,128)(2,1)S(1)}, bf16[2,512,512]{2,1,0:T(8,128)(2,1)S(1)}, u32[]{:S(2)}, u32[]{:S(2)}) %collective-permute-start.28) | collective-permute-done | bytes 1048608 | tf_op jit(solution)/shard_map/ppermute | solution.py:71
  268.5 3.2 place_ffn.5
  273.3 6.2 %collective-permute-done.30 = bf16[512,512]{1,0:T(8,128)(2,1)S(1)} collective-permute-done((bf16[512,512]{1,0:T(8,128)(2,1)S(1)}, bf16[512,512]{1,0:T(8,128)(2,1)S(1)}, u32[]{:S(2)}, u32[]{:S(2)}) %collective-permute-start.30) | collective-permute-done | bytes 524320 | tf_op jit(solution)/shard_map/ppermute | solution.py:138
  279.9 5.3 %back_project.1 = (bf16[512,1024]{1,0:T(8,128)(2,1)S(1)}, f32[1,1024]{1,0:T(1,128)S(1)}, f32[1,128]{1,0:T(1,128)S(1)}, bf16[512,512]{1,0:T(8,128)(2,1)}, bf16[96...) custom-call(bf16[512,1024]{1,0:T(8,128)(2,1)S(1)} %copy-done, ...), custom_call_target="tpu_custom_call" | custom-call | flops 536870912 | bytes 3277984 | tf_op jit(solution)/shard_map/back_project/pallas_call | solution.py:642
  303.4 20.4 %collective-permute-done.35 = bf16[96,1024]{1,0:T(8,128)(2,1)S(1)} collective-permute-done((bf16[96,1024]{1,0:T(8,128)(2,1)S(1)}, bf16[96,1024]{1,0:T(8,128)(2,1)S(1)}, u32[]{:S(2)}, u32[]{:S(2)}) %collective-permute-start.35) | collective-permute-done | bytes 196640 | tf_op jit(solution)/shard_map/ppermute | solution.py:71
  328.2 3.3 place_ffn.6
  344.4 20.7 %collective-permute-done.46 = f32[2176]{0:T(1024)S(1)} collective-permute-done((f32[2176]{0:T(1024)S(1)}, f32[2176]{0:T(1024)S(1)}, u32[]{:S(2)}, u32[]{:S(2)}) %collective-permute-start.46) | collective-permute-done | bytes 8736 | tf_op jit(solution)/shard_map/ppermute | solution.py:233
  369.1 3.3 place_ffn.7
  388.8 5.4 %place_ffn.8 = (f32[1024,2304]{1,0:T(8,128)}, f32[1024,2304]{1,0:T(8,128)}, f32[2304,1024]{1,0:T(8,128)}) custom-call(bf16[2,9,192,256]{3,2,1,0:T(8,128)(2,1)} %collective-permute-done.54.refs_0_, bf16[2,9,192,256]{3,2,1,0:T(8,128)(2,1)} %collective-permute-done.57.refs_1_, ...), custom_call_target="tpu_custom_call", output_to_operand_aliasing={{0}: (2, {}), {1}: (3, {}), {2}: (4, {})} | custom-call | bytes 14155776 | tf_op jit(solution)/shard_map/place_ffn/pallas_call | solution.py:589
  394.2 3.9 collective-permute-done.56.refs_4_
  400.9 5.1 %collective-permute-done.59.refs_6_ = bf16[2,96,1024]{2,1,0:T(8,128)(2,1)S(1)} collective-permute-done((bf16[2,96,1024]{2,1,0:T(8,128)(2,1)S(1)}, bf16[2,96,1024]{2,1,0:T(8,128)(2,1)S(1)}, u32[]{:S(2)}, u32[]{:S(2)}) %collective-permute-start.59) | collective-permute-done | bytes 393248 | tf_op jit(solution)/shard_map/ppermute | solution.py:71
  413.7 3.2 place_qkv.1
  (313 shorter events, 168.0 us)
Async XLA Ops:
  9.5 14.7 %collective-permute-start = (bf16[512,512]{1,0:T(8,128)(2,1)}, bf16[512,512]{1,0:T(8,128)(2,1)S(1)}, u32[]{:S(2)}, u32[]{:S(2)}) collective-permute-start(bf16[512,512]{1,0:T(8,128)(2,1)} %get-tuple-element.317.refs_0_), channel_id=1, source_target_pairs={{0,8},{2,6},{8,16},{10,2},{16,24},{18,10},{24,28},{26,18},{28,20},... | collective-permute-start | bytes 1572872 | tf_op jit(solution)/shard_map/ppermute | solution.py:71
  25.6 14.9 %collective-permute-start.2 = (bf16[2,512,512]{2,1,0:T(8,128)(2,1)S(1)}, bf16[2,512,512]{2,1,0:T(8,128)(2,1)S(1)}, u32[]{:S(2)}, u32[]{:S(2)}) collective-permute-start(bf16[2,512,512]{2,1,0:T(8,128)(2,1)S(1)} %pad_maximum_fusion.2.refs_0_), channel_id=1, source_target_pairs={{0,8},{2,6},{8,16},{10,2},{16,24},{18,10},{24,28},{26,18},{28,20},... | collective-permute-start | bytes 3145736 | tf_op jit(solution)/shard_map/ppermute | solution.py:71
  27.7 15.0 %collective-permute-start.5 = (bf16[2,512,512]{2,1,0:T(8,128)(2,1)S(1)}, bf16[2,512,512]{2,1,0:T(8,128)(2,1)S(1)}, u32[]{:S(2)}, u32[]{:S(2)}) collective-permute-start(bf16[2,512,512]{2,1,0:T(8,128)(2,1)S(1)} %pad_maximum_fusion.2.refs_0_), channel_id=1, source_target_pairs={{0,2},{2,0},{4,6},{6,4},{8,10},{10,8},{12,14},{14,12},{16,18},{18,... | collective-permute-start | bytes 3145736 | tf_op jit(solution)/shard_map/ppermute | solution.py:74
  40.5 15.1 %collective-permute-start.4 = (bf16[2,512,512]{2,1,0:T(8,128)(2,1)S(1)}, bf16[2,512,512]{2,1,0:T(8,128)(2,1)}, u32[]{:S(2)}, u32[]{:S(2)}) collective-permute-start(bf16[2,512,512]{2,1,0:T(8,128)(2,1)S(1)} %collective-permute-done.2.refs_1_.refs_0_), channel_id=1, source_target_pairs={{0,8},{2,6},{8,16},{10,2},{16,24},{18,10},{24,28},{26,18},{28,20},... | collective-permute-start | bytes 3145736 | tf_op jit(solution)/shard_map/ppermute | solution.py:71
  42.7 16.0 %collective-permute-start.7 = (bf16[2,512,512]{2,1,0:T(8,128)(2,1)S(1)}, bf16[2,512,512]{2,1,0:T(8,128)(2,1)S(1)}, u32[]{:S(2)}, u32[]{:S(2)}) collective-permute-start(bf16[2,512,512]{2,1,0:T(8,128)(2,1)S(1)} %collective-permute-done.2.refs_1_.refs_0_), channel_id=1, source_target_pairs={{0,2},{2,0},{4,6},{6,4},{8,10},{10,8},{12,14},{14,12},{16,18},{18,... | collective-permute-start | bytes 3145736 | tf_op jit(solution)/shard_map/ppermute | solution.py:74
  111.4 15.8 %collective-permute-start.13 = (bf16[256,1024]{1,0:T(8,128)(2,1)S(1)}, bf16[256,1024]{1,0:T(8,128)(2,1)S(1)}, u32[]{:S(2)}, u32[]{:S(2)}) collective-permute-start(bf16[256,1024]{1,0:T(8,128)(2,1)S(1)} %get-tuple-element.350.refs_3_), channel_id=1, source_target_pairs={{0,1},{1,0},{2,3},{3,2},{4,5},{5,4},{6,7},{7,6},{8,9},{9,8},{10,11... | collective-permute-start | bytes 1572872 | tf_op jit(solution)/shard_map/ppermute | solution.py:240
  130.8 21.1 %collective-permute-start.15 = (bf16[7,9,192,256]{3,2,1,0:T(8,128)(2,1)}, bf16[7,9,192,256]{3,2,1,0:T(8,128)(2,1)}, u32[]{:S(2)}, u32[]{:S(2)}) collective-permute-start(bf16[7,9,192,256]{3,2,1,0:T(8,128)(2,1)} %copy-done.52), channel_id=1, source_target_pairs={{0,2},{2,0},{4,6},{6,4},{8,10},{10,8},{12,14},{14,12},{16,18},{18,... | collective-permute-start | bytes 18579464 | tf_op jit(solution)/shard_map/ppermute | solution.py:74
  131.5 20.5 %collective-permute-start.16 = (bf16[9,192,256]{2,1,0:T(8,128)(2,1)S(1)}, bf16[9,192,256]{2,1,0:T(8,128)(2,1)S(1)}, u32[]{:S(2)}, u32[]{:S(2)}) collective-permute-start(bf16[9,192,256]{2,1,0:T(8,128)(2,1)S(1)} %add_convert_fusion.5), channel_id=1, source_target_pairs={{0,8},{2,6},{8,16},{10,2},{16,24},{18,10},{24,28},{26,18},{28,20},... | collective-permute-start | bytes 2654216 | tf_op jit(solution)/shard_map/ppermute | solution.py:71
  155.0 22.7 %collective-permute-start.17 = (bf16[2,9,192,256]{3,2,1,0:T(8,128)(2,1)S(1)}, bf16[2,9,192,256]{3,2,1,0:T(8,128)(2,1)S(1)}, u32[]{:S(2)}, u32[]{:S(2)}) collective-permute-start(bf16[2,9,192,256]{3,2,1,0:T(8,128)(2,1)S(1)} %pad_maximum_fusion), channel_id=1, source_target_pairs={{0,8},{2,6},{8,16},{10,2},{16,24},{18,10},{24,28},{26,18},{28,20},... | collective-permute-start | bytes 5308424 | tf_op jit(solution)/shard_map/ppermute | solution.py:71
  180.1 28.2 %collective-permute-start.19 = (bf16[2,9,192,256]{3,2,1,0:T(8,128)(2,1)S(1)}, bf16[2,9,192,256]{3,2,1,0:T(8,128)(2,1)S(1)}, u32[]{:S(2)}, u32[]{:S(2)}) collective-permute-start(bf16[2,9,192,256]{3,2,1,0:T(8,128)(2,1)S(1)} %add_convert_fusion), channel_id=1, source_target_pairs={{0,8},{2,6},{8,16},{10,2},{16,24},{18,10},{24,28},{26,18},{28,20},... | collective-permute-start | bytes 5308424 | tf_op jit(solution)/shard_map/ppermute | solution.py:71
  182.6 25.7 %collective-permute-start.20 = (bf16[512,512]{1,0:T(8,128)(2,1)S(1)}, bf16[512,512]{1,0:T(8,128)(2,1)S(1)}, u32[]{:S(2)}, u32[]{:S(2)}) collective-permute-start(bf16[512,512]{1,0:T(8,128)(2,1)S(1)} %add_convert_fusion.10), channel_id=1, source_target_pairs={{0,8},{2,6},{8,16},{10,2},{16,24},{18,10},{24,28},{26,18},{28,20},... | collective-permute-start | bytes 1572872 | tf_op jit(solution)/shard_map/ppermute | solution.py:71
  211.0 33.8 %collective-permute-start.24 = (bf16[2,512,512]{2,1,0:T(8,128)(2,1)S(1)}, bf16[2,512,512]{2,1,0:T(8,128)(2,1)S(1)}, u32[]{:S(2)}, u32[]{:S(2)}) collective-permute-start(bf16[2,512,512]{2,1,0:T(8,128)(2,1)S(1)} %pad_maximum_fusion.3), channel_id=1, source_target_pairs={{0,8},{2,6},{8,16},{10,2},{16,24},{18,10},{24,28},{26,18},{28,20},... | collective-permute-start | bytes 3145736 | tf_op jit(solution)/shard_map/ppermute | solution.py:71
  213.6 21.8 %collective-permute-start.22 = (bf16[9,192,256]{2,1,0:T(8,128)(2,1)S(1)}, bf16[9,192,256]{2,1,0:T(8,128)(2,1)S(1)}, u32[]{:S(2)}, u32[]{:S(2)}) collective-permute-start(bf16[9,192,256]{2,1,0:T(8,128)(2,1)S(1)} %get-tuple-element.414), channel_id=1, source_target_pairs={{0,8},{2,6},{8,16},{10,2},{16,24},{18,10},{24,28},{26,18},{28,20},... | collective-permute-start | bytes 2654216 | tf_op jit(solution)/shard_map/ppermute | solution.py:71
  215.4 29.5 %collective-permute-start.23 = (bf16[9,192,256]{2,1,0:T(8,128)(2,1)S(1)}, bf16[9,192,256]{2,1,0:T(8,128)(2,1)S(1)}, u32[]{:S(2)}, u32[]{:S(2)}) collective-permute-start(bf16[9,192,256]{2,1,0:T(8,128)(2,1)S(1)} %get-tuple-element.415), channel_id=1, source_target_pairs={{0,10},{2,4},{8,18},{10,0},{16,26},{18,8},{24,30},{26,16},{28,22},... | collective-permute-start | bytes 2654216 | tf_op jit(solution)/shard_map/ppermute | solution.py:138
  215.4 32.0 %collective-permute-start.25 = (bf16[2,512,512]{2,1,0:T(8,128)(2,1)S(1)}, bf16[2,512,512]{2,1,0:T(8,128)(2,1)S(1)}, u32[]{:S(2)}, u32[]{:S(2)}) collective-permute-start(bf16[2,512,512]{2,1,0:T(8,128)(2,1)S(1)} %get-tuple-element.423), channel_id=1, source_target_pairs={{0,2},{2,0},{4,6},{6,4},{8,10},{10,8},{12,14},{14,12},{16,18},{18,... | collective-permute-start | bytes 3145736 | tf_op jit(solution)/shard_map/ppermute | solution.py:74
  247.9 14.9 %collective-permute-start.28 = (bf16[2,512,512]{2,1,0:T(8,128)(2,1)S(1)}, bf16[2,512,512]{2,1,0:T(8,128)(2,1)S(1)}, u32[]{:S(2)}, u32[]{:S(2)}) collective-permute-start(bf16[2,512,512]{2,1,0:T(8,128)(2,1)S(1)} %add_convert_fusion.1), channel_id=1, source_target_pairs={{0,8},{2,6},{8,16},{10,2},{16,24},{18,10},{24,28},{26,18},{28,20},... | collective-permute-start | bytes 3145736 | tf_op jit(solution)/shard_map/ppermute | solution.py:71
  249.7 16.9 %collective-permute-start.31 = (bf16[9,192,256]{2,1,0:T(8,128)(2,1)}, bf16[9,192,256]{2,1,0:T(8,128)(2,1)S(1)}, u32[]{:S(2)}, u32[]{:S(2)}) collective-permute-start(bf16[9,192,256]{2,1,0:T(8,128)(2,1)} %fusion.8.refs_0_), channel_id=1, source_target_pairs={{0,2},{2,0},{4,6},{6,4},{8,10},{10,8},{12,14},{14,12},{16,18},{18,... | collective-permute-start | bytes 2654216 | tf_op jit(solution)/shard_map/ppermute | solution.py:74
  265.2 14.3 %collective-permute-start.30 = (bf16[512,512]{1,0:T(8,128)(2,1)S(1)}, bf16[512,512]{1,0:T(8,128)(2,1)S(1)}, u32[]{:S(2)}, u32[]{:S(2)}) collective-permute-start(bf16[512,512]{1,0:T(8,128)(2,1)S(1)} %get-tuple-element.437), channel_id=1, source_target_pairs={{0,10},{2,4},{8,18},{10,0},{16,26},{18,8},{24,30},{26,16},{28,22},... | collective-permute-start | bytes 1572872 | tf_op jit(solution)/shard_map/ppermute | solution.py:138
  265.2 14.3 %collective-permute-start.32 = (bf16[512,512]{1,0:T(8,128)(2,1)S(1)}, bf16[512,512]{1,0:T(8,128)(2,1)S(1)}, u32[]{:S(2)}, u32[]{:S(2)}) collective-permute-start(bf16[512,512]{1,0:T(8,128)(2,1)S(1)} %get-tuple-element.455), channel_id=1, source_target_pairs={{0,2},{2,0},{4,6},{6,4},{8,10},{10,8},{12,14},{14,12},{16,18},{18,... | collective-permute-start | bytes 1572872 | tf_op jit(solution)/shard_map/ppermute | solution.py:74
  265.5 25.3 %collective-permute-start.26 = (bf16[512,1024]{1,0:T(8,128)(2,1)S(1)}, bf16[512,1024]{1,0:T(8,128)(2,1)S(1)}, u32[]{:S(2)}, u32[]{:S(2)}) collective-permute-start(bf16[512,1024]{1,0:T(8,128)(2,1)S(1)} %down.1), channel_id=1, source_target_pairs={{0,1},{1,0},{2,3},{3,2},{4,5},{5,4},{6,7},{7,6},{8,9},{9,8},{10,11... | collective-permute-start | bytes 3145736 | tf_op jit(solution)/shard_map/ppermute | solution.py:224
  266.7 30.6 %collective-permute-start.36 = (bf16[9,192,256]{2,1,0:T(8,128)(2,1)}, bf16[9,192,256]{2,1,0:T(8,128)(2,1)}, u32[]{:S(2)}, u32[]{:S(2)}) collective-permute-start(bf16[9,192,256]{2,1,0:T(8,128)(2,1)} %fusion.8.refs_0_), channel_id=1, source_target_pairs={{0,8},{2,6},{8,16},{10,2},{16,24},{18,10},{24,28},{26,18},{28,20},... | collective-permute-start | bytes 2654216 | tf_op jit(solution)/shard_map/ppermute | solution.py:71
  273.2 24.0 %collective-permute-start.37 = (bf16[9,192,256]{2,1,0:T(8,128)(2,1)}, bf16[9,192,256]{2,1,0:T(8,128)(2,1)}, u32[]{:S(2)}, u32[]{:S(2)}) collective-permute-start(bf16[9,192,256]{2,1,0:T(8,128)(2,1)} %fusion.8.refs_0_), channel_id=1, source_target_pairs={{0,6},{2,8},{8,2},{10,16},{16,10},{18,24},{24,18},{26,28},{28,26},... | collective-permute-start | bytes 2654216 | tf_op jit(solution)/shard_map/ppermute | solution.py:101
  290.8 33.0 %collective-permute-start.34 = (bf16[7,96,1024]{2,1,0:T(8,128)(2,1)}, bf16[7,96,1024]{2,1,0:T(8,128)(2,1)}, u32[]{:S(2)}, u32[]{:S(2)}) collective-permute-start(bf16[7,96,1024]{2,1,0:T(8,128)(2,1)} %get-tuple-element.466), channel_id=1, source_target_pairs={{0,2},{2,0},{4,6},{6,4},{8,10},{10,8},{12,14},{14,12},{16,18},{18,... | collective-permute-start | bytes 4128776 | tf_op jit(solution)/shard_map/ppermute | solution.py:74
  299.0 29.2 %collective-permute-start.42 = (bf16[2,9,192,256]{3,2,1,0:T(8,128)(2,1)S(1)}, bf16[2,9,192,256]{3,2,1,0:T(8,128)(2,1)S(1)}, u32[]{:S(2)}, u32[]{:S(2)}) collective-permute-start(bf16[2,9,192,256]{3,2,1,0:T(8,128)(2,1)S(1)} %pad_maximum_fusion.1.refs_0_), channel_id=1, source_target_pairs={{0,2},{2,0},{4,6},{6,4},{8,10},{10,8},{12,14},{14,12},{16,18},{18,... | collective-permute-start | bytes 5308424 | tf_op jit(solution)/shard_map/ppermute | solution.py:74
  299.1 37.8 %collective-permute-start.44 = (bf16[2,9,192,256]{3,2,1,0:T(8,128)(2,1)S(1)}, bf16[2,9,192,256]{3,2,1,0:T(8,128)(2,1)S(1)}, u32[]{:S(2)}, u32[]{:S(2)}) collective-permute-start(bf16[2,9,192,256]{3,2,1,0:T(8,128)(2,1)S(1)} %pad_maximum_fusion.1.refs_0_), channel_id=1, source_target_pairs={{0,8},{2,6},{8,16},{10,2},{16,24},{18,10},{24,28},{26,18},{28,20},... | collective-permute-start | bytes 5308424 | tf_op jit(solution)/shard_map/ppermute | solution.py:71
  300.8 23.0 %collective-permute-start.35 = (bf16[96,1024]{1,0:T(8,128)(2,1)S(1)}, bf16[96,1024]{1,0:T(8,128)(2,1)S(1)}, u32[]{:S(2)}, u32[]{:S(2)}) collective-permute-start(bf16[96,1024]{1,0:T(8,128)(2,1)S(1)} %add_convert_fusion.16), channel_id=1, source_target_pairs={{0,8},{2,6},{8,16},{10,2},{16,24},{18,10},{24,28},{26,18},{28,20},... | collective-permute-start | bytes 589832 | tf_op jit(solution)/shard_map/ppermute | solution.py:71
  339.0 30.1 %collective-permute-start.50 = (bf16[2,9,192,256]{3,2,1,0:T(8,128)(2,1)S(1)}, bf16[2,9,192,256]{3,2,1,0:T(8,128)(2,1)S(1)}, u32[]{:S(2)}, u32[]{:S(2)}) collective-permute-start(bf16[2,9,192,256]{3,2,1,0:T(8,128)(2,1)S(1)} %collective-permute-done.44.refs_0_), channel_id=1, source_target_pairs={{0,2},{2,0},{4,6},{6,4},{8,10},{10,8},{12,14},{14,12},{16,18},{18,... | collective-permute-start | bytes 5308424 | tf_op jit(solution)/shard_map/ppermute | solution.py:74
  339.0 36.8 %collective-permute-start.54 = (bf16[2,9,192,256]{3,2,1,0:T(8,128)(2,1)S(1)}, bf16[2,9,192,256]{3,2,1,0:T(8,128)(2,1)}, u32[]{:S(2)}, u32[]{:S(2)}) collective-permute-start(bf16[2,9,192,256]{3,2,1,0:T(8,128)(2,1)S(1)} %collective-permute-done.44.refs_0_), channel_id=1, source_target_pairs={{0,8},{2,6},{8,16},{10,2},{16,24},{18,10},{24,28},{26,18},{28,20},... | collective-permute-start | bytes 5308424 | tf_op jit(solution)/shard_map/ppermute | solution.py:71
  340.6 34.0 %collective-permute-start.49 = (bf16[512,1024]{1,0:T(8,128)(2,1)S(1)}, bf16[512,1024]{1,0:T(8,128)(2,1)S(1)}, u32[]{:S(2)}, u32[]{:S(2)}) collective-permute-start(bf16[512,1024]{1,0:T(8,128)(2,1)S(1)} %get-tuple-element.534), channel_id=1, source_target_pairs={{0,1},{1,0},{2,3},{3,2},{4,5},{5,4},{6,7},{7,6},{8,9},{9,8},{10,11... | collective-permute-start | bytes 3145736 | tf_op jit(solution)/shard_map/ppermute | solution.py:224
  341.1 24.7 %collective-permute-start.43 = (bf16[2,96,1024]{2,1,0:T(8,128)(2,1)S(1)}, bf16[2,96,1024]{2,1,0:T(8,128)(2,1)S(1)}, u32[]{:S(2)}, u32[]{:S(2)}) collective-permute-start(bf16[2,96,1024]{2,1,0:T(8,128)(2,1)S(1)} %add_convert_fusion.12), channel_id=1, source_target_pairs={{0,8},{2,6},{8,16},{10,2},{16,24},{18,10},{24,28},{26,18},{28,20},... | collective-permute-start | bytes 1179656 | tf_op jit(solution)/shard_map/ppermute | solution.py:71
  342.5 22.6 %collective-permute-start.46 = (f32[2176]{0:T(1024)S(1)}, f32[2176]{0:T(1024)S(1)}, u32[]{:S(2)}, u32[]{:S(2)}) collective-permute-start(f32[2176]{0:T(1024)S(1)} %add.267), channel_id=1, source_target_pairs={{0,16},{2,18},{4,20},{6,22},{8,24},{10,26},{12,28},{14,30},{16,0},... | collective-permute-start | bytes 26120 | tf_op jit(solution)/shard_map/ppermute | solution.py:233
  380.9 18.4 %collective-permute-start.60 = (bf16[9,192,256]{2,1,0:T(8,128)(2,1)S(1)}, bf16[9,192,256]{2,1,0:T(8,128)(2,1)S(1)}, u32[]{:S(2)}, u32[]{:S(2)}) collective-permute-start(bf16[9,192,256]{2,1,0:T(8,128)(2,1)S(1)} %slice_bitcast_fusion.1), channel_id=1, source_target_pairs={{0,8},{2,6},{8,16},{10,2},{16,24},{18,10},{24,28},{26,18},{28,20},... | collective-permute-start | bytes 2654216 | tf_op jit(solution)/shard_map/ppermute | solution.py:71
  (100 other events, 828.8 us)

commit v2 on v1

--- a/solution.py
+++ b/solution.py
@@ -13,7 +13,7 @@
 EPSILON = 1e-05
 ROPE_BASE = 1000000.0
 LOG2E = 1.4426950408889634
-VMEM_BYTES = 24 * 2**20
+VMEM_BYTES = 18 * 2**20
 COST_SCALE = 4
 FFN_COLS = 768
 LATE = True
@@ -23,7 +23,8 @@
 
 
 class Ring:
-    def __init__(self, n_ctx):
+    def __init__(self, n_ctx, sign=1):
+        self.sign = sign
         n = self.n = n_ctx // 2
         self.zs = 4 if n % 4 == 0 else n
         self.ys = n // self.zs
@@ -31,7 +32,7 @@
 
         def steps(flip, turned):
             return [
-                (order[i] * 2 + c, order[(i + (1 - 2 * (c ^ turned))) % n] * 2 + (c ^ flip))
+                (order[i] * 2 + c, order[(i + sign * (1 - 2 * (c ^ turned))) % n] * 2 + (c ^ flip))
                 for i in range(n)
                 for c in (0, 1)
             ]
@@ -61,7 +62,8 @@
     def at(self, slot):
         place, core = self.here()
         distance, other = slot
-        return (place + (1 - 2 * core) * distance + self.n) % self.n, (core + other) % 2
+        ahead = self.sign * (1 - 2 * core) * distance
+        return (place + ahead + self.n) % self.n, (core + other) % 2
 
     def device_at(self, slot):
         place, core = self.at(slot)
@@ -225,15 +227,16 @@
     return theirs
 
 
-def pair_steps(x, axes):
-    for axis, size in axes:
-        step = 1
-        while step < size:
-            (mine,) = yield [x]
-            (theirs,) = yield [lax.ppermute(mine, axis, [(i, i ^ step) for i in range(size)])]
-            x = mine + theirs
-            step *= 2
+def pair_steps(x, exchanges):
+    for axis, size, step in exchanges:
+        (mine,) = yield [x]
+        (theirs,) = yield [lax.ppermute(mine, axis, [(i, i ^ step) for i in range(size)])]
+        x = mine + theirs
     return x
+
+
+def bits(size):
+    return [1 << k for k in range(size.bit_length() - 1)]
 
 
 def from_other(xs):
@@ -497,12 +500,15 @@
     return [jax.ShapeDtypeStruct((*head, *cut.shape), cut.dtype) for head in heads]
 
 
+def exchanged(ring, outs, *others):
+    keep_far, give_far, *keep, give = outs
+    give, got_far, *others = lax.optimization_barrier((give, ring.sibling(give_far), *others))
+    return [keep_far, got_far, *keep, ring.sibling(give)], others
+
+
 def dealt_terms(ring, outs):
     far = ring.n // 2
-    keep_far, give_far, *keep, give = outs
-    got_far = ring.sibling(give_far)
-    give, got_far = lax.optimization_barrier((give, got_far))
-    got = ring.sibling(give)
+    keep_far, got_far, *keep, got = outs
 
     def terms(d):
         if d == far:
@@ -977,6 +983,7 @@
 ):
     devices = lax.axis_size("ctx")
     ring = Ring(devices)
+    other_ring = Ring(devices, -1)
     far = ring.n // 2
     rows, width = tokens.shape
     seq_count = segment_ids.shape[0]
@@ -1102,6 +1109,7 @@
     if packed:
         dealt_out = ffn_grads(ring, hidden_two, back_gate, back_up, hidden_ffn, cots)
         first, *dealt_out = lax.optimization_barrier((first, *dealt_out))
+        dealt_out, _ = exchanged(ring, dealt_out)
         ffn_box = []
         ffn_sum = Steps(sum_steps(ring, dealt_terms(ring, dealt_out), ffn_box))
         first, last = advance([ffn_sum], first, last)
@@ -1141,8 +1149,9 @@
     for d in range(far, -1, -1):
         if d < far:
             chains = [ffn_sum, dkv_sum if d < far - 1 else None]
-            if d == 0 and pair:
+            if d == far - 2 and pair:
                 output_swap = Steps(exchange_steps(output_part))
+            if d in (far - 2, far - 3):
                 chains.append(output_swap)
             do_tiles, dq, *more = advance(chains, do_tiles, dq, *more)
             if d == far - 1:
@@ -1172,7 +1181,7 @@
     own_dkv = dkv_sum.result
     wide = width // (2 * ring.n) + w_out.shape[0] // (2 * ring.n)
     one_low, grad_norm_gain, grad_key_gain, kv_delta, *cuts = whole_call(
-        functools.partial(back_project_kernel, ring),
+        functools.partial(back_project_kernel, other_ring),
         "back_project",
         [
             shape(rows, width, dtype=bf16),
@@ -1207,23 +1216,26 @@
             grad_key_gain[0, :HEAD_SIZE],
         ]
     )
-    gain_sum = Steps(pair_steps(gains, [("tp", lax.axis_size("tp")), ("ctx", devices)]))
+    exchanges = [("ctx", devices, k) for k in bits(devices)[2:] + bits(devices)[1::-1]]
+    exchanges += [("tp", lax.axis_size("tp"), k) for k in bits(lax.axis_size("tp"))]
+    gain_sum = Steps(pair_steps(gains, exchanges))
     one_swap = Steps(exchange_steps(one_low)) if pair else None
     if packed:
         qkv_box = []
-        qkv_sum = Steps(sum_steps(ring, dealt_terms(ring, cuts), qkv_box))
+        cuts, _ = exchanged(other_ring, cuts)
+        qkv_sum = Steps(sum_steps(other_ring, dealt_terms(other_ring, cuts), qkv_box))
         gather = ffn_box[0]
         round_at = 0
         while qkv_sum.generator is not None:
             came = len(gather.pieces)
-            chains = [qkv_sum, gain_sum]
-            if round_at == 0:
-                chains.append(output_swap)
-            elif round_at in (1, 4):
+            chains = [qkv_sum]
+            if round_at in (1, 4):
                 chains.append(one_swap)
+            if round_at > 5:
+                chains.append(gain_sum)
             placed = advance(chains, *placed)
             if round_at % 2 == 0:
-                placed = advance([ffn_sum, gain_sum], *placed)
+                placed = advance([ffn_sum, gain_sum if round_at < 5 else None], *placed)
             if came > done:
                 placed = place_ffn(ring, gather.pieces[done:came], width, placed)
                 done = came
@@ -1232,11 +1244,9 @@
             placed = place_ffn(ring, gather.pieces[done:], width, placed)
         grad_w_gate, grad_w_up, grad_w_down = placed
         grad_w_query, grad_w_key, grad_w_value, grad_w_out = place_qkv(
-            ring, qkv_box[0].pieces, width, (q_cols, k_cols, k_cols)
+            other_ring, qkv_box[0].pieces, width, (q_cols, k_cols, k_cols)
         )
     else:
-        while gain_sum.generator is not None:
-            advance([gain_sum])
         grad_w_query, grad_kv, grad_w_out = sum_over_ctx(
             ring,
             [
@@ -1248,6 +1258,8 @@
         grad_kv = grad_kv.reshape(width, kv_heads, 2, HEAD_SIZE)
         grad_w_key = grad_kv[:, :, 0].reshape(width, k_cols)
         grad_w_value = grad_kv[:, :, 1].reshape(width, k_cols)
+    while gain_sum.generator is not None:
+        advance([gain_sum])
     gains = gain_sum.result
     if pair:
         for swap in (output_swap, one_swap):

time: 425 us -> 402 us (0.946)
  Pallas kernels: 108 us -> 170 us
  waiting for transfers between devices: 184 us -> 132 us
  starting transfers between devices: 74.6 us -> 52.7 us
  local copies, waits for them, and re-layouts: 19.1 us -> 13.2 us
  other arithmetic: 26.8 us -> 21.5 us
    ppermute x24, waiting for transfers between devices: 118 us -> 73.2 us  [hop(): return lax.ppermute(x, 'ctx', self.onward)]
    pallas_call x5, Pallas kernels: 22.1 us -> 60.1 us  [backward(): pl.pallas_call(functools.partial(backward_kernel, self._make(slots), len(...]
    ppermute x24, starting transfers between devices: 52.3 us -> 30.5 us  [hop(): return lax.ppermute(x, 'ctx', self.onward)]
    pallas_call x6, Pallas kernels: 15.4 us -> 36.5 us  [forward(): pl.pallas_call(functools.partial(forward_kernel, self._make(slots), len(c...]
    ppermute x5, waiting for transfers between devices: 26.8 us -> 11.2 us  [pair_steps(): lax.ppermute(mine, axis, [(i, i ^ step) for i in range(size)])]
    ppermute x4, waiting for transfers between devices: 10.4 us -> 17.3 us  [from_other(): return [lax.ppermute(x, 'tp', [(0, 1), (1, 0)]) for x in xs]]
    unnamed x134 -> x106, local copies, waits for them, and re-layouts: 11.5 us -> 4.84 us
    convert_element_type x16, other arithmetic: 16.5 us -> 9.98 us  [total(): return out.astype(bf16)]
  transfers between devices with their start and end apart: 65 -> 65, of which waited for: 35 -> 35; matrix products, arithmetic and copies ran while one was open for 6% -> 7% of each run, Pallas kernels for 22% -> 39%
where the time goes in v2:
time: 402 us; the launch traced here: 394 us
  Pallas kernels  170 us (42%)
  waiting for transfers between devices  132 us (33%)
  starting transfers between devices  52.7 us (13%)
  other arithmetic  21.5 us (5%)
  local copies, waits for them, and re-layouts  13.2 us (3%)
    ppermute x24, waiting for transfers between devices, hop(): return lax.ppermute(x, 'ctx', self.onward)  73.2 us
    pallas_call x5, Pallas kernels, backward(): pl.pallas_call(functools.partial(backward_kernel, self._make(slots), len(...  60.1 us
    pallas_call x6, Pallas kernels, forward(): pl.pallas_call(functools.partial(forward_kernel, self._make(slots), len(c...  36.5 us
    ppermute x24, starting transfers between devices, hop(): return lax.ppermute(x, 'ctx', self.onward)  30.5 us
    pallas_call x8, Pallas kernels, whole_call(): pl.pallas_call(kernel, out_shape=list(outs), in_specs=[in_smem()] * scala...  27.5 us
    ppermute x3, waiting for transfers between devices, sum_steps(): got = (yield [ring.hop(x[0]), lax.ppermute(x[1], 'ctx', ring.across)])  20.7 us
    pallas_call x5, Pallas kernels, place_ffn(): pl.pallas_call(functools.partial(place_kernel, ring, slots, len(parts)),...  19.3 us
    ppermute x4, waiting for transfers between devices, from_other(): return [lax.ppermute(x, 'tp', [(0, 1), (1, 0)]) for x in xs]  17.3 us
  transfers between devices with their start and end apart: 65, of which 35 were waited for; matrix products, arithmetic and copies ran while one was open for 7% of the time, Pallas kernels for 39%

profile of v2, /device:TPU:0, one launch (start us, length us, event | category | flops | bytes accessed | tf_op | source)
XLA Modules:
  0.0 394.3 jit_solution(11204065707375348643)
XLA Ops:
  2.0 7.4 %project_kv.1 = (s32[1,3]{1,0:T(1,128)}, bf16[512,1024]{1,0:T(8,128)(2,1)}, f32[512,512]{1,0:T(8,128)}, bf16[512,512]{1,0:T(8,128)(2,1)}, bf16[1024,512]{1,0:T(8...) custom-call(s32[16]{0:T(128)} %order_ref.21, s32[1,8192]{1,0:T(1,128)} %segments.1, bf16[512,1024]{1,0:T(8,128)(2,1)} %tokens.3, ...), custom_call_target="tpu_custom_call" | custom-call | flops 134217728 | bytes 1581747 | tf_op jit(solution)/shard_map/project_kv/pallas_call | solution.py:648
  29.6 6.1 %attend_forward.7.refs_2_ = f32[4,2,512,128]{3,2,1,0:T(8,128)S(1)} custom-call(s32[16]{0:T(128)S(1)} %copy-done.37, s32[1,3]{1,0:T(1,128)S(1)} %copy-done.38, bf16[4,2,512,128]{3,2,1,0:T(8,128)(2,1)S(1)} %get-tuple-element.316.q_ref, bf16[512,512]{1,0:T(8,128)(2,1)S(1)} %collective-permute-done.3.refs_0_.refs_1_, ...), custom_call_target="tpu_custom_call" | custom-call | flops 805306368 | bytes 1703936 | tf_op jit(solution)/shard_map/attend_forward/pallas_call | solution.py:418
  35.7 4.7 %collective-permute-done.2.refs_1_.refs_0_ = bf16[2,512,512]{2,1,0:T(8,128)(2,1)S(1)} collective-permute-done((bf16[2,512,512]{2,1,0:T(8,128)(2,1)S(1)}, bf16[2,512,512]{2,1,0:T(8,128)(2,1)S(1)}, u32[]{:S(2)}, u32[]{:S(2)}) %collective-permute-start.2) | collective-permute-done | bytes 1048608 | tf_op jit(solution)/shard_map/ppermute | solution.py:73
  42.7 7.9 %attend_forward.8.refs_2_ = f32[4,2,512,128]{3,2,1,0:T(8,128)S(1)} custom-call(s32[16]{0:T(128)S(1)} %copy-done.37, s32[1,3]{1,0:T(1,128)S(1)} %copy-done.38, bf16[4,2,512,128]{3,2,1,0:T(8,128)(2,1)S(1)} %get-tuple-element.316.q_ref, bf16[2,512,512]{2,1,0:T(8,128)(2,1)S(1)} %collective-permute-done.5.refs_0_.refs_1_, ...), custom_call_target="tpu_custom_call" | custom-call | flops 1073741824 | bytes 1835008 | tf_op jit(solution)/shard_map/attend_forward/pallas_call | solution.py:418
  50.6 4.9 %collective-permute-done.4.refs_1_.refs_0_ = bf16[2,512,512]{2,1,0:T(8,128)(2,1)} collective-permute-done((bf16[2,512,512]{2,1,0:T(8,128)(2,1)S(1)}, bf16[2,512,512]{2,1,0:T(8,128)(2,1)}, u32[]{:S(2)}, u32[]{:S(2)}) %collective-permute-start.4) | collective-permute-done | bytes 1048608 | tf_op jit(solution)/shard_map/ppermute | solution.py:73
  58.7 9.0 %attend_forward.9.refs_1_ = f32[4,2,512,128]{3,2,1,0:T(8,128)S(1)} custom-call(s32[16]{0:T(128)S(1)} %copy-done.37, s32[1,3]{1,0:T(1,128)S(1)} %copy-done.38, bf16[4,2,512,128]{3,2,1,0:T(8,128)(2,1)S(1)} %get-tuple-element.316.q_ref, bf16[2,512,512]{2,1,0:T(8,128)(2,1)S(1)} %collective-permute-done.7.refs_0_.refs_1_, ...), custom_call_target="tpu_custom_call" | custom-call | flops 1073741824 | bytes 1835008 | tf_op jit(solution)/shard_map/attend_forward/pallas_call | solution.py:418
  69.2 5.1 %attend_forward.10.refs_2_ = f32[4,2,512,128]{3,2,1,0:T(8,128)S(1)} custom-call(s32[16]{0:T(128)S(1)} %copy-done.37, s32[1,3]{1,0:T(1,128)S(1)} %copy-done.38, bf16[4,2,512,128]{3,2,1,0:T(8,128)(2,1)S(1)} %get-tuple-element.316.q_ref, bf16[2,512,512]{2,1,0:T(8,128)(2,1)} %collective-permute-done.9.refs_0_.refs_1_, f32[4,2,512,128]{3,2,1,0:T(8,128)S(1)} %attend_forward.9.refs_1_), custom_call_target="tpu_custom_call" | custom-call | flops 536870912 | bytes 1572864 | tf_op jit(solution)/shard_map/attend_forward/pallas_call | solution.py:418
  74.4 5.1 %attend_forward.11.acc = f32[4,2,512,128]{3,2,1,0:T(8,128)S(1)} custom-call(s32[16]{0:T(128)S(1)} %copy-done.37, s32[1,3]{1,0:T(1,128)S(1)} %copy-done.38, bf16[4,2,512,128]{3,2,1,0:T(8,128)(2,1)S(1)} %get-tuple-element.316.q_ref, bf16[512,512]{1,0:T(8,128)(2,1)} %collective-permute-done.6.refs_0_, bf16[512,512]{1,0:T(8,128)(2,1)} %collective-permute-done.8.refs_1_, ...), custom_call_target="tpu_custom_call" | custom-call | flops 536870912 | bytes 1572864 | tf_op jit(solution)/shard_map/attend_forward/pallas_call | solution.py:418
  85.5 9.7 %collective-permute-done.10 = bf16[256,1024]{1,0:T(8,128)(2,1)S(1)} collective-permute-done((bf16[256,1024]{1,0:T(8,128)(2,1)S(1)}, bf16[256,1024]{1,0:T(8,128)(2,1)S(1)}, u32[]{:S(2)}, u32[]{:S(2)}) %collective-permute-start.10) | collective-permute-done | bytes 524320 | tf_op jit(solution)/shard_map/ppermute | solution.py:243
  97.2 7.6 %feed_forward.2 = (f32[256,1024]{1,0:T(8,128)S(1)}, bf16[256,1024]{1,0:T(8,128)(2,1)S(1)}, bf16[9,256,256]{2,1,0:T(8,128)(2,1)S(1)}, bf16[9,256,256]{2,1,0:T(8,1...) custom-call(bf16[256,1024]{1,0:T(8,128)(2,1)S(1)} %get-tuple-element.622.tokens, ...), custom_call_target="tpu_custom_call" | custom-call | flops 1207959552 | bytes 1048576 | tf_op jit(solution)/shard_map/feed_forward/pallas_call | solution.py:837
  104.8 4.1 %collective-permute-done.11.attn = bf16[256,1024]{1,0:T(8,128)(2,1)S(1)} collective-permute-done((bf16[256,1024]{1,0:T(8,128)(2,1)S(1)}, bf16[256,1024]{1,0:T(8,128)(2,1)S(1)}, u32[]{:S(2)}, u32[]{:S(2)}) %collective-permute-start.11) | collective-permute-done | bytes 524320 | tf_op jit(solution)/shard_map/ppermute | solution.py:243
  110.4 7.4 %feed_forward.3 = (f32[256,1024]{1,0:T(8,128)S(1)}, bf16[256,1024]{1,0:T(8,128)(2,1)S(1)}, bf16[9,256,256]{2,1,0:T(8,128)(2,1)S(1)}, bf16[9,256,256]{2,1,0:T(8,1...) custom-call(bf16[256,1024]{1,0:T(8,128)(2,1)S(1)} %get-tuple-element.621.tokens, ...), custom_call_target="tpu_custom_call" | custom-call | flops 1207959552 | bytes 1048576 | tf_op jit(solution)/shard_map/feed_forward/pallas_call | solution.py:837
  117.8 3.5 collective-permute-done.12.refs_5_
  122.9 11.1 %ffn_grads.1 = (bf16[9,192,256]{2,1,0:T(8,128)(2,1)S(1)}, bf16[9,192,256]{2,1,0:T(8,128)(2,1)S(1)}, bf16[9,192,256]{2,1,0:T(8,128)(2,1)S(1)}, bf16[2,9,192,256]{...) custom-call(bf16[256,1024]{1,0:T(8,128)(2,1)S(1)} %get-tuple-element, ...), custom_call_target="tpu_custom_call" | custom-call | flops 1811939328 | bytes 1048576 | tf_op jit(solution)/shard_map/ffn_grads/pallas_call | solution.py:538
  141.6 8.9 %attend_backward.5 = (f32[4,2,64,512]{3,2,1,0:T(8,128)S(1)}, f32[512,512]{1,0:T(8,128)S(1)}, bf16[512,512]{1,0:T(8,128)(2,1)S(1)}) custom-call(s32[16]{0:T(128)S(1)} %copy-done.37, s32[1,3]{1,0:T(1,128)S(1)} %copy-done.38, bf16[4,2,512,128]{3,2,1,0:T(8,128)(2,1)S(1)} %get-tuple-element.316.q_ref, bf16[4,2,512,128]{3,2,1,0:T(8,128)(2,1)S(1)} %get-tuple-element.433.do_ref, ...), custom_call_target="tpu_custom_call" | custom-call | flops 1342177280 | bytes 1703936 | tf_op jit(solution)/shard_map/attend_backward/pallas_call | solution.py:439
  157.7 14.9 %attend_backward.6 = (f32[4,2,64,512]{3,2,1,0:T(8,128)S(1)}, f32[2,512,512]{2,1,0:T(8,128)S(1)}, bf16[2,512,512]{2,1,0:T(8,128)(2,1)S(1)}) custom-call(s32[16]{0:T(128)S(1)} %copy-done.37, s32[1,3]{1,0:T(1,128)S(1)} %copy-done.38, bf16[4,2,512,128]{3,2,1,0:T(8,128)(2,1)S(1)} %get-tuple-element.316.q_ref, ...), custom_call_target="tpu_custom_call" | custom-call | flops 2684354560 | bytes 2359296 | tf_op jit(solution)/shard_map/attend_backward/pallas_call | solution.py:439
  179.3 13.7 %attend_backward.7 = (f32[4,2,64,512]{3,2,1,0:T(8,128)S(1)}, f32[2,512,512]{2,1,0:T(8,128)S(1)}, bf16[2,512,512]{2,1,0:T(8,128)(2,1)S(1)}) custom-call(s32[16]{0:T(128)S(1)} %copy-done.37, s32[1,3]{1,0:T(1,128)S(1)} %copy-done.38, bf16[4,2,512,128]{3,2,1,0:T(8,128)(2,1)S(1)} %get-tuple-element.316.q_ref, ...), custom_call_target="tpu_custom_call" | custom-call | flops 2684354560 | bytes 2359296 | tf_op jit(solution)/shard_map/attend_backward/pallas_call | solution.py:439
  193.0 10.0 %collective-permute-done.20 = bf16[512,512]{1,0:T(8,128)(2,1)S(1)} collective-permute-done((bf16[512,512]{1,0:T(8,128)(2,1)S(1)}, bf16[512,512]{1,0:T(8,128)(2,1)S(1)}, u32[]{:S(2)}, u32[]{:S(2)}) %collective-permute-start.20) | collective-permute-done | bytes 524320 | tf_op jit(solution)/shard_map/ppermute | solution.py:73
  208.8 13.5 %attend_backward.8 = (f32[4,2,64,512]{3,2,1,0:T(8,128)S(1)}, f32[2,512,512]{2,1,0:T(8,128)S(1)}, bf16[2,512,512]{2,1,0:T(8,128)(2,1)S(1)}) custom-call(s32[16]{0:T(128)S(1)} %copy-done.37, s32[1,3]{1,0:T(1,128)S(1)} %copy-done.38, bf16[4,2,512,128]{3,2,1,0:T(8,128)(2,1)S(1)} %get-tuple-element.316.q_ref, ...), custom_call_target="tpu_custom_call" | custom-call | flops 2684354560 | bytes 2359296 | tf_op jit(solution)/shard_map/attend_backward/pallas_call | solution.py:439
  222.3 7.0 %collective-permute-done.24 = bf16[9,192,256]{2,1,0:T(8,128)(2,1)S(1)} collective-permute-done((bf16[9,192,256]{2,1,0:T(8,128)(2,1)S(1)}, bf16[9,192,256]{2,1,0:T(8,128)(2,1)S(1)}, u32[]{:S(2)}, u32[]{:S(2)}) %collective-permute-start.24) | collective-permute-done | bytes 884768 | tf_op jit(solution)/shard_map/ppermute | solution.py:73
  229.3 8.6 %collective-permute-done.25 = bf16[9,192,256]{2,1,0:T(8,128)(2,1)S(1)} collective-permute-done((bf16[9,192,256]{2,1,0:T(8,128)(2,1)S(1)}, bf16[9,192,256]{2,1,0:T(8,128)(2,1)S(1)}, u32[]{:S(2)}, u32[]{:S(2)}) %collective-permute-start.25) | collective-permute-done | bytes 884768 | tf_op jit(solution)/shard_map/ppermute | solution.py:140
  240.9 9.1 %attend_backward.9 = (f32[4,2,64,512]{3,2,1,0:T(8,128)S(1)}, f32[512,512]{1,0:T(8,128)S(1)}, bf16[512,512]{1,0:T(8,128)(2,1)S(1)}) custom-call(s32[16]{0:T(128)S(1)} %copy-done.37, s32[1,3]{1,0:T(1,128)S(1)} %copy-done.38, bf16[4,2,512,128]{3,2,1,0:T(8,128)(2,1)S(1)} %get-tuple-element.316.q_ref, bf16[4,2,512,128]{3,2,1,0:T(8,128)(2,1)S(1)} %get-tuple-element.433.do_ref, ...), custom_call_target="tpu_custom_call" | custom-call | flops 1677721600 | bytes 1703936 | tf_op jit(solution)/shard_map/attend_backward/pallas_call | solution.py:439
  250.0 3.8 collective-permute-done.28
  261.5 4.6 %collective-permute-done.29 = bf16[512,512]{1,0:T(8,128)(2,1)S(1)} collective-permute-done((bf16[512,512]{1,0:T(8,128)(2,1)S(1)}, bf16[512,512]{1,0:T(8,128)(2,1)S(1)}, u32[]{:S(2)}, u32[]{:S(2)}) %collective-permute-start.29) | collective-permute-done | bytes 524320 | tf_op jit(solution)/shard_map/ppermute | solution.py:73
  266.1 10.2 %collective-permute-done.30 = bf16[512,512]{1,0:T(8,128)(2,1)S(1)} collective-permute-done((bf16[512,512]{1,0:T(8,128)(2,1)S(1)}, bf16[512,512]{1,0:T(8,128)(2,1)S(1)}, u32[]{:S(2)}, u32[]{:S(2)}) %collective-permute-start.30) | collective-permute-done | bytes 524320 | tf_op jit(solution)/shard_map/ppermute | solution.py:140
  276.6 5.4 %back_project.1 = (bf16[512,1024]{1,0:T(8,128)(2,1)S(1)}, f32[1,1024]{1,0:T(1,128)S(1)}, f32[1,128]{1,0:T(1,128)S(1)}, bf16[512,512]{1,0:T(8,128)(2,1)}, bf16[96...) custom-call(bf16[512,1024]{1,0:T(8,128)(2,1)S(1)} %copy-done, ...), custom_call_target="tpu_custom_call" | custom-call | flops 536870912 | bytes 3277984 | tf_op jit(solution)/shard_map/back_project/pallas_call | solution.py:648
  293.3 7.4 %collective-permute-done.35 = bf16[96,1024]{1,0:T(8,128)(2,1)S(1)} collective-permute-done((bf16[96,1024]{1,0:T(8,128)(2,1)}, bf16[96,1024]{1,0:T(8,128)(2,1)S(1)}, u32[]{:S(2)}, u32[]{:S(2)}) %collective-permute-start.35) | collective-permute-done | bytes 196640 | tf_op jit(solution)/shard_map/ppermute | solution.py:73
  305.1 5.3 %place_ffn.6 = (f32[1024,2304]{1,0:T(8,128)}, f32[1024,2304]{1,0:T(8,128)}, f32[2304,1024]{1,0:T(8,128)}) custom-call(bf16[2,9,192,256]{3,2,1,0:T(8,128)(2,1)} %pad_maximum_fusion.1.refs_0_, bf16[2,9,192,256]{3,2,1,0:T(8,128)(2,1)} %collective-permute-done.39.refs_1_, ...), custom_call_target="tpu_custom_call", output_to_operand_aliasing={{0}: (2, {}), {1}: (3, {}), {2}: (4, {})} | custom-call | bytes 14155776 | tf_op jit(solution)/shard_map/place_ffn/pallas_call | solution.py:595
  310.4 4.7 %collective-permute-done.38 = bf16[2,96,1024]{2,1,0:T(8,128)(2,1)S(1)} collective-permute-done((bf16[2,96,1024]{2,1,0:T(8,128)(2,1)S(1)}, bf16[2,96,1024]{2,1,0:T(8,128)(2,1)S(1)}, u32[]{:S(2)}, u32[]{:S(2)}) %collective-permute-start.38) | collective-permute-done | bytes 393248 | tf_op jit(solution)/shard_map/ppermute | solution.py:73
  323.0 11.8 %collective-permute-done.40 = bf16[2,96,1024]{2,1,0:T(8,128)(2,1)S(1)} collective-permute-done((bf16[2,96,1024]{2,1,0:T(8,128)(2,1)S(1)}, bf16[2,96,1024]{2,1,0:T(8,128)(2,1)S(1)}, u32[]{:S(2)}, u32[]{:S(2)}) %collective-permute-start.40) | collective-permute-done | bytes 393248 | tf_op jit(solution)/shard_map/ppermute | solution.py:73
  365.7 5.4 %place_ffn.8 = (f32[1024,2304]{1,0:T(8,128)}, f32[1024,2304]{1,0:T(8,128)}, f32[2304,1024]{1,0:T(8,128)}) custom-call(bf16[2,9,192,256]{3,2,1,0:T(8,128)(2,1)} %collective-permute-done.50.refs_0_, bf16[2,9,192,256]{3,2,1,0:T(8,128)(2,1)} %collective-permute-done.55.refs_1_, ...), custom_call_target="tpu_custom_call", output_to_operand_aliasing={{0}: (2, {}), {1}: (3, {}), {2}: (4, {})} | custom-call | bytes 14155776 | tf_op jit(solution)/shard_map/place_ffn/pallas_call | solution.py:595
  377.5 4.8 %collective-permute-done.56.refs_6_ = bf16[2,96,1024]{2,1,0:T(8,128)(2,1)S(1)} collective-permute-done((bf16[2,96,1024]{2,1,0:T(8,128)(2,1)S(1)}, bf16[2,96,1024]{2,1,0:T(8,128)(2,1)S(1)}, u32[]{:S(2)}, u32[]{:S(2)}) %collective-permute-start.56) | collective-permute-done | bytes 393248 | tf_op jit(solution)/shard_map/ppermute | solution.py:73
  (285 shorter events, 149.5 us)
Async XLA Ops:
  9.5 14.7 %collective-permute-start = (bf16[512,512]{1,0:T(8,128)(2,1)}, bf16[512,512]{1,0:T(8,128)(2,1)S(1)}, u32[]{:S(2)}, u32[]{:S(2)}) collective-permute-start(bf16[512,512]{1,0:T(8,128)(2,1)} %get-tuple-element.317.refs_0_), channel_id=1, source_target_pairs={{0,8},{2,6},{8,16},{10,2},{16,24},{18,10},{24,28},{26,18},{28,20},... | collective-permute-start | bytes 1572872 | tf_op jit(solution)/shard_map/ppermute | solution.py:73
  25.6 14.9 %collective-permute-start.2 = (bf16[2,512,512]{2,1,0:T(8,128)(2,1)S(1)}, bf16[2,512,512]{2,1,0:T(8,128)(2,1)S(1)}, u32[]{:S(2)}, u32[]{:S(2)}) collective-permute-start(bf16[2,512,512]{2,1,0:T(8,128)(2,1)S(1)} %pad_maximum_fusion.2.refs_0_), channel_id=1, source_target_pairs={{0,8},{2,6},{8,16},{10,2},{16,24},{18,10},{24,28},{26,18},{28,20},... | collective-permute-start | bytes 3145736 | tf_op jit(solution)/shard_map/ppermute | solution.py:73
  27.7 15.0 %collective-permute-start.5 = (bf16[2,512,512]{2,1,0:T(8,128)(2,1)S(1)}, bf16[2,512,512]{2,1,0:T(8,128)(2,1)S(1)}, u32[]{:S(2)}, u32[]{:S(2)}) collective-permute-start(bf16[2,512,512]{2,1,0:T(8,128)(2,1)S(1)} %pad_maximum_fusion.2.refs_0_), channel_id=1, source_target_pairs={{0,2},{2,0},{4,6},{6,4},{8,10},{10,8},{12,14},{14,12},{16,18},{18,... | collective-permute-start | bytes 3145736 | tf_op jit(solution)/shard_map/ppermute | solution.py:76
  40.5 15.1 %collective-permute-start.4 = (bf16[2,512,512]{2,1,0:T(8,128)(2,1)S(1)}, bf16[2,512,512]{2,1,0:T(8,128)(2,1)}, u32[]{:S(2)}, u32[]{:S(2)}) collective-permute-start(bf16[2,512,512]{2,1,0:T(8,128)(2,1)S(1)} %collective-permute-done.2.refs_1_.refs_0_), channel_id=1, source_target_pairs={{0,8},{2,6},{8,16},{10,2},{16,24},{18,10},{24,28},{26,18},{28,20},... | collective-permute-start | bytes 3145736 | tf_op jit(solution)/shard_map/ppermute | solution.py:73
  42.7 16.0 %collective-permute-start.7 = (bf16[2,512,512]{2,1,0:T(8,128)(2,1)S(1)}, bf16[2,512,512]{2,1,0:T(8,128)(2,1)S(1)}, u32[]{:S(2)}, u32[]{:S(2)}) collective-permute-start(bf16[2,512,512]{2,1,0:T(8,128)(2,1)S(1)} %collective-permute-done.2.refs_1_.refs_0_), channel_id=1, source_target_pairs={{0,2},{2,0},{4,6},{6,4},{8,10},{10,8},{12,14},{14,12},{16,18},{18,... | collective-permute-start | bytes 3145736 | tf_op jit(solution)/shard_map/ppermute | solution.py:76
  55.5 13.7 %collective-permute-start.9 = (bf16[2,512,512]{2,1,0:T(8,128)(2,1)}, bf16[2,512,512]{2,1,0:T(8,128)(2,1)}, u32[]{:S(2)}, u32[]{:S(2)}) collective-permute-start(bf16[2,512,512]{2,1,0:T(8,128)(2,1)} %collective-permute-done.4.refs_1_.refs_0_), channel_id=1, source_target_pairs={{0,2},{2,0},{4,6},{6,4},{8,10},{10,8},{12,14},{14,12},{16,18},{18,... | collective-permute-start | bytes 3145736 | tf_op jit(solution)/shard_map/ppermute | solution.py:76
  81.0 14.2 %collective-permute-start.10 = (bf16[256,1024]{1,0:T(8,128)(2,1)S(1)}, bf16[256,1024]{1,0:T(8,128)(2,1)S(1)}, u32[]{:S(2)}, u32[]{:S(2)}) collective-permute-start(bf16[256,1024]{1,0:T(8,128)(2,1)S(1)} %get-tuple-element.328), channel_id=1, source_target_pairs={{0,1},{1,0},{2,3},{3,2},{4,5},{5,4},{6,7},{7,6},{8,9},{9,8},{10,11... | collective-permute-start | bytes 1572872 | tf_op jit(solution)/shard_map/ppermute | solution.py:243
  136.5 14.0 %collective-permute-start.15 = (bf16[7,9,192,256]{3,2,1,0:T(8,128)(2,1)S(1)}, bf16[7,9,192,256]{3,2,1,0:T(8,128)(2,1)S(1)}, u32[]{:S(2)}, u32[]{:S(2)}) collective-permute-start(bf16[7,9,192,256]{3,2,1,0:T(8,128)(2,1)S(1)} %get-tuple-element.369), channel_id=1, source_target_pairs={{0,2},{2,0},{4,6},{6,4},{8,10},{10,8},{12,14},{14,12},{16,18},{18,... | collective-permute-start | bytes 18579464 | tf_op jit(solution)/shard_map/ppermute | solution.py:76
  151.4 22.6 %collective-permute-start.17 = (bf16[2,9,192,256]{3,2,1,0:T(8,128)(2,1)S(1)}, bf16[2,9,192,256]{3,2,1,0:T(8,128)(2,1)S(1)}, u32[]{:S(2)}, u32[]{:S(2)}) collective-permute-start(bf16[2,9,192,256]{3,2,1,0:T(8,128)(2,1)S(1)} %pad_maximum_fusion), channel_id=1, source_target_pairs={{0,8},{2,6},{8,16},{10,2},{16,24},{18,10},{24,28},{26,18},{28,20},... | collective-permute-start | bytes 5308424 | tf_op jit(solution)/shard_map/ppermute | solution.py:73
  174.9 28.2 %collective-permute-start.19 = (bf16[2,9,192,256]{3,2,1,0:T(8,128)(2,1)S(1)}, bf16[2,9,192,256]{3,2,1,0:T(8,128)(2,1)S(1)}, u32[]{:S(2)}, u32[]{:S(2)}) collective-permute-start(bf16[2,9,192,256]{3,2,1,0:T(8,128)(2,1)S(1)} %add_convert_fusion), channel_id=1, source_target_pairs={{0,8},{2,6},{8,16},{10,2},{16,24},{18,10},{24,28},{26,18},{28,20},... | collective-permute-start | bytes 5308424 | tf_op jit(solution)/shard_map/ppermute | solution.py:73
  176.5 26.6 %collective-permute-start.21 = (bf16[512,1024]{1,0:T(8,128)(2,1)S(1)}, bf16[512,1024]{1,0:T(8,128)(2,1)S(1)}, u32[]{:S(2)}, u32[]{:S(2)}) collective-permute-start(bf16[512,1024]{1,0:T(8,128)(2,1)S(1)} %down.1), channel_id=1, source_target_pairs={{0,1},{1,0},{2,3},{3,2},{4,5},{5,4},{6,7},{7,6},{8,9},{9,8},{10,11... | collective-permute-start | bytes 3145736 | tf_op jit(solution)/shard_map/ppermute | solution.py:226
  177.0 26.0 %collective-permute-start.20 = (bf16[512,512]{1,0:T(8,128)(2,1)S(1)}, bf16[512,512]{1,0:T(8,128)(2,1)S(1)}, u32[]{:S(2)}, u32[]{:S(2)}) collective-permute-start(bf16[512,512]{1,0:T(8,128)(2,1)S(1)} %add_convert_fusion.10), channel_id=1, source_target_pairs={{0,8},{2,6},{8,16},{10,2},{16,24},{18,10},{24,28},{26,18},{28,20},... | collective-permute-start | bytes 1572872 | tf_op jit(solution)/shard_map/ppermute | solution.py:73
  205.0 32.9 %collective-permute-start.26 = (bf16[2,512,512]{2,1,0:T(8,128)(2,1)S(1)}, bf16[2,512,512]{2,1,0:T(8,128)(2,1)S(1)}, u32[]{:S(2)}, u32[]{:S(2)}) collective-permute-start(bf16[2,512,512]{2,1,0:T(8,128)(2,1)S(1)} %pad_maximum_fusion.3), channel_id=1, source_target_pairs={{0,8},{2,6},{8,16},{10,2},{16,24},{18,10},{24,28},{26,18},{28,20},... | collective-permute-start | bytes 3145736 | tf_op jit(solution)/shard_map/ppermute | solution.py:73
  206.6 22.7 %collective-permute-start.24 = (bf16[9,192,256]{2,1,0:T(8,128)(2,1)S(1)}, bf16[9,192,256]{2,1,0:T(8,128)(2,1)S(1)}, u32[]{:S(2)}, u32[]{:S(2)}) collective-permute-start(bf16[9,192,256]{2,1,0:T(8,128)(2,1)S(1)} %get-tuple-element.421), channel_id=1, source_target_pairs={{0,8},{2,6},{8,16},{10,2},{16,24},{18,10},{24,28},{26,18},{28,20},... | collective-permute-start | bytes 2654216 | tf_op jit(solution)/shard_map/ppermute | solution.py:73
  208.0 29.9 %collective-permute-start.25 = (bf16[9,192,256]{2,1,0:T(8,128)(2,1)S(1)}, bf16[9,192,256]{2,1,0:T(8,128)(2,1)S(1)}, u32[]{:S(2)}, u32[]{:S(2)}) collective-permute-start(bf16[9,192,256]{2,1,0:T(8,128)(2,1)S(1)} %get-tuple-element.422), channel_id=1, source_target_pairs={{0,10},{2,4},{8,18},{10,0},{16,26},{18,8},{24,30},{26,16},{28,22},... | collective-permute-start | bytes 2654216 | tf_op jit(solution)/shard_map/ppermute | solution.py:140
  208.0 30.4 %collective-permute-start.27 = (bf16[2,512,512]{2,1,0:T(8,128)(2,1)S(1)}, bf16[2,512,512]{2,1,0:T(8,128)(2,1)S(1)}, u32[]{:S(2)}, u32[]{:S(2)}) collective-permute-start(bf16[2,512,512]{2,1,0:T(8,128)(2,1)S(1)} %get-tuple-element.428), channel_id=1, source_target_pairs={{0,2},{2,0},{4,6},{6,4},{8,10},{10,8},{12,14},{14,12},{16,18},{18,... | collective-permute-start | bytes 3145736 | tf_op jit(solution)/shard_map/ppermute | solution.py:76
  238.9 14.9 %collective-permute-start.28 = (bf16[2,512,512]{2,1,0:T(8,128)(2,1)S(1)}, bf16[2,512,512]{2,1,0:T(8,128)(2,1)S(1)}, u32[]{:S(2)}, u32[]{:S(2)}) collective-permute-start(bf16[2,512,512]{2,1,0:T(8,128)(2,1)S(1)} %add_convert_fusion.1), channel_id=1, source_target_pairs={{0,8},{2,6},{8,16},{10,2},{16,24},{18,10},{24,28},{26,18},{28,20},... | collective-permute-start | bytes 3145736 | tf_op jit(solution)/shard_map/ppermute | solution.py:73
  240.4 17.5 %collective-permute-start.31 = (bf16[9,192,256]{2,1,0:T(8,128)(2,1)S(1)}, bf16[9,192,256]{2,1,0:T(8,128)(2,1)S(1)}, u32[]{:S(2)}, u32[]{:S(2)}) collective-permute-start(bf16[9,192,256]{2,1,0:T(8,128)(2,1)S(1)} %fusion.8.refs_0_), channel_id=1, source_target_pairs={{0,2},{2,0},{4,6},{6,4},{8,10},{10,8},{12,14},{14,12},{16,18},{18,... | collective-permute-start | bytes 2654216 | tf_op jit(solution)/shard_map/ppermute | solution.py:76
  255.7 20.6 %collective-permute-start.30 = (bf16[512,512]{1,0:T(8,128)(2,1)S(1)}, bf16[512,512]{1,0:T(8,128)(2,1)S(1)}, u32[]{:S(2)}, u32[]{:S(2)}) collective-permute-start(bf16[512,512]{1,0:T(8,128)(2,1)S(1)} %get-tuple-element.439), channel_id=1, source_target_pairs={{0,10},{2,4},{8,18},{10,0},{16,26},{18,8},{24,30},{26,16},{28,22},... | collective-permute-start | bytes 1572872 | tf_op jit(solution)/shard_map/ppermute | solution.py:140
  255.7 20.6 %collective-permute-start.32 = (bf16[512,512]{1,0:T(8,128)(2,1)S(1)}, bf16[512,512]{1,0:T(8,128)(2,1)S(1)}, u32[]{:S(2)}, u32[]{:S(2)}) collective-permute-start(bf16[512,512]{1,0:T(8,128)(2,1)S(1)} %get-tuple-element.452), channel_id=1, source_target_pairs={{0,2},{2,0},{4,6},{6,4},{8,10},{10,8},{12,14},{14,12},{16,18},{18,... | collective-permute-start | bytes 1572872 | tf_op jit(solution)/shard_map/ppermute | solution.py:76
  256.4 31.6 %collective-permute-start.36 = (bf16[9,192,256]{2,1,0:T(8,128)(2,1)S(1)}, bf16[9,192,256]{2,1,0:T(8,128)(2,1)S(1)}, u32[]{:S(2)}, u32[]{:S(2)}) collective-permute-start(bf16[9,192,256]{2,1,0:T(8,128)(2,1)S(1)} %fusion.8.refs_0_), channel_id=1, source_target_pairs={{0,8},{2,6},{8,16},{10,2},{16,24},{18,10},{24,28},{26,18},{28,20},... | collective-permute-start | bytes 2654216 | tf_op jit(solution)/shard_map/ppermute | solution.py:73
  257.8 30.2 %collective-permute-start.37 = (bf16[9,192,256]{2,1,0:T(8,128)(2,1)S(1)}, bf16[9,192,256]{2,1,0:T(8,128)(2,1)S(1)}, u32[]{:S(2)}, u32[]{:S(2)}) collective-permute-start(bf16[9,192,256]{2,1,0:T(8,128)(2,1)S(1)} %fusion.8.refs_0_), channel_id=1, source_target_pairs={{0,6},{2,8},{8,2},{10,16},{16,10},{18,24},{24,18},{26,28},{28,26},... | collective-permute-start | bytes 2654216 | tf_op jit(solution)/shard_map/ppermute | solution.py:103
  285.0 15.8 %collective-permute-start.34 = (bf16[7,96,1024]{2,1,0:T(8,128)(2,1)}, bf16[7,96,1024]{2,1,0:T(8,128)(2,1)}, u32[]{:S(2)}, u32[]{:S(2)}) collective-permute-start(bf16[7,96,1024]{2,1,0:T(8,128)(2,1)} %get-tuple-element.463), channel_id=1, source_target_pairs={{0,2},{2,0},{4,6},{6,4},{8,10},{10,8},{12,14},{14,12},{16,18},{18,... | collective-permute-start | bytes 4128776 | tf_op jit(solution)/shard_map/ppermute | solution.py:76
  289.4 15.6 %collective-permute-start.39 = (bf16[2,9,192,256]{3,2,1,0:T(8,128)(2,1)}, bf16[2,9,192,256]{3,2,1,0:T(8,128)(2,1)}, u32[]{:S(2)}, u32[]{:S(2)}) collective-permute-start(bf16[2,9,192,256]{3,2,1,0:T(8,128)(2,1)} %pad_maximum_fusion.1.refs_0_), channel_id=1, source_target_pairs={{0,2},{2,0},{4,6},{6,4},{8,10},{10,8},{12,14},{14,12},{16,18},{18,... | collective-permute-start | bytes 5308424 | tf_op jit(solution)/shard_map/ppermute | solution.py:76
  291.3 28.8 %collective-permute-start.41 = (bf16[2,9,192,256]{3,2,1,0:T(8,128)(2,1)}, bf16[2,9,192,256]{3,2,1,0:T(8,128)(2,1)S(1)}, u32[]{:S(2)}, u32[]{:S(2)}) collective-permute-start(bf16[2,9,192,256]{3,2,1,0:T(8,128)(2,1)} %pad_maximum_fusion.1.refs_0_), channel_id=1, source_target_pairs={{0,8},{2,6},{8,16},{10,2},{16,24},{18,10},{24,28},{26,18},{28,20},... | collective-permute-start | bytes 5308424 | tf_op jit(solution)/shard_map/ppermute | solution.py:73
  303.7 15.7 %collective-permute-start.42 = (f32[2176]{0:T(1024)S(1)}, f32[2176]{0:T(1024)S(1)}, u32[]{:S(2)}, u32[]{:S(2)}) collective-permute-start(f32[2176]{0:T(1024)S(1)} %concatenate.7), channel_id=1, source_target_pairs={{0,8},{2,10},{4,12},{6,14},{8,0},{10,2},{12,4},{14,6},{16,24},{18,... | collective-permute-start | bytes 26120 | tf_op jit(solution)/shard_map/ppermute | solution.py:233
  320.1 16.2 %collective-permute-start.46 = (bf16[2,9,192,256]{3,2,1,0:T(8,128)(2,1)S(1)}, bf16[2,9,192,256]{3,2,1,0:T(8,128)(2,1)S(1)}, u32[]{:S(2)}, u32[]{:S(2)}) collective-permute-start(bf16[2,9,192,256]{3,2,1,0:T(8,128)(2,1)S(1)} %collective-permute-done.41.refs_0_), channel_id=1, source_target_pairs={{0,2},{2,0},{4,6},{6,4},{8,10},{10,8},{12,14},{14,12},{16,18},{18,... | collective-permute-start | bytes 5308424 | tf_op jit(solution)/shard_map/ppermute | solution.py:76
  320.2 31.2 %collective-permute-start.50 = (bf16[2,9,192,256]{3,2,1,0:T(8,128)(2,1)S(1)}, bf16[2,9,192,256]{3,2,1,0:T(8,128)(2,1)}, u32[]{:S(2)}, u32[]{:S(2)}) collective-permute-start(bf16[2,9,192,256]{3,2,1,0:T(8,128)(2,1)S(1)} %collective-permute-done.41.refs_0_), channel_id=1, source_target_pairs={{0,8},{2,6},{8,16},{10,2},{16,24},{18,10},{24,28},{26,18},{28,20},... | collective-permute-start | bytes 5308424 | tf_op jit(solution)/shard_map/ppermute | solution.py:73
  322.2 23.9 %collective-permute-start.45 = (bf16[512,1024]{1,0:T(8,128)(2,1)S(1)}, bf16[512,1024]{1,0:T(8,128)(2,1)S(1)}, u32[]{:S(2)}, u32[]{:S(2)}) collective-permute-start(bf16[512,1024]{1,0:T(8,128)(2,1)S(1)} %get-tuple-element.527), channel_id=1, source_target_pairs={{0,1},{1,0},{2,3},{3,2},{4,5},{5,4},{6,7},{7,6},{8,9},{9,8},{10,11... | collective-permute-start | bytes 3145736 | tf_op jit(solution)/shard_map/ppermute | solution.py:226
  336.3 14.4 %collective-permute-start.51 = (f32[2176]{0:T(1024)S(1)}, f32[2176]{0:T(1024)S(1)}, u32[]{:S(2)}, u32[]{:S(2)}) collective-permute-start(f32[2176]{0:T(1024)S(1)} %add.264), channel_id=1, source_target_pairs={{0,16},{2,18},{4,20},{6,22},{8,24},{10,26},{12,28},{14,30},{16,0},... | collective-permute-start | bytes 26120 | tf_op jit(solution)/shard_map/ppermute | solution.py:233
  351.4 14.3 %collective-permute-start.55 = (bf16[2,9,192,256]{3,2,1,0:T(8,128)(2,1)}, bf16[2,9,192,256]{3,2,1,0:T(8,128)(2,1)}, u32[]{:S(2)}, u32[]{:S(2)}) collective-permute-start(bf16[2,9,192,256]{3,2,1,0:T(8,128)(2,1)} %collective-permute-done.50.refs_0_), channel_id=1, source_target_pairs={{0,2},{2,0},{4,6},{6,4},{8,10},{10,8},{12,14},{14,12},{16,18},{18,... | collective-permute-start | bytes 5308424 | tf_op jit(solution)/shard_map/ppermute | solution.py:76
  356.7 18.1 %collective-permute-start.59 = (bf16[9,192,256]{2,1,0:T(8,128)(2,1)}, bf16[9,192,256]{2,1,0:T(8,128)(2,1)}, u32[]{:S(2)}, u32[]{:S(2)}) collective-permute-start(bf16[9,192,256]{2,1,0:T(8,128)(2,1)} %slice_bitcast_fusion.1), channel_id=1, source_target_pairs={{0,8},{2,6},{8,16},{10,2},{16,24},{18,10},{24,28},{26,18},{28,20},... | collective-permute-start | bytes 2654216 | tf_op jit(solution)/shard_map/ppermute | solution.py:73
  (86 other events, 747.1 us)
